TPU v7x, 256 devices: a whole 4x4x8 slice. The times are simulated.
256 devices in a mesh: band: 16 (over z, y_hi), fft: 16 (over y_lo, x, core).
Axes of the slice: x: 4, y: 4 (y_hi: 2, y_lo: 2; y = y_hi * 2 + y_lo), z: 8, core: 2. Of those that a mesh axis runs over, the one named last changes fastest.
Arguments:
- orbitals: float32 [32, 128, 128, 128], P('band', 'fft'), may hold values from -6 to 6
Outputs:
- applied: float32 [32, 128, 128, 128], P('band', 'fft')
- owner_terms: float32 [4, 128, 128, 128], P(None, 'fft')
All inputs are finite; a program needn't handle non-finite values.
Results may differ from a plain program's by a relative error of at most 0.0001.
Values sent between devices are 32-bit elements; how exact they have to be, the bound alone decides.
No kernel may reach another device: no remote copies, remote signals or barrier semaphores. Data moves between devices by JAX's collectives and lax.ppermute only.
A program may use at most 128 MiB of HBM per device.

v0:
```python
import math

import jax
import jax.numpy as jnp
from jax import lax
from jax.sharding import PartitionSpec as P

STEPS = 2


SPACING = 0.29
OMEGA = 0.106
MIX = -0.25


def broadcast(shard, axis, root):
    mine = lax.axis_index(axis) == root
    return lax.psum(jnp.where(mine, shard, jnp.zeros_like(shard)), axis)


def tables(length):
    idx = jnp.arange(length, dtype=jnp.int32)
    product = idx[:, None] * idx[None, :] % length
    angle = 2.0 * math.pi / length * product.astype(jnp.float32)
    return (jnp.cos(angle), jnp.sin(angle))


def wavenumber(idx, length):
    shifted = jnp.where(idx < length // 2, idx, idx - length)
    return 2.0 * math.pi / (length * SPACING) * shifted.astype(jnp.float32)


def screened(gsq):
    ratio = gsq / (4.0 * OMEGA * OMEGA)
    safe = jnp.where(ratio > 0, ratio, 1.0)
    return math.pi / (OMEGA * OMEGA) * jnp.where(ratio > 0, -jnp.expm1(-safe) / safe, 1.0)


def along(field, table, form):
    return jnp.einsum(form, field, table, precision=lax.Precision.HIGHEST)


def forward(real_part, imag_part, form, cos_t, sin_t):
    if imag_part is None:
        return (along(real_part, cos_t, form), -along(real_part, sin_t, form))
    return (
        along(real_part, cos_t, form) + along(imag_part, sin_t, form),
        along(imag_part, cos_t, form) - along(real_part, sin_t, form),
    )


def inverse(real_part, imag_part, form, cos_t, sin_t, length):
    return (
        (along(real_part, cos_t, form) - along(imag_part, sin_t, form)) / length,
        (along(imag_part, cos_t, form) + along(real_part, sin_t, form)) / length,
    )


def solve(real_part, imag_part):
    slab_z, size_y, size_x = (real_part.shape[1], real_part.shape[2], real_part.shape[3])
    groups = lax.axis_size("fft")
    size_z = slab_z * groups
    local_y = size_y // groups
    cos_x, sin_x = tables(size_x)
    cos_y, sin_y = tables(size_y)
    cos_z, sin_z = tables(size_z)
    form_x = "fzyx,xk->fzyk"
    form_y = "fzyx,yk->fzkx"
    form_z = "fzyx,zk->fkyx"
    real_part, imag_part = forward(real_part, imag_part, form_x, cos_x, sin_x)
    real_part, imag_part = forward(real_part, imag_part, form_y, cos_y, sin_y)
    y_index = lax.axis_index("fft") * local_y + jnp.arange(local_y, dtype=jnp.int32)
    g_z = wavenumber(jnp.arange(size_z, dtype=jnp.int32), size_z)[:, None, None]
    g_y = wavenumber(y_index, size_y)[None, :, None]
    g_x = wavenumber(jnp.arange(size_x, dtype=jnp.int32), size_x)[None, None, :]
    kernel = screened(g_z * g_z + g_y * g_y + g_x * g_x)
    line_re, line_im = forward(
        lax.all_to_all(real_part, "fft", split_axis=2, concat_axis=1, tiled=True),
        lax.all_to_all(imag_part, "fft", split_axis=2, concat_axis=1, tiled=True),
        form_z,
        cos_z,
        sin_z,
    )
    line_re, line_im = inverse(line_re * kernel, line_im * kernel, form_z, cos_z, sin_z, size_z)
    real_part = lax.all_to_all(line_re, "fft", split_axis=1, concat_axis=2, tiled=True)
    imag_part = lax.all_to_all(line_im, "fft", split_axis=1, concat_axis=2, tiled=True)
    real_part, imag_part = inverse(real_part, imag_part, form_y, cos_y, sin_y, size_y)
    real_part, imag_part = inverse(real_part, imag_part, form_x, cos_x, sin_x, size_x)
    return (real_part, imag_part)


def potentials(phi, orbitals):
    density = (phi[:, None] * orbitals[None]).reshape((-1,) + orbitals.shape[1:])
    result, unused = solve(density, None)
    return result.reshape((phi.shape[0], orbitals.shape[0]) + orbitals.shape[1:])


def per_device(orbitals):
    nband = lax.axis_size("band")
    applied = jnp.zeros_like(orbitals)
    pieces = []
    for step in range(STEPS):
        phi = broadcast(orbitals, "band", step * nband // STEPS)
        result = potentials(phi, orbitals)
        applied = applied + MIX * jnp.sum(result * phi[:, None], 0)
        pieces.append(MIX * jnp.sum(result * orbitals[None], 1))
    owner_part = jnp.concatenate(pieces, 0)
    owner_terms = lax.psum(owner_part, "band")
    return (applied, owner_terms)


def solution(mesh):
    placed = (P("band", "fft", None, None),)
    return jax.shard_map(
        per_device,
        mesh=mesh,
        in_specs=placed,
        out_specs=(P("band", "fft", None, None), P(None, "fft", None, None)),
        check_vma=False,
    )
```

profile of v0, /device:TPU:2, one launch (start us, length us, event | category | flops | bytes accessed | tf_op | source)
XLA Modules:
  0.0 654.6 jit_solution(15727371944030868358)
XLA Ops:
  7.2 2.9 broadcast_select_fusion
  10.1 171.5 %all-reduce.6.cloned.1.call-done = (f32[2,8,128,128]{3,2,1,0:T(8,128)}, f32[2,8,128,128]{3,2,1,0:T(8,128)}) async-done(((f32[2,8,128,128]{3,2,1,0:T(8,128)}, f32[2,8,128,128]{3,2,1,0:T(8,128)}), (f32[2,8,128,128]{3,2,1,0:T(8,128)}, f32[2,8,128,128]{3,2,1,0:T(8,128)})) %all-reduce.6.cloned.1.call-update) | async-done | bytes 2097168 | tf_op jit(solution)/shard_map/psum | solution.py:18
  181.6 3.4 broadcast_multiply_fusion
  185.0 2.1 fusion.162
  189.2 2.2 fusion.152
  191.4 2.1 add_bitcast_fusion
  193.6 2.5 copy.135
  196.1 5.8 all-to-all-start.4
  201.9 3.7 fusion.129
  205.6 2.1 subtract_bitcast_fusion
  207.7 2.6 copy.140
  210.3 20.1 %all-to-all-done.4 = f32[4,8,128,128]{3,1,0,2:T(8,128)} async-done(((f32[4,8,128,128]{3,1,0,2:T(8,128)}), f32[4,8,128,128]{3,1,0,2:T(8,128)}, u32[]{:S(2)}, u32[]{:S(2)}) %all-to-all-start.4) | async-done | bytes 2097184 | tf_op jit(solution)/shard_map/all_to_all | solution.py:78
  230.5 4.3 all-to-all-start.5
  234.8 2.1 fusion.165
  239.0 2.2 fusion.167
  241.2 2.1 add_bitcast_fusion.1
  243.3 2.5 copy.109
  245.9 17.3 %all-to-all-done.5 = f32[4,8,128,128]{3,1,0,2:T(8,128)} async-done(((f32[4,8,128,128]{3,1,0,2:T(8,128)}), f32[4,8,128,128]{3,1,0,2:T(8,128)}, u32[]{:S(2)}, u32[]{:S(2)}) %all-to-all-start.5) | async-done | bytes 2097184 | tf_op jit(solution)/shard_map/all_to_all | solution.py:79
  263.2 4.5 all-to-all-start
  268.2 3.7 fusion.138
  272.0 2.1 subtract_bitcast_fusion.1
  274.1 2.6 copy.114
  276.7 19.4 %all-to-all-done = f32[4,8,128,128]{3,1,0,2:T(8,128)} async-done(((f32[4,8,128,128]{3,1,0,2:T(8,128)}), f32[4,8,128,128]{3,1,0,2:T(8,128)}, u32[]{:S(2)}, u32[]{:S(2)}) %all-to-all-start) | async-done | bytes 2097184 | tf_op jit(solution)/shard_map/all_to_all | solution.py:78
  296.1 4.5 all-to-all-start.1
  300.7 3.7 fusion.16
  304.4 3.7 fusion.18
  308.2 4.1 subtract_multiply_fusion.1
  312.3 2.2 fusion.12
  314.5 4.1 add_multiply_fusion
  318.6 2.8 multiply_bitcast_fusion
  321.3 2.5 copy.153
  323.9 5.0 all-to-all-done.1
  328.9 4.3 all-to-all-start.7
  333.2 3.7 fusion.14
  336.9 2.3 multiply_bitcast_fusion.1
  339.3 2.6 copy.147
  341.9 19.7 %all-to-all-done.7 = f32[4,128,8,128]{3,2,0,1:T(8,128)} async-done(((f32[4,128,8,128]{3,2,0,1:T(8,128)}), f32[4,128,8,128]{3,2,0,1:T(8,128)}, u32[]{:S(2)}, u32[]{:S(2)}) %all-to-all-start.7) | async-done | bytes 2097184 | tf_op jit(solution)/shard_map/all_to_all | solution.py:86
  361.6 4.5 all-to-all-start.6
  366.1 3.7 fusion.44
  369.8 3.7 fusion.46
  373.6 4.1 subtract_multiply_fusion.3
  377.7 2.2 fusion.42
  379.9 4.1 add_multiply_fusion.1
  384.0 2.6 multiply_bitcast_fusion.3
  386.6 2.6 copy.121
  389.2 5.2 all-to-all-done.6
  394.3 4.3 all-to-all-start.2
  398.7 3.7 fusion.40
  402.4 2.4 multiply_bitcast_fusion.2
  404.8 2.6 copy.127
  407.4 19.7 %all-to-all-done.2 = f32[4,128,8,128]{3,2,0,1:T(8,128)} async-done(((f32[4,128,8,128]{3,2,0,1:T(8,128)}), f32[4,128,8,128]{3,2,0,1:T(8,128)}, u32[]{:S(2)}, u32[]{:S(2)}) %all-to-all-start.2) | async-done | bytes 2097184 | tf_op jit(solution)/shard_map/all_to_all | solution.py:85
  427.1 4.0 all-to-all-start.3
  431.5 5.1 fusion.8
  436.6 5.1 fusion.10
  441.7 5.1 fusion.4
  446.8 5.1 fusion.6
  451.9 5.0 fusion.36
  456.9 5.3 fusion.38
  462.2 2.2 fusion.32
  464.4 2.2 fusion.34
  473.0 4.0 multiply_reduce_fusion.1
  479.8 2.9 multiply_reduce_fusion.2
  483.8 160.6 %all-reduce.4.cloned.1.call-done = f32[4,8,128,128]{3,2,1,0:T(8,128)} async-done(((f32[4,8,128,128]{3,2,1,0:T(8,128)}), f32[4,8,128,128]{3,2,1,0:T(8,128)}) %all-reduce.4.cloned.1.call-update) | async-done | bytes 2097168 | tf_op jit(solution)/shard_map/psum | solution.py:108
  644.4 3.1 copy.304
  (47 shorter events, 15.3 us)
Async XLA Ops:
  7.2 174.4 %all-reduce.6.cloned.1.call-start = ((), (), s32[]{:S(2)}) async-start(), calls=%async_computation.9 | async-start | bytes 4194304 | tf_op jit(solution)/shard_map/psum | solution.py:18
  7.2 174.4 %copy-start.6 = (f32[2,8,128,128]{3,2,1,0:T(8,128)S(1)}, f32[2,8,128,128]{3,2,1,0:T(8,128)}, u32[]{:S(2)}) copy-start(f32[2,8,128,128]{3,2,1,0:T(8,128)} %param.1) | copy-start | bytes 3145732
  187.2 2.1 copy-start.5
  196.1 34.4 %all-to-all-start.4 = ((f32[4,8,128,128]{3,1,0,2:T(8,128)}), f32[4,8,128,128]{3,1,0,2:T(8,128)}, u32[]{:S(2)}, u32[]{:S(2)}) async-start(f32[4,8,128,128]{3,1,0,2:T(8,128)} %copy.135), calls=%async_computation.4 | async-start | bytes 4194304 | tf_op jit(solution)/shard_map/all_to_all | solution.py:78
  210.3 24.5 %copy-start = (f32[2,2,8,128,128]{4,3,2,1,0:T(8,128)S(1)}, f32[2,2,8,128,128]{4,3,2,1,0:T(8,128)}, u32[]{:S(2)}) copy-start(f32[2,2,8,128,128]{4,3,2,1,0:T(8,128)} %get-tuple-element.7) | copy-start | bytes 6291460
  230.5 32.7 %all-to-all-start.5 = ((f32[4,8,128,128]{3,1,0,2:T(8,128)}), f32[4,8,128,128]{3,1,0,2:T(8,128)}, u32[]{:S(2)}, u32[]{:S(2)}) async-start(f32[4,8,128,128]{3,1,0,2:T(8,128)} %copy.140), calls=%async_computation.5 | async-start | bytes 4194304 | tf_op jit(solution)/shard_map/all_to_all | solution.py:79
  234.8 2.2 copy-start.1
  237.0 2.1 copy-start.2
  263.2 32.9 %all-to-all-start = ((f32[4,8,128,128]{3,1,0,2:T(8,128)}), f32[4,8,128,128]{3,1,0,2:T(8,128)}, u32[]{:S(2)}, u32[]{:S(2)}) async-start(f32[4,8,128,128]{3,1,0,2:T(8,128)} %copy.109), calls=%async_computation | async-start | bytes 4194304 | tf_op jit(solution)/shard_map/all_to_all | solution.py:78
  296.1 32.7 %all-to-all-start.1 = ((f32[4,8,128,128]{3,1,0,2:T(8,128)}), f32[4,8,128,128]{3,1,0,2:T(8,128)}, u32[]{:S(2)}, u32[]{:S(2)}) async-start(f32[4,8,128,128]{3,1,0,2:T(8,128)} %copy.114), calls=%async_computation.1 | async-start | bytes 4194304 | tf_op jit(solution)/shard_map/all_to_all | solution.py:79
  312.3 2.2 copy-start.4
  328.9 32.7 %all-to-all-start.7 = ((f32[4,128,8,128]{3,2,0,1:T(8,128)}), f32[4,128,8,128]{3,2,0,1:T(8,128)}, u32[]{:S(2)}, u32[]{:S(2)}) async-start(f32[4,128,8,128]{3,2,0,1:T(8,128)} %copy.153), calls=%async_computation.7 | async-start | bytes 4194304 | tf_op jit(solution)/shard_map/all_to_all | solution.py:86
  361.6 32.7 %all-to-all-start.6 = ((f32[4,128,8,128]{3,2,0,1:T(8,128)}), f32[4,128,8,128]{3,2,0,1:T(8,128)}, u32[]{:S(2)}, u32[]{:S(2)}) async-start(f32[4,128,8,128]{3,2,0,1:T(8,128)} %copy.147), calls=%async_computation.6 | async-start | bytes 4194304 | tf_op jit(solution)/shard_map/all_to_all | solution.py:85
  377.7 2.2 copy-start.3
  394.3 32.7 %all-to-all-start.2 = ((f32[4,128,8,128]{3,2,0,1:T(8,128)}), f32[4,128,8,128]{3,2,0,1:T(8,128)}, u32[]{:S(2)}, u32[]{:S(2)}) async-start(f32[4,128,8,128]{3,2,0,1:T(8,128)} %copy.121), calls=%async_computation.2 | async-start | bytes 4194304 | tf_op jit(solution)/shard_map/all_to_all | solution.py:85
  427.1 35.1 %all-to-all-start.3 = ((f32[4,128,8,128]{3,2,0,1:T(8,128)}), f32[4,128,8,128]{3,2,0,1:T(8,128)S(1)}, u32[]{:S(2)}, u32[]{:S(2)}) async-start(f32[4,128,8,128]{3,2,0,1:T(8,128)} %copy.127), calls=%async_computation.3 | async-start | bytes 4194304 | tf_op jit(solution)/shard_map/all_to_all | solution.py:86
  431.1 213.3 %all-reduce.4.cloned.1.call-start = ((), (), s32[]{:S(2)}) async-start(), calls=%async_computation.8 | async-start | bytes 4194304 | tf_op jit(solution)/shard_map/psum | solution.py:108
  464.4 2.2 copy-start.8
  464.4 2.2 copy-start.9
  466.6 2.0 copy-start.10
  468.7 2.1 copy-start.12
  468.7 2.2 copy-start.13
  470.9 2.1 copy-start.7
  470.9 2.1 copy-start.11
  478.6 1.2 copy-start.14
Sparse Core Ops, SparseCore 0:
  11.3 170.2 all-reduce.5
  478.8 165.6 all-reduce.3
where the time goes:
time: 663 us; the launch traced here: 655 us
  waiting for transfers between devices  439 us (66%)
  matrix products  127 us (19%)
  starting transfers between devices  36.8 us (6%)
  local copies, waits for them, and re-layouts  25.2 us (4%)
  between operations  14.8 us (2%)
  other arithmetic  12.3 us (2%)
    psum x1, waiting for transfers between devices, broadcast(): return lax.psum(jnp.where(mine, shard, jnp.zeros_like(shard)), axis)  171 us
    psum x1, waiting for transfers between devices, per_device(): owner_terms = lax.psum(owner_part, 'band')  161 us
    dot_general x40, matrix products, along(): return jnp.einsum(form, field, table, precision=lax.Precision.HIGHEST)  127 us
    all_to_all x2, waiting for transfers between devices, solve(): lax.all_to_all(real_part, 'fft', split_axis=2, concat_axis=1, tiled=True)  39.5 us
    all_to_all x2, waiting for transfers between devices, solve(): lax.all_to_all(line_re, 'fft', split_axis=1, concat_axis=2, tiled=True)  24.9 us
    all_to_all x2, waiting for transfers between devices, solve(): lax.all_to_all(imag_part, 'fft', split_axis=2, concat_axis=1, tiled=True)  22.3 us
    all_to_all x2, waiting for transfers between devices, solve(): lax.all_to_all(line_im, 'fft', split_axis=1, concat_axis=2, tiled=True)  19.7 us
  transfers between devices with their start and end apart: 10, of which 9 were waited for; matrix products, arithmetic and copies ran while one was open for 19% of the time, Pallas kernels for 0%

commit v1 on v0

v1 whole, which is shorter than its diff:
```python
import math

import jax
import jax.numpy as jnp
import ml_dtypes
import numpy as np
from jax import lax
from jax.experimental import pallas as pl
from jax.experimental.pallas import tpu as pltpu
from jax.sharding import PartitionSpec as P

N = 128
SPACING = 0.29
OMEGA = 0.106
MIX = -0.25
VMEM = 48 * 1024 * 1024


def cas_tables():
    idx = np.arange(N)
    angle = 2.0 * np.pi / N * (idx[:, None] * idx[None, :] % N)
    full = np.cos(angle) + np.sin(angle)
    high = full.astype(ml_dtypes.bfloat16)
    low = (full - high.astype(np.float64)).astype(ml_dtypes.bfloat16)
    left = np.concatenate([high, low], 1)
    right = np.concatenate([left, left], 0)
    return left, right


def halves(value):
    high = value.astype(jnp.bfloat16)
    low = (value - high.astype(jnp.float32)).astype(jnp.bfloat16)
    return high, low


def dot(a, b):
    return lax.dot_general(a, b, (((1,), (0,)), ((), ())), preferred_element_type=jnp.float32)


def rows_by_table(value, right):
    out = dot(jnp.concatenate(halves(value), 1), right)
    return out[:, :N] + out[:, N:]


def table_by_rows(left, value):
    pair = jnp.concatenate(halves(value), 1)
    out = dot(left, jnp.concatenate([pair, pair], 0))
    size = value.shape[1]
    return out[:, :size] + out[:, size:]


def spread_kernel(phi_ref, orb_ref, left_ref, right_ref, out_ref):
    slab = orb_ref.shape[1]
    density = (phi_ref[0] * orb_ref[0]).reshape(slab * N, N)
    lines = rows_by_table(density, right_ref[...])
    flat = out_ref.reshape(N * slab, N)
    for z in range(slab):
        plane = table_by_rows(left_ref[...], lines[z * N:(z + 1) * N])
        flat[pl.ds(z, N, stride=slab), :] = plane


def line_kernel(in_ref, green_ref, left_ref, out_ref):
    groups, _, local, slab, _ = in_ref.shape
    for a in range(local):
        block = in_ref[:, 0, a].reshape(N, N)
        block = table_by_rows(left_ref[...], block) * green_ref[a]
        block = table_by_rows(left_ref[...], block)
        out_ref[:, 0, a] = block.reshape(groups, slab, N)


def gather_kernel(in_ref, phi_ref, orb_ref, left_ref, right_ref, applied_ref, owner_ref, lines):
    slab = orb_ref.shape[1]
    item, orbit = pl.program_id(0), pl.program_id(1)
    flat = in_ref.reshape(N * slab, N)
    for z in range(slab):
        plane = flat[pl.ds(z, N, stride=slab), :]
        lines[z * N:(z + 1) * N] = table_by_rows(left_ref[...], plane)
    result = rows_by_table(lines[...], right_ref[...]).reshape(slab, N, N) * MIX
    applied = result * phi_ref[0]
    owner = result * orb_ref[0]

    @pl.when(item == 0)
    def _():
        applied_ref[orbit] = applied

    @pl.when(item > 0)
    def _():
        applied_ref[orbit] += applied

    @pl.when(orbit == 0)
    def _():
        owner_ref[0] = owner

    @pl.when(orbit > 0)
    def _():
        owner_ref[0] += owner


def params():
    return pltpu.CompilerParams(vmem_limit_bytes=VMEM)


def whole(array):
    return pl.BlockSpec(array.shape, lambda *_: (0,) * array.ndim)


def spread(phi, orbitals, left, right, groups):
    items, slab = phi.shape[:2]
    count = orbitals.shape[0]
    local = N // groups
    fields = items * count
    return pl.pallas_call(
        spread_kernel,
        grid=(items, count),
        out_shape=jax.ShapeDtypeStruct((groups, fields, local, slab, N), jnp.float32),
        in_specs=[
            pl.BlockSpec((1, slab, N, N), lambda i, j: (i, 0, 0, 0)),
            pl.BlockSpec((1, slab, N, N), lambda i, j: (j, 0, 0, 0)),
            whole(left),
            whole(right),
        ],
        out_specs=pl.BlockSpec((groups, 1, local, slab, N), lambda i, j: (0, i * count + j, 0, 0, 0)),
        compiler_params=params(),
        cost_estimate=pl.CostEstimate(flops=fields * slab * N * N * 4096, bytes_accessed=fields * slab * N * N * 12, transcendentals=0),
    )(phi, orbitals, left, right)


def lines(field, green, left):
    groups, fields, local, slab, _ = field.shape
    block = pl.BlockSpec((groups, 1, local, slab, N), lambda f: (0, f, 0, 0, 0))
    return pl.pallas_call(
        line_kernel,
        grid=(fields,),
        out_shape=jax.ShapeDtypeStruct(field.shape, jnp.float32),
        in_specs=[block, whole(green), whole(left)],
        out_specs=block,
        compiler_params=params(),
        cost_estimate=pl.CostEstimate(flops=fields * slab * N * N * 4096, bytes_accessed=fields * slab * N * N * 12, transcendentals=0),
    )(field, green, left)


def collect(field, phi, orbitals, left, right):
    groups, fields, local, slab, _ = field.shape
    items, count = phi.shape[0], orbitals.shape[0]
    return pl.pallas_call(
        gather_kernel,
        grid=(items, count),
        out_shape=(
            jax.ShapeDtypeStruct(orbitals.shape, jnp.float32),
            jax.ShapeDtypeStruct(phi.shape, jnp.float32),
        ),
        in_specs=[
            pl.BlockSpec((groups, 1, local, slab, N), lambda i, j: (0, i * count + j, 0, 0, 0)),
            pl.BlockSpec((1, slab, N, N), lambda i, j: (i, 0, 0, 0)),
            pl.BlockSpec((1, slab, N, N), lambda i, j: (j, 0, 0, 0)),
            whole(left),
            whole(right),
        ],
        out_specs=(
            pl.BlockSpec(orbitals.shape, lambda i, j: (0, 0, 0, 0)),
            pl.BlockSpec((1, slab, N, N), lambda i, j: (i, 0, 0, 0)),
        ),
        scratch_shapes=[pltpu.VMEM((slab * N, N), jnp.float32)],
        compiler_params=params(),
        cost_estimate=pl.CostEstimate(flops=fields * slab * N * N * 4096, bytes_accessed=fields * slab * N * N * 16, transcendentals=0),
    )(field, phi, orbitals, left, right)


def wavenumber(idx):
    shifted = jnp.where(idx < N // 2, idx, idx - N)
    return 2.0 * math.pi / (N * SPACING) * shifted.astype(jnp.float32)


def green_table(groups):
    local = N // groups
    every = jnp.arange(N, dtype=jnp.int32)
    g_y = wavenumber(lax.axis_index("fft") * local + jnp.arange(local, dtype=jnp.int32))[:, None, None]
    g_z = wavenumber(every)[None, :, None]
    g_x = wavenumber(every)[None, None, :]
    ratio = (g_z * g_z + g_y * g_y + g_x * g_x) / (4.0 * OMEGA * OMEGA)
    safe = jnp.where(ratio > 0, ratio, 1.0)
    kernel = math.pi / (OMEGA * OMEGA) * jnp.where(ratio > 0, -jnp.expm1(-safe) / safe, 1.0)
    return kernel * (1.0 / N**3)


def sent_orbitals(orbitals):
    band = lax.axis_index("band")
    ring = band // 2
    zero = jnp.zeros_like(orbitals[0])
    parts = []
    for item in range(orbitals.shape[0]):
        own = orbitals[item]
        near = jnp.where(band == 0, own, zero)
        far = jnp.where(band == 8, own, zero)
        send = lax.ppermute(own, "band", [(0, 1), (8, 9)])
        near = near + jnp.where(ring == 0, send, zero)
        far = far + jnp.where(ring == 4, send, zero)
        for step in range(1, 5):
            up = []
            down = []
            for y in range(2):
                for start in (0, 4):
                    up.append(((start + step - 1) % 8 * 2 + y, (start + step) % 8 * 2 + y))
                    down.append(((start - step + 1) % 8 * 2 + y, (start - step) % 8 * 2 + y))
            got = lax.ppermute(jnp.where(ring < 4, near, far), "band", up)
            low_end = (ring >= 1) & (ring <= 4)
            if step < 4:
                back = lax.ppermute(jnp.where((ring > 4) | (ring == 0), near, far), "band", down)
                near = near + jnp.where(low_end, got, back)
                far = far + jnp.where(low_end, back, got)
            else:
                near = near + jnp.where(low_end, got, zero)
                far = far + jnp.where(low_end, zero, got)
        parts.append((near, far))
    return [parts[0][0], parts[1][0], parts[0][1], parts[1][1]]


def swap(array, axis):
    return lax.all_to_all(array, axis, split_axis=0, concat_axis=0)


def per_device(orbitals):
    groups, nband = lax.axis_size("fft"), lax.axis_size("band")
    left, right = (jnp.asarray(t) for t in cas_tables())
    green = green_table(groups)
    phis = sent_orbitals(orbitals)
    applied = None
    terms = []
    for chunk in range(2):
        phi = jnp.stack(phis[2 * chunk:2 * chunk + 2])
        field = spread(phi, orbitals, left, right, groups)
        field = lines(swap(field, "fft"), green, left)
        part, owner = collect(swap(field, "fft"), phi, orbitals, left, right)
        applied = part if applied is None else applied + part
        share = swap(owner.reshape(nband, 1, N, N), "band")
        share = jnp.sum(share, 0)
        every = swap(jnp.broadcast_to(share[None], (nband, 1, N, N)), "band")
        terms.append(every.reshape(owner.shape))
    return applied, jnp.concatenate(terms, 0)


def solution(mesh):
    return jax.shard_map(
        per_device,
        mesh=mesh,
        in_specs=(P("band", "fft", None, None),),
        out_specs=(P("band", "fft", None, None), P(None, "fft", None, None)),
        check_vma=False,
    )
```

time: 663 us -> 389 us (0.59); the launches traced: 655 us -> 387 us
  waiting for transfers between devices: 439 us -> 273 us
  matrix products: 127 us -> 0 us
  starting transfers between devices: 36.8 us -> 63.7 us
  Pallas kernels: 0 us -> 20.6 us
  between operations: 14.8 us -> 1.13 us
  local copies, waits for them, and re-layouts: 25.2 us -> 14.2 us
    psum x2 -> x0, waiting for transfers between devices: 332 us -> none  [the longest x1 171 us: broadcast(): return lax.psum(jnp.where(mine, shard, jnp.zeros_like(shard)), axis)]
    dot_general x40 -> x0, matrix products: 127 us -> none  [along(): return jnp.einsum(form, field, table, precision=lax.Precision.HIGHEST)]
    all_to_all x8, waiting for transfers between devices: 106 us -> 202 us  [swap(): return lax.all_to_all(array, axis, split_axis=0, concat_axis=0)]
    ppermute x0 -> x16, waiting for transfers between devices: none -> 71 us  [the longest x8 47.2 us: sent_orbitals(): got = lax.ppermute(jnp.where(ring < 4, near, far), 'band', up)]
    ppermute x0 -> x16, starting transfers between devices: none -> 22.2 us  [the longest x8 8.8 us: sent_orbitals(): got = lax.ppermute(jnp.where(ring < 4, near, far), 'band', up)]
    pallas_call x0 -> x6, Pallas kernels: none -> 20.6 us  [the longest x2 7.9 us: collect(): pl.pallas_call(gather_kernel, grid=(items, count), out_shape=(jax.ShapeDt...]
    div x4 -> x0, local copies, waits for them, and re-layouts: 10.4 us -> none  [the longest x2 5.2 us: inverse(): (along(real_part, cos_t, form) - along(imag_part, sin_t, form)) / length]
  transfers between devices with their start and end apart: 10 -> 24, of which waited for: 9 -> 16; matrix products, arithmetic and copies ran while one was open for 19% -> 2% of each run, Pallas kernels for 0% -> 5%
where the time goes in v1:
time: 389 us; the launch traced here: 387 us
  waiting for transfers between devices  273 us (70%)
  starting transfers between devices  63.7 us (16%)
  Pallas kernels  20.6 us (5%)
  other arithmetic  14.9 us (4%)
  local copies, waits for them, and re-layouts  14.2 us (4%)
    all_to_all x8, waiting for transfers between devices, swap(): return lax.all_to_all(array, axis, split_axis=0, concat_axis=0)  202 us
    ppermute x8, waiting for transfers between devices, sent_orbitals(): got = lax.ppermute(jnp.where(ring < 4, near, far), 'band', up)  47.2 us
    all_to_all x8, starting transfers between devices, swap(): return lax.all_to_all(array, axis, split_axis=0, concat_axis=0)  41.5 us
    ppermute x2, waiting for transfers between devices, sent_orbitals(): send = lax.ppermute(own, 'band', [(0, 1), (8, 9)])  19.5 us
    unnamed x30, local copies, waits for them, and re-layouts  10.7 us
    ppermute x8, starting transfers between devices, sent_orbitals(): got = lax.ppermute(jnp.where(ring < 4, near, far), 'band', up)  8.8 us
    pallas_call x2, Pallas kernels, collect(): pl.pallas_call(gather_kernel, grid=(items, count), out_shape=(jax.ShapeDt...  7.9 us
  transfers between devices with their start and end apart: 24, of which 16 were waited for; matrix products, arithmetic and copies ran while one was open for 2% of the time, Pallas kernels for 5%

profile of v1, /device:TPU:2, one launch (start us, length us, event | category | flops | bytes accessed | tf_op | source)
XLA Modules:
  0.0 387.3 jit_solution(6357431606626288859)
XLA Ops:
  0.6 1.4 slice_bitcast_fusion.1
  2.0 5.1 %collective-permute-start = (f32[8,128,128]{2,1,0:T(8,128)S(1)}, f32[8,128,128]{2,1,0:T(8,128)S(1)}, u32[]{:S(2)}, u32[]{:S(2)}) collective-permute-start(f32[8,128,128]{2,1,0:T(8,128)S(1)} %get-tuple-element.35), channel_id=1, source_target_pairs={{0,16},{128,144},{1,17},{129,145},{2,18},{130,146},{3,19},{131,147... | collective-permute-start | bytes 1572872 | tf_op jit(solution)/shard_map/ppermute | solution.py:195
  7.1 2.1 collective-permute-start.8
  9.2 10.2 %collective-permute-done = f32[8,128,128]{2,1,0:T(8,128)S(1)} collective-permute-done((f32[8,128,128]{2,1,0:T(8,128)S(1)}, f32[8,128,128]{2,1,0:T(8,128)S(1)}, u32[]{:S(2)}, u32[]{:S(2)}) %collective-permute-start) | collective-permute-done | bytes 524320 | tf_op jit(solution)/shard_map/ppermute | solution.py:195
  19.4 0.8 copy-done.14
  20.2 9.3 %collective-permute-done.8 = f32[8,128,128]{2,1,0:T(8,128)} collective-permute-done((f32[8,128,128]{2,1,0:T(8,128)S(1)}, f32[8,128,128]{2,1,0:T(8,128)}, u32[]{:S(2)}, u32[]{:S(2)}) %collective-permute-start.8) | collective-permute-done | bytes 524320 | tf_op jit(solution)/shard_map/ppermute | solution.py:195
  29.5 2.6 broadcast_select_fusion.5
  32.1 0.9 broadcast_select_fusion.13
  33.0 2.1 collective-permute-start.1
  35.1 2.1 collective-permute-start.2
  37.3 1.3 collective-permute-start.9
  38.6 1.3 collective-permute-start.10
  39.9 7.0 %collective-permute-done.1 = f32[8,128,128]{2,1,0:T(8,128)} collective-permute-done((f32[8,128,128]{2,1,0:T(8,128)}, f32[8,128,128]{2,1,0:T(8,128)}, u32[]{:S(2)}, u32[]{:S(2)}) %collective-permute-start.1) | collective-permute-done | bytes 524320 | tf_op jit(solution)/shard_map/ppermute | solution.py:205
  47.0 2.1 collective-permute-done.2
  49.1 1.3 broadcast_select_fusion.4
  50.5 0.7 collective-permute-start.3
  51.9 4.4 %collective-permute-done.9 = f32[8,128,128]{2,1,0:T(8,128)S(1)} collective-permute-done((f32[8,128,128]{2,1,0:T(8,128)S(1)}, f32[8,128,128]{2,1,0:T(8,128)S(1)}, u32[]{:S(2)}, u32[]{:S(2)}) %collective-permute-start.9) | collective-permute-done | bytes 524320 | tf_op jit(solution)/shard_map/ppermute | solution.py:205
  56.3 2.2 collective-permute-done.10
  58.8 0.7 collective-permute-start.11
  59.5 0.7 collective-permute-start.12
  62.1 0.7 collective-permute-start.13
  63.7 1.3 collective-permute-start.7
  65.1 1.3 collective-permute-start.15
  66.4 23.8 %collective-permute-done.7 = f32[8,128,128]{2,1,0:T(8,128)S(1)} collective-permute-done((f32[8,128,128]{2,1,0:T(8,128)S(1)}, f32[8,128,128]{2,1,0:T(8,128)S(1)}, u32[]{:S(2)}, u32[]{:S(2)}) %collective-permute-start.7) | collective-permute-done | bytes 524320 | tf_op jit(solution)/shard_map/ppermute | solution.py:205
  90.2 1.0 add_bitcast_fusion.1
  91.3 11.9 %collective-permute-done.15 = f32[8,128,128]{2,1,0:T(8,128)S(1)} collective-permute-done((f32[8,128,128]{2,1,0:T(8,128)S(1)}, f32[8,128,128]{2,1,0:T(8,128)S(1)}, u32[]{:S(2)}, u32[]{:S(2)}) %collective-permute-start.15) | collective-permute-done | bytes 524320 | tf_op jit(solution)/shard_map/ppermute | solution.py:205
  103.1 1.0 add_bitcast_fusion
  104.2 2.5 shard_map.50
  106.8 1.3 copy-done.3
  108.1 1.0 copy-done.6
  109.1 5.0 %all-to-all-start = ((f32[16,4,8,8,128]{4,3,2,1,0:T(8,128)}), f32[16,4,8,8,128]{4,3,2,1,0:T(8,128)S(1)}, u32[]{:S(2)}, u32[]{:S(2)}) async-start(f32[16,4,8,8,128]{4,3,2,1,0:T(8,128)} %copy-done.3), calls=%async_computation | async-start | bytes 4194304 | tf_op jit(solution)/shard_map/all_to_all | solution.py:219
  114.0 1.3 pad_maximum_fusion.2.phi_ref
  115.3 2.5 shard_map.53
  117.9 1.3 copy-done.1
  119.2 1.0 copy-done.4
  120.2 22.5 %all-to-all-done.in_ref = f32[16,4,8,8,128]{4,3,2,1,0:T(8,128)S(1)} async-done(((f32[16,4,8,8,128]{4,3,2,1,0:T(8,128)}), f32[16,4,8,8,128]{4,3,2,1,0:T(8,128)S(1)}, u32[]{:S(2)}, u32[]{:S(2)}) %all-to-all-start) | async-done | bytes 2097184 | tf_op jit(solution)/shard_map/all_to_all | solution.py:219
  142.7 4.3 %all-to-all-start.2 = ((f32[16,4,8,8,128]{4,3,2,1,0:T(8,128)}), f32[16,4,8,8,128]{4,3,2,1,0:T(8,128)}, u32[]{:S(2)}, u32[]{:S(2)}) async-start(f32[16,4,8,8,128]{4,3,2,1,0:T(8,128)} %copy-done.1), calls=%async_computation.2 | async-start | bytes 4194304 | tf_op jit(solution)/shard_map/all_to_all | solution.py:219
  147.5 2.7 shard_map.51
  150.2 1.3 copy-done.2
  151.5 0.8 copy-done.10
  152.3 23.1 %all-to-all-done.2.in_ref = f32[16,4,8,8,128]{4,3,2,1,0:T(8,128)} async-done(((f32[16,4,8,8,128]{4,3,2,1,0:T(8,128)}), f32[16,4,8,8,128]{4,3,2,1,0:T(8,128)}, u32[]{:S(2)}, u32[]{:S(2)}) %all-to-all-start.2) | async-done | bytes 2097184 | tf_op jit(solution)/shard_map/all_to_all | solution.py:219
  175.4 4.5 %all-to-all-start.1 = ((f32[16,4,8,8,128]{4,3,2,1,0:T(8,128)}), f32[16,4,8,8,128]{4,3,2,1,0:T(8,128)}, u32[]{:S(2)}, u32[]{:S(2)}) async-start(f32[16,4,8,8,128]{4,3,2,1,0:T(8,128)} %copy-done.2), calls=%async_computation.1 | async-start | bytes 4194304 | tf_op jit(solution)/shard_map/all_to_all | solution.py:219
  179.9 5.0 %shard_map.54 = f32[16,4,8,8,128]{4,3,2,1,0:T(8,128)} custom-call(f32[16,4,8,8,128]{4,3,2,1,0:T(8,128)} %all-to-all-done.2.in_ref, f32[8,128,128]{2,1,0:T(8,128)S(1)} %copy-done.11, bf16[128,256]{1,0:T(8,128)(2,1)S(1)} %copy-done.13), custom_call_target="tpu_custom_call" | custom-call | flops 2147483648 | bytes 6291456 | tf_op jit(solution)/shard_map/pallas_call | solution.py:131
  184.8 23.4 %all-to-all-done.1.in_ref = f32[16,4,8,8,128]{4,3,2,1,0:T(8,128)} async-done(((f32[16,4,8,8,128]{4,3,2,1,0:T(8,128)}), f32[16,4,8,8,128]{4,3,2,1,0:T(8,128)}, u32[]{:S(2)}, u32[]{:S(2)}) %all-to-all-start.1) | async-done | bytes 2097184 | tf_op jit(solution)/shard_map/all_to_all | solution.py:219
  208.3 4.3 %all-to-all-start.3 = ((f32[16,4,8,8,128]{4,3,2,1,0:T(8,128)}), f32[16,4,8,8,128]{4,3,2,1,0:T(8,128)}, u32[]{:S(2)}, u32[]{:S(2)}) async-start(f32[16,4,8,8,128]{4,3,2,1,0:T(8,128)} %shard_map.54), calls=%async_computation.3 | async-start | bytes 4194304 | tf_op jit(solution)/shard_map/all_to_all | solution.py:219
  212.6 4.0 %shard_map.52 = (f32[2,8,128,128]{3,2,1,0:T(8,128)S(1)}, f32[2,8,128,128]{3,2,1,0:T(8,128)S(1)}) custom-call(f32[16,4,8,8,128]{4,3,2,1,0:T(8,128)} %all-to-all-done.1.in_ref, f32[2,8,128,128]{3,2,1,0:T(8,128)S(1)} %copy-done.7, f32[2,8,128,128]{3,2,1,0:T(8,128)S(1)} %copy-done, bf16[128,256]{1,0:T(8,128)(2,1)S(1)} %copy-done.13, bf16[256,256]{1,0:T(8,128)(2,1)S(1)} %copy-done.12), custom_call_target="tpu_custom_call" | custom-call | flops 2147483648 | bytes 8388608 | tf_op jit(solution)/shard_map/pallas_call | solution.py:145
  216.6 1.0 copy-done.8
  217.6 23.5 %all-to-all-done.3.in_ref = f32[16,4,8,8,128]{4,3,2,1,0:T(8,128)} async-done(((f32[16,4,8,8,128]{4,3,2,1,0:T(8,128)}), f32[16,4,8,8,128]{4,3,2,1,0:T(8,128)}, u32[]{:S(2)}, u32[]{:S(2)}) %all-to-all-start.3) | async-done | bytes 2097184 | tf_op jit(solution)/shard_map/all_to_all | solution.py:219
  241.0 11.8 %all-to-all-start.4 = ((f32[16,1,128,128]{3,2,1,0:T(8,128)}), f32[16,1,128,128]{3,2,1,0:T(8,128)}, u32[]{:S(2)}, u32[]{:S(2)}) async-start(f32[16,1,128,128]{3,2,1,0:T(8,128)} %bitcast.32), calls=%async_computation.4 | async-start | bytes 2097152 | tf_op jit(solution)/shard_map/all_to_all | solution.py:219
  252.8 1.2 copy-done.5
  254.0 3.9 %shard_map.55 = (f32[2,8,128,128]{3,2,1,0:T(8,128)S(1)}, f32[2,8,128,128]{3,2,1,0:T(8,128)S(1)}) custom-call(f32[16,4,8,8,128]{4,3,2,1,0:T(8,128)} %all-to-all-done.3.in_ref, f32[2,8,128,128]{3,2,1,0:T(8,128)S(1)} %copy-done.5, f32[2,8,128,128]{3,2,1,0:T(8,128)S(1)} %copy-done, bf16[128,256]{1,0:T(8,128)(2,1)S(1)} %copy-done.13, bf16[256,256]{1,0:T(8,128)(2,1)S(1)} %copy-done.12), custom_call_target="tpu_custom_call" | custom-call | flops 2147483648 | bytes 8388608 | tf_op jit(solution)/shard_map/pallas_call | solution.py:145
  258.0 1.0 copy-done.9
  259.0 24.2 %all-to-all-done.4 = f32[16,1,128,128]{3,2,1,0:T(8,128)} async-done(((f32[16,1,128,128]{3,2,1,0:T(8,128)}), f32[16,1,128,128]{3,2,1,0:T(8,128)}, u32[]{:S(2)}, u32[]{:S(2)}) %all-to-all-start.4) | async-done | bytes 1048608 | tf_op jit(solution)/shard_map/all_to_all | solution.py:219
  283.2 3.7 all-to-all-start.6
  286.8 1.3 reduce_sum.18
  288.1 27.9 %all-to-all-done.6 = f32[16,1,128,128]{3,2,1,0:T(8,128)S(1)} async-done(((f32[16,1,128,128]{3,2,1,0:T(8,128)}), f32[16,1,128,128]{3,2,1,0:T(8,128)S(1)}, u32[]{:S(2)}, u32[]{:S(2)}) %all-to-all-start.6) | async-done | bytes 1048608 | tf_op jit(solution)/shard_map/all_to_all | solution.py:219
  316.0 1.1 broadcast_in_dim.10
  317.0 4.3 %all-to-all-start.5 = ((f32[16,1,128,128]{3,2,1,0:T(8,128)}), f32[16,1,128,128]{3,2,1,0:T(8,128)}, u32[]{:S(2)}, u32[]{:S(2)}) async-start(f32[16,1,128,128]{3,2,1,0:T(8,128)} %broadcast_in_dim.10), calls=%async_computation.5 | async-start | bytes 2097152 | tf_op jit(solution)/shard_map/all_to_all | solution.py:219
  321.5 28.9 %all-to-all-done.5 = f32[16,1,128,128]{3,2,1,0:T(8,128)} async-done(((f32[16,1,128,128]{3,2,1,0:T(8,128)}), f32[16,1,128,128]{3,2,1,0:T(8,128)}, u32[]{:S(2)}, u32[]{:S(2)}) %all-to-all-start.5) | async-done | bytes 1048608 | tf_op jit(solution)/shard_map/all_to_all | solution.py:219
  350.3 1.1 broadcast_in_dim.11
  351.4 3.7 all-to-all-start.7
  355.1 1.1 add.147
  356.1 28.4 %all-to-all-done.7 = f32[16,1,128,128]{3,2,1,0:T(8,128)S(1)} async-done(((f32[16,1,128,128]{3,2,1,0:T(8,128)}), f32[16,1,128,128]{3,2,1,0:T(8,128)S(1)}, u32[]{:S(2)}, u32[]{:S(2)}) %all-to-all-start.7) | async-done | bytes 1048608 | tf_op jit(solution)/shard_map/all_to_all | solution.py:219
  384.6 2.8 pad_maximum_fusion
  (48 shorter events, 4.5 us)
Async XLA Ops:
  0.6 28.9 %copy-start = (f32[2,8,128,128]{3,2,1,0:T(8,128)S(1)}, f32[2,8,128,128]{3,2,1,0:T(8,128)}, u32[]{:S(2)}) copy-start(f32[2,8,128,128]{3,2,1,0:T(8,128)} %orb_ref.7) | copy-start | bytes 3145732
  2.0 17.4 %collective-permute-start = (f32[8,128,128]{2,1,0:T(8,128)S(1)}, f32[8,128,128]{2,1,0:T(8,128)S(1)}, u32[]{:S(2)}, u32[]{:S(2)}) collective-permute-start(f32[8,128,128]{2,1,0:T(8,128)S(1)} %get-tuple-element.35), channel_id=1, source_target_pairs={{0,16},{128,144},{1,17},{129,145},{2,18},{130,146},{3,19},{131,147... | collective-permute-start | bytes 1572872 | tf_op jit(solution)/shard_map/ppermute | solution.py:195
  7.1 22.4 %collective-permute-start.8 = (f32[8,128,128]{2,1,0:T(8,128)S(1)}, f32[8,128,128]{2,1,0:T(8,128)}, u32[]{:S(2)}, u32[]{:S(2)}) collective-permute-start(f32[8,128,128]{2,1,0:T(8,128)S(1)} %get-tuple-element.36), channel_id=1, source_target_pairs={{0,16},{128,144},{1,17},{129,145},{2,18},{130,146},{3,19},{131,147... | collective-permute-start | bytes 1572872 | tf_op jit(solution)/shard_map/ppermute | solution.py:195
  19.4 0.8 copy-start.14
  33.0 14.0 %collective-permute-start.1 = (f32[8,128,128]{2,1,0:T(8,128)}, f32[8,128,128]{2,1,0:T(8,128)}, u32[]{:S(2)}, u32[]{:S(2)}) collective-permute-start(f32[8,128,128]{2,1,0:T(8,128)} %broadcast_select_fusion.13), channel_id=1, source_target_pairs={{0,32},{128,160},{16,48},{144,176},{1,33},{129,161},{17,49},{145,1... | collective-permute-start | bytes 1572872 | tf_op jit(solution)/shard_map/ppermute | solution.py:205
  35.1 14.0 %collective-permute-start.2 = (f32[8,128,128]{2,1,0:T(8,128)}, f32[8,128,128]{2,1,0:T(8,128)}, u32[]{:S(2)}, u32[]{:S(2)}) collective-permute-start(f32[8,128,128]{2,1,0:T(8,128)} %get-tuple-element.16), channel_id=1, source_target_pairs={{0,224},{128,96},{16,240},{144,112},{1,225},{129,97},{17,241},{145... | collective-permute-start | bytes 1572872 | tf_op jit(solution)/shard_map/ppermute | solution.py:208
  37.3 19.0 %collective-permute-start.9 = (f32[8,128,128]{2,1,0:T(8,128)S(1)}, f32[8,128,128]{2,1,0:T(8,128)S(1)}, u32[]{:S(2)}, u32[]{:S(2)}) collective-permute-start(f32[8,128,128]{2,1,0:T(8,128)S(1)} %broadcast_select_fusion.9), channel_id=1, source_target_pairs={{0,32},{128,160},{16,48},{144,176},{1,33},{129,161},{17,49},{145,1... | collective-permute-start | bytes 1572872 | tf_op jit(solution)/shard_map/ppermute | solution.py:205
  38.6 19.9 %collective-permute-start.10 = (f32[8,128,128]{2,1,0:T(8,128)}, f32[8,128,128]{2,1,0:T(8,128)S(1)}, u32[]{:S(2)}, u32[]{:S(2)}) collective-permute-start(f32[8,128,128]{2,1,0:T(8,128)} %get-tuple-element.32), channel_id=1, source_target_pairs={{0,224},{128,96},{16,240},{144,112},{1,225},{129,97},{17,241},{145... | collective-permute-start | bytes 1572872 | tf_op jit(solution)/shard_map/ppermute | solution.py:208
  50.5 9.7 %collective-permute-start.3 = (f32[8,128,128]{2,1,0:T(8,128)S(1)}, f32[8,128,128]{2,1,0:T(8,128)S(1)}, u32[]{:S(2)}, u32[]{:S(2)}) collective-permute-start(f32[8,128,128]{2,1,0:T(8,128)S(1)} %broadcast_select_fusion.12), channel_id=1, source_target_pairs={{32,64},{160,192},{48,80},{176,208},{33,65},{161,193},{49,81},{177... | collective-permute-start | bytes 1572872 | tf_op jit(solution)/shard_map/ppermute | solution.py:205
  51.2 9.0 %collective-permute-start.4 = (f32[8,128,128]{2,1,0:T(8,128)S(1)}, f32[8,128,128]{2,1,0:T(8,128)S(1)}, u32[]{:S(2)}, u32[]{:S(2)}) collective-permute-start(f32[8,128,128]{2,1,0:T(8,128)S(1)} %get-tuple-element.13), channel_id=1, source_target_pairs={{224,192},{96,64},{240,208},{112,80},{225,193},{97,65},{241,209},{... | collective-permute-start | bytes 1572872 | tf_op jit(solution)/shard_map/ppermute | solution.py:208
  58.8 3.1 collective-permute-start.11
  59.5 2.4 collective-permute-start.12
  60.5 3.1 collective-permute-start.5
  61.2 2.4 collective-permute-start.6
  62.1 2.8 collective-permute-start.13
  62.8 2.2 collective-permute-start.14
  63.7 26.5 %collective-permute-start.7 = (f32[8,128,128]{2,1,0:T(8,128)S(1)}, f32[8,128,128]{2,1,0:T(8,128)S(1)}, u32[]{:S(2)}, u32[]{:S(2)}) collective-permute-start(f32[8,128,128]{2,1,0:T(8,128)S(1)} %broadcast_select_fusion.10), channel_id=1, source_target_pairs={{96,128},{224,0},{112,144},{240,16},{97,129},{225,1},{113,145},{24... | collective-permute-start | bytes 1572872 | tf_op jit(solution)/shard_map/ppermute | solution.py:205
  65.1 38.0 %collective-permute-start.15 = (f32[8,128,128]{2,1,0:T(8,128)S(1)}, f32[8,128,128]{2,1,0:T(8,128)S(1)}, u32[]{:S(2)}, u32[]{:S(2)}) collective-permute-start(f32[8,128,128]{2,1,0:T(8,128)S(1)} %broadcast_select_fusion.6), channel_id=1, source_target_pairs={{96,128},{224,0},{112,144},{240,16},{97,129},{225,1},{113,145},{24... | collective-permute-start | bytes 1572872 | tf_op jit(solution)/shard_map/ppermute | solution.py:205
  91.2 13.0 %copy-start.12 = (bf16[256,256]{1,0:T(8,128)(2,1)S(1)}, bf16[256,256]{1,0:T(8,128)(2,1)}, u32[]{:S(2)}) copy-start(bf16[256,256]{1,0:T(8,128)(2,1)} %constant.55.clone.right_ref) | copy-start | bytes 393220
  91.2 13.0 %copy-start.13 = (bf16[128,256]{1,0:T(8,128)(2,1)S(1)}, bf16[128,256]{1,0:T(8,128)(2,1)}, u32[]{:S(2)}) copy-start(bf16[128,256]{1,0:T(8,128)(2,1)} %constant.54.clone.left_ref) | copy-start | bytes 196612
  106.8 1.3 copy-start.3
  108.1 1.0 copy-start.6
  109.1 33.6 %all-to-all-start = ((f32[16,4,8,8,128]{4,3,2,1,0:T(8,128)}), f32[16,4,8,8,128]{4,3,2,1,0:T(8,128)S(1)}, u32[]{:S(2)}, u32[]{:S(2)}) async-start(f32[16,4,8,8,128]{4,3,2,1,0:T(8,128)} %copy-done.3), calls=%async_computation | async-start | bytes 4194304 | tf_op jit(solution)/shard_map/all_to_all | solution.py:219
  117.9 1.3 copy-start.1
  119.2 1.0 copy-start.4
  142.7 32.7 %all-to-all-start.2 = ((f32[16,4,8,8,128]{4,3,2,1,0:T(8,128)}), f32[16,4,8,8,128]{4,3,2,1,0:T(8,128)}, u32[]{:S(2)}, u32[]{:S(2)}) async-start(f32[16,4,8,8,128]{4,3,2,1,0:T(8,128)} %copy-done.1), calls=%async_computation.2 | async-start | bytes 4194304 | tf_op jit(solution)/shard_map/all_to_all | solution.py:219
  150.2 1.3 copy-start.2
  151.5 0.8 copy-start.10
  175.4 4.5 %copy-start.11 = (f32[8,128,128]{2,1,0:T(8,128)S(1)}, f32[8,128,128]{2,1,0:T(8,128)}, u32[]{:S(2)}) copy-start(f32[8,128,128]{2,1,0:T(8,128)} %copy-done.10) | copy-start | bytes 1572868
  175.4 32.9 %all-to-all-start.1 = ((f32[16,4,8,8,128]{4,3,2,1,0:T(8,128)}), f32[16,4,8,8,128]{4,3,2,1,0:T(8,128)}, u32[]{:S(2)}, u32[]{:S(2)}) async-start(f32[16,4,8,8,128]{4,3,2,1,0:T(8,128)} %copy-done.2), calls=%async_computation.1 | async-start | bytes 4194304 | tf_op jit(solution)/shard_map/all_to_all | solution.py:219
  184.8 27.8 %copy-start.7 = (f32[2,8,128,128]{3,2,1,0:T(8,128)S(1)}, f32[2,8,128,128]{3,2,1,0:T(8,128)}, u32[]{:S(2)}) copy-start(f32[2,8,128,128]{3,2,1,0:T(8,128)} %copy-done.6) | copy-start | bytes 3145732
  208.3 32.7 %all-to-all-start.3 = ((f32[16,4,8,8,128]{4,3,2,1,0:T(8,128)}), f32[16,4,8,8,128]{4,3,2,1,0:T(8,128)}, u32[]{:S(2)}, u32[]{:S(2)}) async-start(f32[16,4,8,8,128]{4,3,2,1,0:T(8,128)} %shard_map.54), calls=%async_computation.3 | async-start | bytes 4194304 | tf_op jit(solution)/shard_map/all_to_all | solution.py:219
  216.6 1.0 copy-start.8
  241.0 42.1 %all-to-all-start.4 = ((f32[16,1,128,128]{3,2,1,0:T(8,128)}), f32[16,1,128,128]{3,2,1,0:T(8,128)}, u32[]{:S(2)}, u32[]{:S(2)}) async-start(f32[16,1,128,128]{3,2,1,0:T(8,128)} %bitcast.32), calls=%async_computation.4 | async-start | bytes 2097152 | tf_op jit(solution)/shard_map/all_to_all | solution.py:219
  252.8 1.2 copy-start.5
  258.0 1.0 copy-start.9
  283.2 32.8 %all-to-all-start.6 = ((f32[16,1,128,128]{3,2,1,0:T(8,128)}), f32[16,1,128,128]{3,2,1,0:T(8,128)S(1)}, u32[]{:S(2)}, u32[]{:S(2)}) async-start(f32[16,1,128,128]{3,2,1,0:T(8,128)} %bitcast.33), calls=%async_computation.6 | async-start | bytes 2097152 | tf_op jit(solution)/shard_map/all_to_all | solution.py:219
  317.0 33.3 %all-to-all-start.5 = ((f32[16,1,128,128]{3,2,1,0:T(8,128)}), f32[16,1,128,128]{3,2,1,0:T(8,128)}, u32[]{:S(2)}, u32[]{:S(2)}) async-start(f32[16,1,128,128]{3,2,1,0:T(8,128)} %broadcast_in_dim.10), calls=%async_computation.5 | async-start | bytes 2097152 | tf_op jit(solution)/shard_map/all_to_all | solution.py:219
  351.4 33.2 %all-to-all-start.7 = ((f32[16,1,128,128]{3,2,1,0:T(8,128)}), f32[16,1,128,128]{3,2,1,0:T(8,128)S(1)}, u32[]{:S(2)}, u32[]{:S(2)}) async-start(f32[16,1,128,128]{3,2,1,0:T(8,128)} %broadcast_in_dim.11), calls=%async_computation.7 | async-start | bytes 2097152 | tf_op jit(solution)/shard_map/all_to_all | solution.py:219

commit v2 on v0

v2 whole, which is shorter than its diff:
```python
import functools
import math

import jax
import jax.numpy as jnp
import ml_dtypes
import numpy as np
from jax import lax
from jax.experimental import pallas as pl
from jax.experimental.pallas import tpu as pltpu
from jax.sharding import PartitionSpec as P

N = 128
SPACING = 0.29
OMEGA = 0.106
MIX = -0.25
VMEM = 32 * 1024 * 1024
SLAB = 8
PLANES = 4
ORBS = 4
SENT = 4
FIELDS = ORBS * SENT
GROUP = 32
LOCAL = N // GROUP


def split(full):
    high = full.astype(ml_dtypes.bfloat16)
    low = (full - high.astype(np.float64)).astype(ml_dtypes.bfloat16)
    return np.concatenate([high, low], -1)


def cas_tables():
    idx = np.arange(N)
    angle = 2.0 * np.pi / N * (idx[:, None] * idx[None, :] % N)
    full = np.cos(angle) + np.sin(angle)
    left = split(full)
    right = np.concatenate([left, left], 0)
    order = np.array([(2 * chip + c) * SLAB + 2 * q + p for c in range(2) for p in range(2) for chip in range(8) for q in range(4)])
    return left, right, split(full[:, order]), split(full[order])


def halves(value):
    high = value.astype(jnp.bfloat16)
    low = (value - high.astype(jnp.float32)).astype(jnp.bfloat16)
    return high, low


def dot(a, b):
    return lax.dot_general(a, b, (((1,), (0,)), ((), ())), preferred_element_type=jnp.float32)


def rows_by_table(value, right):
    out = dot(jnp.concatenate(halves(value), 1), right)
    return out[:, :N] + out[:, N:]


def table_by_rows(left, value):
    pair = jnp.concatenate(halves(value), 1)
    out = dot(left, jnp.concatenate([pair, pair], 0))
    return out[:, :N] + out[:, N:]


def spread_kernel(phi_ref, orb_ref, left_ref, right_ref, out_ref):
    item, orbit = pl.program_id(0), pl.program_id(1)
    flat = out_ref.reshape(N * PLANES, N)
    density = [phi_ref[item, c, p] * orb_ref[c, orbit, p] for c in range(2) for p in range(2)]
    lines = rows_by_table(jnp.concatenate(density, 0), right_ref[...])
    for z in range(PLANES):
        flat[pl.ds(z, N, stride=PLANES), :] = table_by_rows(left_ref[...], lines[z * N:(z + 1) * N])


def line_kernel(in_ref, green_ref, to_z_ref, from_z_ref, out_ref):
    given, taken = (ref.reshape(GROUP * LOCAL * PLANES, N) for ref in (in_ref, out_ref))
    for a in range(LOCAL):
        rows = [pl.ds(a * PLANES + z, GROUP, stride=LOCAL * PLANES) for z in range(PLANES)]
        block = jnp.concatenate([given[r, :] for r in rows], 0)
        block = table_by_rows(to_z_ref[...], block) * green_ref[a]
        block = table_by_rows(from_z_ref[...], block)
        for z, r in enumerate(rows):
            taken[r, :] = block[z * GROUP:(z + 1) * GROUP]


def gather_kernel(in_ref, phi_ref, orb_ref, left_ref, right_ref, applied_ref, owner_ref, lines):
    item, orbit = pl.program_id(0), pl.program_id(1)
    flat = in_ref.reshape(N * PLANES, N)
    for z in range(PLANES):
        lines[z * N:(z + 1) * N] = table_by_rows(left_ref[...], flat[pl.ds(z, N, stride=PLANES), :])
    result = rows_by_table(lines[...], right_ref[...]) * MIX
    for c in range(2):
        for p in range(2):
            plane = result[(2 * c + p) * N:(2 * c + p + 1) * N]
            applied = plane * phi_ref[item, c, p]
            owner = plane * orb_ref[c, orbit, p]

            @pl.when(item == 0)
            def _():
                applied_ref[c, orbit, p] = applied

            @pl.when(item > 0)
            def _():
                applied_ref[c, orbit, p] += applied

            @pl.when(orbit == 0)
            def _():
                owner_ref[c, item, p] = owner

            @pl.when(orbit > 0)
            def _():
                owner_ref[c, item, p] += owner


def params():
    return pltpu.CompilerParams(vmem_limit_bytes=VMEM)


def cost(planes):
    return pl.CostEstimate(flops=planes * N * N * 2048, bytes_accessed=planes * N * N * 12, transcendentals=0)


FIELD_SHAPE = jax.ShapeDtypeStruct((GROUP, FIELDS, LOCAL * PLANES, N), jnp.float32)
FIELD_BLOCK = pl.BlockSpec((GROUP, 1, LOCAL * PLANES, N), lambda i, j: (0, ORBS * i + j, 0, 0))


def whole(array):
    return pl.BlockSpec(array.shape, lambda *_: (0,) * array.ndim)


def spread(phi, orbs, left, right):
    given = (phi, orbs, left, right)
    return pl.pallas_call(
        spread_kernel,
        grid=(SENT, ORBS),
        out_shape=FIELD_SHAPE,
        in_specs=[whole(array) for array in given],
        out_specs=FIELD_BLOCK,
        compiler_params=params(),
        cost_estimate=cost(FIELDS * PLANES),
    )(*given)


def lines(field, green, to_z, from_z):
    return pl.pallas_call(
        line_kernel,
        grid=(SENT, ORBS),
        out_shape=FIELD_SHAPE,
        in_specs=[FIELD_BLOCK, whole(green), whole(to_z), whole(from_z)],
        out_specs=FIELD_BLOCK,
        compiler_params=params(),
        cost_estimate=cost(FIELDS * PLANES),
    )(field, green, to_z, from_z)


def collect(field, phi, orbs, left, right):
    given = (phi, orbs, left, right)
    shapes = (jax.ShapeDtypeStruct(orbs.shape, jnp.float32), jax.ShapeDtypeStruct((2, SENT, 2, N, N), jnp.float32))
    return pl.pallas_call(
        gather_kernel,
        grid=(SENT, ORBS),
        out_shape=shapes,
        in_specs=[FIELD_BLOCK] + [whole(array) for array in given],
        out_specs=tuple(whole(shape) for shape in shapes),
        scratch_shapes=[pltpu.VMEM((PLANES * N, N), jnp.float32)],
        compiler_params=params(),
        cost_estimate=cost(FIELDS * PLANES),
    )(field, *given)


def wavenumber(idx):
    shifted = jnp.where(idx < N // 2, idx, idx - N)
    return 2.0 * math.pi / (N * SPACING) * shifted.astype(jnp.float32)


def green_table(group):
    every = jnp.arange(N, dtype=jnp.int32)
    g_y = wavenumber(group * LOCAL + jnp.arange(LOCAL, dtype=jnp.int32))[:, None, None]
    g_z = wavenumber(every)[None, :, None]
    g_x = wavenumber(every)[None, None, :]
    ratio = (g_z * g_z + g_y * g_y + g_x * g_x) / (4.0 * OMEGA * OMEGA)
    safe = jnp.where(ratio > 0, ratio, 1.0)
    kernel = math.pi / (OMEGA * OMEGA) * jnp.where(ratio > 0, -jnp.expm1(-safe) / safe, 1.0)
    return kernel * (1.0 / N**3)


def over_core(array):
    return lax.ppermute(array, "fft", [(i, i ^ 1) for i in range(16)])


EVERY = ("band", "fft")
POOL_CORES = [
    [(4 * pool + k) * 16 + 2 * chip + c for c in range(2) for k in range(4)] for pool in range(4) for chip in range(8)
]
LINES = [[(4 * pool + k) * 16 + 2 * chip + c for chip in range(8) for k in range(4)] for pool in range(4) for c in range(2)]
POOLS = [[4 * pool + k for k in range(4)] for pool in range(4)]
ACROSS = [[4 * pool + k for pool in range(4)] for k in range(4)]


def swap(array, axis, groups):
    return lax.all_to_all(array, axis, 0, 0, axis_index_groups=groups)


def spread_out(array, axis, groups):
    return swap(jnp.broadcast_to(array[None], (4,) + array.shape), axis, groups)


def to_pools(array, moves):
    return lax.ppermute(array, "band", [(4 * a + k, 4 * b + k) for a, b in moves for k in range(4)])


def per_device(orbitals):
    place, band = lax.axis_index("fft"), lax.axis_index("band")
    core, pool = place % 2, band // 4
    left, right, to_z, from_z = (jnp.asarray(t) for t in cas_tables())
    green = green_table(place // 2 * 4 + band % 4)

    orbs = swap(orbitals.reshape(8, 2, N, N), EVERY, POOL_CORES).reshape(2, ORBS, 2, N, N)
    near = orbs[:, 0]
    across = to_pools(near, [(0, 2), (2, 0)])
    above = to_pools(near, [(0, 1), (2, 3)])
    below = to_pools(near, [(0, 3), (2, 1)])

    def pick(*options):
        return lax.select_n(pool, *options)

    mine = jnp.stack([pick(near, above, across, below), pick(across, below, near, above)])
    other = over_core(mine)
    phi = jnp.stack([jnp.where(core == 0, mine, other), jnp.where(core == 0, other, mine)], 1)
    phi = phi.reshape((SENT,) + phi.shape[2:])

    field = swap(spread(phi, orbs, left, right), EVERY, LINES)
    field = swap(lines(field, green, to_z, from_z), EVERY, LINES)
    applied, owner = collect(field, phi, orbs, left, right)

    owner = jnp.where(core == 0, owner[0], owner[1]) + over_core(jnp.where(core == 0, owner[1], owner[0]))
    owner = jnp.sum(swap(owner, "band", ACROSS), 0)
    terms = spread_out(spread_out(owner, "band", ACROSS), "band", POOLS)
    terms = jnp.swapaxes(terms, 0, 1).reshape(SENT, SLAB, N, N)
    applied = swap(applied.reshape(8, 2, N, N), EVERY, POOL_CORES).reshape(orbitals.shape)
    return applied, terms


def solution(mesh):
    return jax.shard_map(
        per_device,
        mesh=mesh,
        in_specs=(P("band", "fft", None, None),),
        out_specs=(P("band", "fft", None, None), P(None, "fft", None, None)),
        check_vma=False,
    )
```

time: 663 us -> 303 us (0.46); the launches traced: 655 us -> 302 us
  waiting for transfers between devices: 439 us -> 117 us
  matrix products: 127 us -> 0 us
  blocking collectives: 0 us -> 122 us
  Pallas kernels: 0 us -> 29.8 us
  local copies, waits for them, and re-layouts: 25.2 us -> 6.11 us
  between operations: 14.8 us -> 0.89 us
  other arithmetic: 12.3 us -> 0.74 us
  starting transfers between devices: 36.8 us -> 25.8 us
    psum x2 -> x0, waiting for transfers between devices: 332 us -> none  [the longest x1 171 us: broadcast(): return lax.psum(jnp.where(mine, shard, jnp.zeros_like(shard)), axis)]
    dot_general x40 -> x0, matrix products: 127 us -> none  [along(): return jnp.einsum(form, field, table, precision=lax.Precision.HIGHEST)]
    all_to_all x0 -> x4, blocking collectives: none -> 122 us  [swap(): return lax.all_to_all(array, axis, 0, 0, axis_index_groups=groups)]
    pallas_call x0 -> x3, Pallas kernels: none -> 29.8 us  [the longest x1 12.5 us: lines(): pl.pallas_call(line_kernel, grid=(SENT, ORBS), out_shape=FIELD_SHAPE, in_...]
    all_to_all x8 -> x3, starting transfers between devices: 36.4 us -> 12.7 us  [swap(): return lax.all_to_all(array, axis, 0, 0, axis_index_groups=groups)]
    ppermute x0 -> x5, waiting for transfers between devices: none -> 18.9 us  [the longest x3 15.1 us: to_pools(): lax.ppermute(array, 'band', [(4 * a + k, 4 * b + k) for a, b in moves for...]
    ppermute x0 -> x5, starting transfers between devices: none -> 13.1 us  [the longest x3 12.9 us: to_pools(): lax.ppermute(array, 'band', [(4 * a + k, 4 * b + k) for a, b in moves for...]
    div x4 -> x0, local copies, waits for them, and re-layouts: 10.4 us -> none  [the longest x2 5.2 us: inverse(): (along(real_part, cos_t, form) - along(imag_part, sin_t, form)) / length]
  transfers between devices with their start and end apart: 10 -> 8, of which waited for: 9 -> 7; matrix products, arithmetic and copies ran while one was open for 19% -> 0% of each run, Pallas kernels for 0% -> 0%
where the time goes in v2:
time: 303 us; the launch traced here: 302 us
  blocking collectives  122 us (40%)
  waiting for transfers between devices  117 us (39%)
  Pallas kernels  29.8 us (10%)
  starting transfers between devices  25.8 us (9%)
  local copies, waits for them, and re-layouts  6.11 us (2%)
    all_to_all x4, blocking collectives, swap(): return lax.all_to_all(array, axis, 0, 0, axis_index_groups=groups)  122 us
    all_to_all x3, waiting for transfers between devices, swap(): return lax.all_to_all(array, axis, 0, 0, axis_index_groups=groups)  97.9 us
    ppermute x3, waiting for transfers between devices, to_pools(): lax.ppermute(array, 'band', [(4 * a + k, 4 * b + k) for a, b in moves for...  15.1 us
    ppermute x3, starting transfers between devices, to_pools(): lax.ppermute(array, 'band', [(4 * a + k, 4 * b + k) for a, b in moves for...  12.9 us
    all_to_all x3, starting transfers between devices, swap(): return lax.all_to_all(array, axis, 0, 0, axis_index_groups=groups)  12.7 us
    pallas_call x1, Pallas kernels, lines(): pl.pallas_call(line_kernel, grid=(SENT, ORBS), out_shape=FIELD_SHAPE, in_...  12.5 us
    pallas_call x1, Pallas kernels, collect(): pl.pallas_call(gather_kernel, grid=(SENT, ORBS), out_shape=shapes, in_spe...  9.66 us
    pallas_call x1, Pallas kernels, spread(): pl.pallas_call(spread_kernel, grid=(SENT, ORBS), out_shape=FIELD_SHAPE, i...  7.66 us
  transfers between devices with their start and end apart: 8, of which 7 were waited for; matrix products, arithmetic and copies ran while one was open for 0% of the time, Pallas kernels for 0%

profile of v2, /device:TPU:2, one launch (start us, length us, event | category | flops | bytes accessed | tf_op | source)
XLA Modules:
  0.0 301.8 jit_solution(2359354167289478986)
XLA Ops:
  0.6 22.3 %all_to_all.35 = f32[8,2,128,128]{3,2,1,0:T(8,128)S(1)} all-to-all(f32[8,2,128,128]{3,2,1,0:T(8,128)} %bitcast.34), channel_id=1, replica_groups={{0,16,32,48,1,17,33,49},{2,18,34,50,3,19,35,51},{4,20,36,52,5,21,37,53}..., dimensions={0} | all-to-all | bytes 2097152 | tf_op jit(solution)/shard_map/all_to_all | solution.py:199
  23.0 5.2 %collective-permute-start = (f32[2,2,128,128]{3,2,1,0:T(8,128)S(1)}, f32[2,2,128,128]{3,2,1,0:T(8,128)S(1)}, u32[]{:S(2)}, u32[]{:S(2)}) collective-permute-start(f32[2,2,128,128]{3,2,1,0:T(8,128)S(1)} %slice_bitcast_fusion), channel_id=1, source_target_pairs={{0,64},{16,80},{32,96},{48,112},{128,192},{144,208},{160,224},{176... | collective-permute-start | bytes 786440 | tf_op jit(solution)/shard_map/ppermute | solution.py:207
  28.2 6.4 %collective-permute-start.1 = (f32[2,2,128,128]{3,2,1,0:T(8,128)S(1)}, f32[2,2,128,128]{3,2,1,0:T(8,128)S(1)}, u32[]{:S(2)}, u32[]{:S(2)}) collective-permute-start(f32[2,2,128,128]{3,2,1,0:T(8,128)S(1)} %slice_bitcast_fusion), channel_id=1, source_target_pairs={{0,128},{16,144},{32,160},{48,176},{128,0},{144,16},{160,32},{176,... | collective-permute-start | bytes 786440 | tf_op jit(solution)/shard_map/ppermute | solution.py:207
  34.6 1.3 collective-permute-start.2
  35.9 0.0 copy-start.3
  36.0 0.0 copy-start.4
  36.0 0.0 collective-permute-done
  36.0 8.8 %collective-permute-done.1 = f32[2,2,128,128]{3,2,1,0:T(8,128)S(1)} collective-permute-done((f32[2,2,128,128]{3,2,1,0:T(8,128)S(1)}, f32[2,2,128,128]{3,2,1,0:T(8,128)S(1)}, u32[]{:S(2)}, u32[]{:S(2)}) %collective-permute-start.1) | collective-permute-done | bytes 262176 | tf_op jit(solution)/shard_map/ppermute | solution.py:207
  44.7 6.4 %collective-permute-done.2 = f32[2,2,128,128]{3,2,1,0:T(8,128)S(1)} collective-permute-done((f32[2,2,128,128]{3,2,1,0:T(8,128)S(1)}, f32[2,2,128,128]{3,2,1,0:T(8,128)S(1)}, u32[]{:S(2)}, u32[]{:S(2)}) %collective-permute-start.2) | collective-permute-done | bytes 262176 | tf_op jit(solution)/shard_map/ppermute | solution.py:207
  51.1 0.1 select_bitcast_fusion.4
  51.2 0.1 collective-permute-start.3
  51.3 1.9 collective-permute-done.3
  53.2 0.1 select_bitcast_fusion.2
  53.3 0.1 pad_maximum_fusion
  53.4 0.1 copy.9
  53.4 0.0 copy-done.3
  53.5 0.0 copy-done.4
  53.5 7.7 %shard_map.68 = f32[32,16,16,128]{3,2,1,0:T(8,128)S(1)} custom-call(f32[4,2,2,128,128]{4,3,2,1,0:T(8,128)S(1)} %bitcast.30, f32[2,4,2,128,128]{4,3,2,1,0:T(8,128)S(1)} %bitcast.28, bf16[128,256]{1,0:T(8,128)(2,1)S(1)} %copy-done.4, bf16[256,256]{1,0:T(8,128)(2,1)S(1)} %copy-done.3), custom_call_target="tpu_custom_call" | custom-call | flops 2147483648 | bytes 12582912 | tf_op jit(solution)/shard_map/pallas_call | solution.py:131
  61.1 0.0 copy-start
  61.1 2.0 copy-done
  63.1 0.0 copy-start.1
  63.1 0.0 copy-start.2
  63.1 5.6 %all-to-all-start.1 = ((f32[32,16,16,128]{3,2,1,0:T(8,128)}), f32[32,16,16,128]{3,2,1,0:T(8,128)}, u32[]{:S(2)}, u32[]{:S(2)}) async-start(f32[32,16,16,128]{3,2,1,0:T(8,128)} %copy-done), calls=%async_computation.1 | async-start | bytes 8388608 | tf_op jit(solution)/shard_map/all_to_all | solution.py:199
  68.8 0.1 broadcast_add_fusion
  68.8 0.2 fusion.green_ref
  69.1 56.0 %all-to-all-done.1.in_ref = f32[32,16,16,128]{3,2,1,0:T(8,128)} async-done(((f32[32,16,16,128]{3,2,1,0:T(8,128)}), f32[32,16,16,128]{3,2,1,0:T(8,128)}, u32[]{:S(2)}, u32[]{:S(2)}) %all-to-all-start.1) | async-done | bytes 4194336 | tf_op jit(solution)/shard_map/all_to_all | solution.py:199
  125.0 0.0 copy-done.1
  125.0 0.0 copy-done.2
  125.0 12.5 %shard_map.69 = f32[32,16,16,128]{3,2,1,0:T(8,128)S(1)} custom-call(f32[32,16,16,128]{3,2,1,0:T(8,128)} %all-to-all-done.1.in_ref, f32[4,128,128]{2,1,0:T(8,128)S(1)} %fusion.green_ref, bf16[128,256]{1,0:T(8,128)(2,1)S(1)} %copy-done.1, bf16[128,256]{1,0:T(8,128)(2,1)S(1)} %copy-done.2), custom_call_target="tpu_custom_call" | custom-call | flops 2147483648 | bytes 12582912 | tf_op jit(solution)/shard_map/pallas_call | solution.py:143
  137.5 57.7 %all_to_all.36.in_ref = f32[32,16,16,128]{3,2,1,0:T(8,128)S(1)} all-to-all(f32[32,16,16,128]{3,2,1,0:T(8,128)S(1)} %shard_map.69), channel_id=1, replica_groups={{0,16,32,48,2,18,34,50,4,20,36,52,6,22,38,54,8,24,40,56,10,26,42,58,12,..., dimensions={0} | all-to-all | bytes 8388608 | tf_op jit(solution)/shard_map/all_to_all | solution.py:199
  195.2 9.7 %shard_map.70 = (f32[2,4,2,128,128]{4,3,2,1,0:T(8,128)}, f32[2,4,2,128,128]{4,3,2,1,0:T(8,128)S(1)}) custom-call(f32[32,16,16,128]{3,2,1,0:T(8,128)S(1)} %all_to_all.36.in_ref, f32[4,2,2,128,128]{4,3,2,1,0:T(8,128)S(1)} %bitcast.31, f32[2,4,2,128,128]{4,3,2,1,0:T(8,128)S(1)} %bitcast.29, bf16[128,256]{1,0:T(8,128)(2,1)S(1)} %copy-done.4, ...), custom_call_target="tpu_custom_call" | custom-call | flops 2147483648 | bytes 12582912 | tf_op jit(solution)/shard_map/pallas_call | solution.py:157
  204.9 0.1 select_bitcast_fusion
  204.9 0.1 collective-permute-start.4
  205.1 1.9 collective-permute-done.4
  206.9 0.1 bitcast_add_fusion
  207.0 21.9 %all_to_all.37 = f32[4,2,128,128]{3,2,1,0:T(8,128)S(1)} all-to-all(f32[4,2,128,128]{3,2,1,0:T(8,128)S(1)} %bitcast_add_fusion), channel_id=1, replica_groups={{0,64,128,192},{16,80,144,208},{32,96,160,224},{48,112,176,240},{1,65,1..., dimensions={0} | all-to-all | bytes 1048576 | tf_op jit(solution)/shard_map/all_to_all | solution.py:199
  228.9 3.6 %all-to-all-start.3 = ((f32[8,2,128,128]{3,2,1,0:T(8,128)}), f32[8,2,128,128]{3,2,1,0:T(8,128)S(1)}, u32[]{:S(2)}, u32[]{:S(2)}) async-start(f32[8,2,128,128]{3,2,1,0:T(8,128)} %bitcast.8), calls=%async_computation.3 | async-start | bytes 2097152 | tf_op jit(solution)/shard_map/all_to_all | solution.py:199
  232.5 16.3 %all-to-all-done.3 = f32[8,2,128,128]{3,2,1,0:T(8,128)S(1)} async-done(((f32[8,2,128,128]{3,2,1,0:T(8,128)}), f32[8,2,128,128]{3,2,1,0:T(8,128)S(1)}, u32[]{:S(2)}, u32[]{:S(2)}) %all-to-all-start.3) | async-done | bytes 1048608 | tf_op jit(solution)/shard_map/all_to_all | solution.py:199
  248.8 19.7 %all_to_all.38 = f32[4,2,128,128]{3,2,1,0:T(8,128)S(1)} all-to-all(f32[4,2,128,128]{3,2,1,0:T(8,128)S(1)} %broadcast_in_dim.10), channel_id=1, replica_groups={{0,64,128,192},{16,80,144,208},{32,96,160,224},{48,112,176,240},{1,65,1..., dimensions={0} | all-to-all | bytes 1048576 | tf_op jit(solution)/shard_map/all_to_all | solution.py:199
  268.5 1.6 broadcast_in_dim.11
  270.1 3.6 %all-to-all-start.6 = ((f32[4,4,2,128,128]{4,3,2,1,0:T(8,128)}), f32[4,4,2,128,128]{4,3,2,1,0:T(8,128)S(1)}, u32[]{:S(2)}, u32[]{:S(2)}) async-start(f32[4,4,2,128,128]{4,3,2,1,0:T(8,128)} %broadcast_in_dim.11), calls=%async_computation.6 | async-start | bytes 4194304 | tf_op jit(solution)/shard_map/all_to_all | solution.py:199
  273.7 25.7 %all-to-all-done.6 = f32[4,4,2,128,128]{4,3,2,1,0:T(8,128)S(1)} async-done(((f32[4,4,2,128,128]{4,3,2,1,0:T(8,128)}), f32[4,4,2,128,128]{4,3,2,1,0:T(8,128)S(1)}, u32[]{:S(2)}, u32[]{:S(2)}) %all-to-all-start.6) | async-done | bytes 2097184 | tf_op jit(solution)/shard_map/all_to_all | solution.py:199
  299.3 1.5 copy.10
  300.8 1.0 copy.12
  (6 shorter events, 0.1 us)
Async XLA Ops:
  23.0 13.0 %collective-permute-start = (f32[2,2,128,128]{3,2,1,0:T(8,128)S(1)}, f32[2,2,128,128]{3,2,1,0:T(8,128)S(1)}, u32[]{:S(2)}, u32[]{:S(2)}) collective-permute-start(f32[2,2,128,128]{3,2,1,0:T(8,128)S(1)} %slice_bitcast_fusion), channel_id=1, source_target_pairs={{0,64},{16,80},{32,96},{48,112},{128,192},{144,208},{160,224},{176... | collective-permute-start | bytes 786440 | tf_op jit(solution)/shard_map/ppermute | solution.py:207
  28.2 16.5 %collective-permute-start.1 = (f32[2,2,128,128]{3,2,1,0:T(8,128)S(1)}, f32[2,2,128,128]{3,2,1,0:T(8,128)S(1)}, u32[]{:S(2)}, u32[]{:S(2)}) collective-permute-start(f32[2,2,128,128]{3,2,1,0:T(8,128)S(1)} %slice_bitcast_fusion), channel_id=1, source_target_pairs={{0,128},{16,144},{32,160},{48,176},{128,0},{144,16},{160,32},{176,... | collective-permute-start | bytes 786440 | tf_op jit(solution)/shard_map/ppermute | solution.py:207
  34.6 16.5 %collective-permute-start.2 = (f32[2,2,128,128]{3,2,1,0:T(8,128)S(1)}, f32[2,2,128,128]{3,2,1,0:T(8,128)S(1)}, u32[]{:S(2)}, u32[]{:S(2)}) collective-permute-start(f32[2,2,128,128]{3,2,1,0:T(8,128)S(1)} %slice_bitcast_fusion), channel_id=1, source_target_pairs={{0,192},{16,208},{32,224},{48,240},{128,64},{144,80},{160,96},{176... | collective-permute-start | bytes 786440 | tf_op jit(solution)/shard_map/ppermute | solution.py:207
  35.9 17.5 %copy-start.3 = (bf16[256,256]{1,0:T(8,128)(2,1)S(1)}, bf16[256,256]{1,0:T(8,128)(2,1)}, u32[]{:S(2)}) copy-start(bf16[256,256]{1,0:T(8,128)(2,1)} %constant.84.clone.right_ref) | copy-start | bytes 393220
  36.0 17.5 %copy-start.4 = (bf16[128,256]{1,0:T(8,128)(2,1)S(1)}, bf16[128,256]{1,0:T(8,128)(2,1)}, u32[]{:S(2)}) copy-start(bf16[128,256]{1,0:T(8,128)(2,1)} %constant.83.clone.left_ref) | copy-start | bytes 196612
  51.2 2.0 collective-permute-start.3
  61.1 2.0 copy-start
  63.1 61.9 %copy-start.1 = (bf16[128,256]{1,0:T(8,128)(2,1)S(1)}, bf16[128,256]{1,0:T(8,128)(2,1)}, u32[]{:S(2)}) copy-start(bf16[128,256]{1,0:T(8,128)(2,1)} %constant.85.clone.to_z_ref) | copy-start | bytes 196612
  63.1 61.9 %copy-start.2 = (bf16[128,256]{1,0:T(8,128)(2,1)S(1)}, bf16[128,256]{1,0:T(8,128)(2,1)}, u32[]{:S(2)}) copy-start(bf16[128,256]{1,0:T(8,128)(2,1)} %constant.86.clone.from_z_ref) | copy-start | bytes 196612
  63.1 61.9 %all-to-all-start.1 = ((f32[32,16,16,128]{3,2,1,0:T(8,128)}), f32[32,16,16,128]{3,2,1,0:T(8,128)}, u32[]{:S(2)}, u32[]{:S(2)}) async-start(f32[32,16,16,128]{3,2,1,0:T(8,128)} %copy-done), calls=%async_computation.1 | async-start | bytes 8388608 | tf_op jit(solution)/shard_map/all_to_all | solution.py:199
  204.9 2.0 collective-permute-start.4
  228.9 19.9 %all-to-all-start.3 = ((f32[8,2,128,128]{3,2,1,0:T(8,128)}), f32[8,2,128,128]{3,2,1,0:T(8,128)S(1)}, u32[]{:S(2)}, u32[]{:S(2)}) async-start(f32[8,2,128,128]{3,2,1,0:T(8,128)} %bitcast.8), calls=%async_computation.3 | async-start | bytes 2097152 | tf_op jit(solution)/shard_map/all_to_all | solution.py:199
  270.1 29.3 %all-to-all-start.6 = ((f32[4,4,2,128,128]{4,3,2,1,0:T(8,128)}), f32[4,4,2,128,128]{4,3,2,1,0:T(8,128)S(1)}, u32[]{:S(2)}, u32[]{:S(2)}) async-start(f32[4,4,2,128,128]{4,3,2,1,0:T(8,128)} %broadcast_in_dim.11), calls=%async_computation.6 | async-start | bytes 4194304 | tf_op jit(solution)/shard_map/all_to_all | solution.py:199

commit v3 on v2

v3 whole, which is shorter than its diff:
```python
import functools
import math

import jax
import jax.numpy as jnp
import ml_dtypes
import numpy as np
from jax import lax
from jax.experimental import pallas as pl
from jax.experimental.pallas import tpu as pltpu
from jax.sharding import PartitionSpec as P

N = 128
SPACING = 0.29
OMEGA = 0.106
MIX = -0.25
VMEM = 32 * 1024 * 1024
SLAB = 8
PLANES = 4
ORBS = 4
SENT = 4
GROUP = 32
LOCAL = N // GROUP
ROWS = ORBS * PLANES


def split(full):
    high = full.astype(ml_dtypes.bfloat16)
    low = (full - high.astype(np.float64)).astype(ml_dtypes.bfloat16)
    return np.concatenate([high, low], -1)


def cas_tables():
    idx = np.arange(N)
    angle = 2.0 * np.pi / N * (idx[:, None] * idx[None, :] % N)
    full = np.cos(angle) + np.sin(angle)
    order = np.array([(2 * chip + c) * SLAB + 2 * q + p for c in range(2) for p in range(2) for chip in range(8) for q in range(4)])
    return [np.concatenate([split(t)] * 2, 0) for t in (full, full[order], full[:, order])]


def halves(value):
    high = value.astype(jnp.bfloat16)
    low = (value - high.astype(jnp.float32)).astype(jnp.bfloat16)
    return high, low


def dot(a, b):
    return lax.dot_general(a, b, (((1,), (0,)), ((), ())), preferred_element_type=jnp.float32)


def rows_by_table(value, right):
    out = dot(jnp.concatenate(halves(value), 1), right)
    return out[:, :N] + out[:, N:]


def turned(value):
    return jnp.concatenate([value[r:r + N].T for r in range(0, value.shape[0], N)], 0)


def spread_kernel(phi_ref, orb_ref, table_ref, out_ref):
    flat = out_ref.reshape(N * ROWS, N)
    for j in range(ORBS):
        density = [phi_ref[0, c, p] * orb_ref[c, j, p] for c in range(2) for p in range(2)]
        field = turned(rows_by_table(jnp.concatenate(density, 0), table_ref[...]))
        field = rows_by_table(field, table_ref[...])
        for z in range(PLANES):
            flat[pl.ds(j * PLANES + z, N, stride=ROWS), :] = field[z * N:(z + 1) * N]


def line_kernel(in_ref, green_ref, to_z_ref, from_z_ref, out_ref):
    given, taken = (ref.reshape(N * ROWS, N) for ref in (in_ref, out_ref))
    for a in range(LOCAL):
        rows = [pl.ds(a * ROWS + r, GROUP, stride=LOCAL * ROWS) for r in range(ROWS)]
        field = turned(jnp.concatenate([given[r, :] for r in rows], 0))
        field = rows_by_table(field, to_z_ref[...]).reshape(ORBS, N, N) * green_ref[a]
        field = turned(rows_by_table(field.reshape(ORBS * N, N), from_z_ref[...]))
        for z, r in enumerate(rows):
            taken[r, :] = field[z * GROUP:(z + 1) * GROUP]


def gather_kernel(in_ref, phi_ref, orb_ref, table_ref, applied_ref, owner_ref):
    item = pl.program_id(0)
    flat = in_ref.reshape(N * ROWS, N)
    owner = None
    for j in range(ORBS):
        field = jnp.concatenate([flat[pl.ds(j * PLANES + z, N, stride=ROWS), :] for z in range(PLANES)], 0)
        field = turned(rows_by_table(field, table_ref[...]))
        result = (rows_by_table(field, table_ref[...]) * MIX).reshape(2, 2, N, N)
        applied = result * phi_ref[0]
        part = result * orb_ref[:, j]
        owner = part if j == 0 else owner + part

        @pl.when(item == 0)
        def _():
            applied_ref[:, j] = applied

        @pl.when(item > 0)
        def _():
            applied_ref[:, j] += applied

    owner_ref[0] = owner


def params():
    return pltpu.CompilerParams(vmem_limit_bytes=VMEM)


def cost(planes):
    return pl.CostEstimate(flops=planes * N * N * 2048, bytes_accessed=planes * N * N * 12, transcendentals=0)


FIELD_SHAPE = jax.ShapeDtypeStruct((GROUP, SENT, LOCAL * ROWS, N), jnp.float32)
FIELD_BLOCK = pl.BlockSpec((GROUP, 1, LOCAL * ROWS, N), lambda i: (0, i, 0, 0))
SENT_BLOCK = pl.BlockSpec((1, 2, 2, N, N), lambda i: (i, 0, 0, 0, 0))


def whole(array):
    return pl.BlockSpec(array.shape, lambda *_: (0,) * array.ndim)


def spread(phi, orbs, table):
    given = (phi, orbs, table)
    return pl.pallas_call(
        spread_kernel,
        grid=(SENT,),
        out_shape=FIELD_SHAPE,
        in_specs=[SENT_BLOCK] + [whole(array) for array in given[1:]],
        out_specs=FIELD_BLOCK,
        compiler_params=params(),
        cost_estimate=cost(SENT * ROWS),
    )(*given)


def lines(field, green, to_z, from_z):
    return pl.pallas_call(
        line_kernel,
        grid=(SENT,),
        out_shape=FIELD_SHAPE,
        in_specs=[FIELD_BLOCK, whole(green), whole(to_z), whole(from_z)],
        out_specs=FIELD_BLOCK,
        compiler_params=params(),
        cost_estimate=cost(SENT * ROWS),
    )(field, green, to_z, from_z)


def collect(field, phi, orbs, table):
    given = (phi, orbs, table)
    shapes = (jax.ShapeDtypeStruct(orbs.shape, jnp.float32), jax.ShapeDtypeStruct((SENT, 2, 2, N, N), jnp.float32))
    return pl.pallas_call(
        gather_kernel,
        grid=(SENT,),
        out_shape=shapes,
        in_specs=[FIELD_BLOCK, SENT_BLOCK] + [whole(array) for array in given[1:]],
        out_specs=(whole(shapes[0]), SENT_BLOCK),
        compiler_params=params(),
        cost_estimate=cost(SENT * ROWS),
    )(field, *given)


def wavenumber(idx):
    shifted = jnp.where(idx < N // 2, idx, idx - N)
    return 2.0 * math.pi / (N * SPACING) * shifted.astype(jnp.float32)


def green_table(group):
    every = jnp.arange(N, dtype=jnp.int32)
    g_y = wavenumber(group * LOCAL + jnp.arange(LOCAL, dtype=jnp.int32))[:, None, None]
    g_z = wavenumber(every)[None, :, None]
    g_x = wavenumber(every)[None, None, :]
    ratio = (g_z * g_z + g_y * g_y + g_x * g_x) / (4.0 * OMEGA * OMEGA)
    safe = jnp.where(ratio > 0, ratio, 1.0)
    kernel = math.pi / (OMEGA * OMEGA) * jnp.where(ratio > 0, -jnp.expm1(-safe) / safe, 1.0)
    return kernel * (1.0 / N**3)


def over_core(array):
    return lax.ppermute(array, "fft", [(i, i ^ 1) for i in range(16)])


EVERY = ("band", "fft")
POOL_CORES = [
    [(4 * pool + k) * 16 + 2 * chip + c for c in range(2) for k in range(4)] for pool in range(4) for chip in range(8)
]
LINES = [[(4 * pool + k) * 16 + 2 * chip + c for chip in range(8) for k in range(4)] for pool in range(4) for c in range(2)]
POOLS = [[4 * pool + k for k in range(4)] for pool in range(4)]
ACROSS = [[4 * pool + k for pool in range(4)] for k in range(4)]


def swap(array, axis, groups):
    return lax.all_to_all(array, axis, 0, 0, axis_index_groups=groups)


def spread_out(array, axis, groups):
    return swap(jnp.broadcast_to(array[None], (4,) + array.shape), axis, groups)


def to_pools(array, moves):
    return lax.ppermute(array, "band", [(4 * a + k, 4 * b + k) for a, b in moves for k in range(4)])


def per_device(orbitals):
    place, band = lax.axis_index("fft"), lax.axis_index("band")
    core, pool = place % 2, band // 4
    table, to_z, from_z = (jnp.asarray(t) for t in cas_tables())
    green = green_table(place // 2 * 4 + band % 4)

    orbs = swap(orbitals.reshape(8, 2, N, N), EVERY, POOL_CORES).reshape(2, ORBS, 2, N, N)
    near = orbs[:, 0]
    across = to_pools(near, [(0, 2), (2, 0)])
    above = to_pools(near, [(0, 1), (2, 3)])
    below = to_pools(near, [(0, 3), (2, 1)])

    def pick(*options):
        return lax.select_n(pool, *options)

    mine = jnp.stack([pick(near, above, across, below), pick(across, below, near, above)])
    other = over_core(mine)
    phi = jnp.stack([jnp.where(core == 0, mine, other), jnp.where(core == 0, other, mine)], 1)
    phi = phi.reshape((SENT,) + phi.shape[2:])

    phi, green, to_z, from_z = lax.optimization_barrier((phi, green, to_z, from_z))
    field = swap(spread(phi, orbs, table), EVERY, LINES)
    field = swap(lines(field, green, to_z, from_z), EVERY, LINES)
    applied, owner = collect(field, phi, orbs, table)

    owner = owner.reshape(2, 2, 2, 2, N, N)
    owner = jnp.where(core == 0, owner[0], owner[1]) + over_core(jnp.where(core == 0, owner[1], owner[0]))
    owner = jnp.sum(swap(jnp.swapaxes(owner, 0, 1).reshape(4, 2, N, N), "band", ACROSS), 0)
    owner = spread_out(owner, "band", ACROSS).reshape(2, 1, 4, N, N)
    both = jnp.concatenate([applied, jnp.broadcast_to(owner, (2, ORBS, 4, N, N))], 2)
    both = swap(both.reshape(8, 6, N, N), EVERY, POOL_CORES)
    applied = both[:, :2].reshape(orbitals.shape)
    terms = both[:, 2:].reshape(2, 4, 2, 2, N, N)
    return applied, jnp.swapaxes(terms, 1, 2).reshape(SENT, SLAB, N, N)


def solution(mesh):
    return jax.shard_map(
        per_device,
        mesh=mesh,
        in_specs=(P("band", "fft", None, None),),
        out_specs=(P("band", "fft", None, None), P(None, "fft", None, None)),
        check_vma=False,
    )
```

time: 303 us -> 271 us (0.89)
  waiting for transfers between devices: 117 us -> 17.5 us
  blocking collectives: 122 us -> 215 us
  starting transfers between devices: 25.8 us -> 11 us
  Pallas kernels: 29.8 us -> 20.3 us
    all_to_all x3 -> x0, waiting for transfers between devices: 97.9 us -> none  [swap(): return lax.all_to_all(array, axis, 0, 0, axis_index_groups=groups)]
    all_to_all x4 -> x6, blocking collectives: 122 us -> 215 us  [swap(): return lax.all_to_all(array, axis, 0, 0, axis_index_groups=groups)]
    all_to_all x3 -> x0, starting transfers between devices: 12.7 us -> none  [swap(): return lax.all_to_all(array, axis, 0, 0, axis_index_groups=groups)]
    pallas_call x3, Pallas kernels: 29.8 us -> 20.3 us  [the longest x1 8.36 us: collect(): pl.pallas_call(gather_kernel, grid=(SENT,), out_shape=shapes, in_specs=[F...]
  transfers between devices with their start and end apart: 8 -> 5, of which waited for: 7 -> 4; matrix products, arithmetic and copies ran while one was open for 0% -> 0% of each run, Pallas kernels for 0% -> 0%
where the time goes in v3:
time: 271 us; the launch traced here: 269 us
  blocking collectives  215 us (79%)
  Pallas kernels  20.3 us (7%)
  waiting for transfers between devices  17.5 us (6%)
  starting transfers between devices  11 us (4%)
  local copies, waits for them, and re-layouts  3.15 us (1%)
    all_to_all x6, blocking collectives, swap(): return lax.all_to_all(array, axis, 0, 0, axis_index_groups=groups)  215 us
    ppermute x3, waiting for transfers between devices, to_pools(): lax.ppermute(array, 'band', [(4 * a + k, 4 * b + k) for a, b in moves for...  14.1 us
    ppermute x3, starting transfers between devices, to_pools(): lax.ppermute(array, 'band', [(4 * a + k, 4 * b + k) for a, b in moves for...  10.8 us
    pallas_call x1, Pallas kernels, collect(): pl.pallas_call(gather_kernel, grid=(SENT,), out_shape=shapes, in_specs=[F...  8.36 us
    pallas_call x1, Pallas kernels, lines(): pl.pallas_call(line_kernel, grid=(SENT,), out_shape=FIELD_SHAPE, in_specs...  7.53 us
  transfers between devices with their start and end apart: 5, of which 4 were waited for; matrix products, arithmetic and copies ran while one was open for 0% of the time, Pallas kernels for 0%

profile of v3, /device:TPU:2, one launch (start us, length us, event | category | flops | bytes accessed | tf_op | source)
XLA Modules:
  0.0 268.8 jit_solution(9133278049887333953)
XLA Ops:
  0.6 22.3 %all_to_all.30 = f32[8,2,128,128]{3,2,1,0:T(8,128)S(1)} all-to-all(f32[8,2,128,128]{3,2,1,0:T(8,128)} %bitcast.38), channel_id=1, replica_groups={{0,16,32,48,1,17,33,49},{2,18,34,50,3,19,35,51},{4,20,36,52,5,21,37,53}..., dimensions={0} | all-to-all | bytes 2097152 | tf_op jit(solution)/shard_map/all_to_all | solution.py:190
  23.0 8.2 %collective-permute-start.1 = (f32[2,2,128,128]{3,2,1,0:T(8,128)S(1)}, f32[2,2,128,128]{3,2,1,0:T(8,128)S(1)}, u32[]{:S(2)}, u32[]{:S(2)}) collective-permute-start(f32[2,2,128,128]{3,2,1,0:T(8,128)S(1)} %slice_bitcast_fusion), channel_id=1, source_target_pairs={{0,128},{16,144},{32,160},{48,176},{128,0},{144,16},{160,32},{176,... | collective-permute-start | bytes 786440 | tf_op jit(solution)/shard_map/ppermute | solution.py:198
  31.2 1.3 collective-permute-start.2
  32.5 1.3 collective-permute-start
  33.9 4.5 %collective-permute-done.1 = f32[2,2,128,128]{3,2,1,0:T(8,128)S(1)} collective-permute-done((f32[2,2,128,128]{3,2,1,0:T(8,128)S(1)}, f32[2,2,128,128]{3,2,1,0:T(8,128)S(1)}, u32[]{:S(2)}, u32[]{:S(2)}) %collective-permute-start.1) | collective-permute-done | bytes 262176 | tf_op jit(solution)/shard_map/ppermute | solution.py:198
  38.4 9.6 %collective-permute-done.2 = f32[2,2,128,128]{3,2,1,0:T(8,128)S(1)} collective-permute-done((f32[2,2,128,128]{3,2,1,0:T(8,128)S(1)}, f32[2,2,128,128]{3,2,1,0:T(8,128)S(1)}, u32[]{:S(2)}, u32[]{:S(2)}) %collective-permute-start.2) | collective-permute-done | bytes 262176 | tf_op jit(solution)/shard_map/ppermute | solution.py:198
  48.0 0.0 collective-permute-done
  48.0 0.1 select_bitcast_fusion.3
  48.1 0.1 collective-permute-start.3
  48.2 0.1 broadcast_add_fusion
  48.3 0.2 fusion.green_ref
  48.5 0.0 copy-start.2
  48.5 1.6 collective-permute-done.3
  50.1 0.1 select_bitcast_fusion.1
  50.2 0.1 pad_maximum_fusion.1
  50.3 0.1 copy.8
  50.4 0.0 copy-done.2
  50.4 4.4 %shard_map.59 = f32[32,4,64,128]{3,2,1,0:T(8,128)S(1)} custom-call(f32[4,2,2,128,128]{4,3,2,1,0:T(8,128)S(1)} %bitcast.31, f32[2,4,2,128,128]{4,3,2,1,0:T(8,128)S(1)} %bitcast.29, bf16[256,256]{1,0:T(8,128)(2,1)S(1)} %copy-done.2), custom_call_target="tpu_custom_call" | custom-call | flops 2147483648 | bytes 12582912 | tf_op jit(solution)/shard_map/pallas_call | solution.py:123
  54.8 0.0 copy-start
  54.8 0.0 copy-start.1
  54.8 57.1 %all_to_all.31.in_ref = f32[32,4,64,128]{3,2,1,0:T(8,128)S(1)} all-to-all(f32[32,4,64,128]{3,2,1,0:T(8,128)S(1)} %shard_map.59), channel_id=1, replica_groups={{0,16,32,48,2,18,34,50,4,20,36,52,6,22,38,54,8,24,40,56,10,26,42,58,12,..., dimensions={0} | all-to-all | bytes 8388608 | tf_op jit(solution)/shard_map/all_to_all | solution.py:190
  111.9 0.0 copy-done
  111.9 0.0 copy-done.1
  111.9 7.5 %shard_map.60 = f32[32,4,64,128]{3,2,1,0:T(8,128)S(1)} custom-call(f32[32,4,64,128]{3,2,1,0:T(8,128)S(1)} %all_to_all.31.in_ref, f32[4,128,128]{2,1,0:T(8,128)S(1)} %fusion.green_ref, bf16[256,256]{1,0:T(8,128)(2,1)S(1)} %copy-done.1, bf16[256,256]{1,0:T(8,128)(2,1)S(1)} %copy-done), custom_call_target="tpu_custom_call" | custom-call | flops 2147483648 | bytes 12582912 | tf_op jit(solution)/shard_map/pallas_call | solution.py:135
  119.5 54.6 %all_to_all.32.in_ref = f32[32,4,64,128]{3,2,1,0:T(8,128)S(1)} all-to-all(f32[32,4,64,128]{3,2,1,0:T(8,128)S(1)} %shard_map.60), channel_id=1, replica_groups={{0,16,32,48,2,18,34,50,4,20,36,52,6,22,38,54,8,24,40,56,10,26,42,58,12,..., dimensions={0} | all-to-all | bytes 8388608 | tf_op jit(solution)/shard_map/all_to_all | solution.py:190
  174.1 8.4 %shard_map.61 = (f32[2,4,2,128,128]{4,3,2,1,0:T(8,128)S(1)}, f32[4,2,2,128,128]{4,3,2,1,0:T(8,128)S(1)}) custom-call(f32[32,4,64,128]{3,2,1,0:T(8,128)S(1)} %all_to_all.32.in_ref, f32[4,2,2,128,128]{4,3,2,1,0:T(8,128)S(1)} %bitcast.32, f32[2,4,2,128,128]{4,3,2,1,0:T(8,128)S(1)} %bitcast.30, bf16[256,256]{1,0:T(8,128)(2,1)S(1)} %copy-done.2), custom_call_target="tpu_custom_call" | custom-call | flops 2147483648 | bytes 12582912 | tf_op jit(solution)/shard_map/pallas_call | solution.py:149
  182.5 0.1 slice_select_fusion
  182.5 0.1 collective-permute-start.4
  182.6 1.9 collective-permute-done.4
  184.5 0.1 add_bitcast_fusion
  184.7 20.8 %all_to_all.33 = f32[4,2,128,128]{3,2,1,0:T(8,128)S(1)} all-to-all(f32[4,2,128,128]{3,2,1,0:T(8,128)S(1)} %bitcast.37), channel_id=1, replica_groups={{0,64,128,192},{16,80,144,208},{32,96,160,224},{48,112,176,240},{1,65,1..., dimensions={0} | all-to-all | bytes 1048576 | tf_op jit(solution)/shard_map/all_to_all | solution.py:190
  205.5 18.4 %all_to_all.34 = f32[4,2,128,128]{3,2,1,0:T(8,128)S(1)} all-to-all(f32[4,2,128,128]{3,2,1,0:T(8,128)S(1)} %broadcast_in_dim.22), channel_id=1, replica_groups={{0,64,128,192},{16,80,144,208},{32,96,160,224},{48,112,176,240},{1,65,1..., dimensions={0} | all-to-all | bytes 1048576 | tf_op jit(solution)/shard_map/all_to_all | solution.py:190
  223.9 0.2 broadcast_in_dim.24
  224.2 0.3 pad_maximum_fusion
  224.5 41.6 %all_to_all.35 = f32[8,6,128,128]{3,2,1,0:T(8,128)S(1)} all-to-all(f32[8,6,128,128]{3,2,1,0:T(8,128)S(1)} %bitcast.33), channel_id=1, replica_groups={{0,16,32,48,1,17,33,49},{2,18,34,50,3,19,35,51},{4,20,36,52,5,21,37,53}..., dimensions={0} | all-to-all | bytes 6291456 | tf_op jit(solution)/shard_map/all_to_all | solution.py:190
  266.1 0.2 slice.26
  266.3 1.5 copy.10
  267.8 1.0 slice.25
  (7 shorter events, 0.2 us)
Async XLA Ops:
  23.0 15.4 %collective-permute-start.1 = (f32[2,2,128,128]{3,2,1,0:T(8,128)S(1)}, f32[2,2,128,128]{3,2,1,0:T(8,128)S(1)}, u32[]{:S(2)}, u32[]{:S(2)}) collective-permute-start(f32[2,2,128,128]{3,2,1,0:T(8,128)S(1)} %slice_bitcast_fusion), channel_id=1, source_target_pairs={{0,128},{16,144},{32,160},{48,176},{128,0},{144,16},{160,32},{176,... | collective-permute-start | bytes 786440 | tf_op jit(solution)/shard_map/ppermute | solution.py:198
  31.2 16.8 %collective-permute-start.2 = (f32[2,2,128,128]{3,2,1,0:T(8,128)S(1)}, f32[2,2,128,128]{3,2,1,0:T(8,128)S(1)}, u32[]{:S(2)}, u32[]{:S(2)}) collective-permute-start(f32[2,2,128,128]{3,2,1,0:T(8,128)S(1)} %slice_bitcast_fusion), channel_id=1, source_target_pairs={{0,192},{16,208},{32,224},{48,240},{128,64},{144,80},{160,96},{176... | collective-permute-start | bytes 786440 | tf_op jit(solution)/shard_map/ppermute | solution.py:198
  32.5 15.5 %collective-permute-start = (f32[2,2,128,128]{3,2,1,0:T(8,128)S(1)}, f32[2,2,128,128]{3,2,1,0:T(8,128)S(1)}, u32[]{:S(2)}, u32[]{:S(2)}) collective-permute-start(f32[2,2,128,128]{3,2,1,0:T(8,128)S(1)} %slice_bitcast_fusion), channel_id=1, source_target_pairs={{0,64},{16,80},{32,96},{48,112},{128,192},{144,208},{160,224},{176... | collective-permute-start | bytes 786440 | tf_op jit(solution)/shard_map/ppermute | solution.py:198
  48.1 2.0 collective-permute-start.3
  48.5 1.9 copy-start.2
  54.8 57.1 %copy-start = (bf16[256,256]{1,0:T(8,128)(2,1)S(1)}, bf16[256,256]{1,0:T(8,128)(2,1)}, u32[]{:S(2)}) copy-start(bf16[256,256]{1,0:T(8,128)(2,1)} %constant.83.clone.from_z_ref) | copy-start | bytes 393220
  54.8 57.1 %copy-start.1 = (bf16[256,256]{1,0:T(8,128)(2,1)S(1)}, bf16[256,256]{1,0:T(8,128)(2,1)}, u32[]{:S(2)}) copy-start(bf16[256,256]{1,0:T(8,128)(2,1)} %constant.82.clone.to_z_ref) | copy-start | bytes 393220
  182.5 2.0 collective-permute-start.4

commit v4 on v3

v4 whole, which is shorter than its diff:
```python
import functools
import math

import jax
import jax.numpy as jnp
import ml_dtypes
import numpy as np
from jax import lax
from jax.experimental import pallas as pl
from jax.experimental.pallas import tpu as pltpu
from jax.sharding import PartitionSpec as P

N = 128
SPACING = 0.29
OMEGA = 0.106
MIX = -0.25
VMEM = 32 * 1024 * 1024
SLAB = 8
PLANES = 4
ORBS = 4
SENT = 4
GROUP = 32
LOCAL = N // GROUP
ROWS = ORBS * PLANES


def split(full):
    high = full.astype(ml_dtypes.bfloat16)
    low = (full - high.astype(np.float64)).astype(ml_dtypes.bfloat16)
    return np.concatenate([high, low], -1)


def cas_tables():
    idx = np.arange(N)
    angle = 2.0 * np.pi / N * (idx[:, None] * idx[None, :] % N)
    full = np.cos(angle) + np.sin(angle)
    to_z = np.zeros((2, 2 * N, 2, N))
    for c in range(2):
        held = [
            (j, (2 * chip + (c ^ q)) * SLAB + 2 * k + p)
            for chip in range(8) for k in range(4) for j in range(2) for q in range(2) for p in range(2)
        ]
        for row, (j, z) in enumerate(held):
            to_z[c, row, j] = full[z]
    to_z = to_z.reshape(2, 2 * N, 2 * N)
    pairs = [np.stack(np.split(split(t), 2, -1), 1) for t in (to_z, to_z.transpose(0, 2, 1))]
    return [np.concatenate([split(full)] * 2, 0)] + pairs


def halves(value):
    high = value.astype(jnp.bfloat16)
    low = (value - high.astype(jnp.float32)).astype(jnp.bfloat16)
    return high, low


def dot(a, b):
    return lax.dot_general(a, b, (((1,), (0,)), ((), ())), preferred_element_type=jnp.float32)


def rows_by_table(value, right):
    out = dot(jnp.concatenate(halves(value), 1), right)
    return out[:, :N] + out[:, N:]


def turned(value):
    return jnp.concatenate([value[r:r + N].T for r in range(0, value.shape[0], N)], 0)


def spread_kernel(phi_ref, phi_beside_ref, orb_ref, orb_beside_ref, table_ref, out_ref):
    fields = []
    for j in range(ORBS):
        density = [phi_ref[0, p] * orb_ref[j, p] for p in range(2)]
        density += [phi_beside_ref[0, p] * orb_beside_ref[j, p] for p in range(2)]
        field = turned(rows_by_table(jnp.concatenate(density, 0), table_ref[...]))
        fields.append(rows_by_table(field, table_ref[...]).reshape(PLANES, N, N))
    for j in range(0, ORBS, 2):
        pair = jnp.swapaxes(jnp.concatenate(fields[j:j + 2], 0), 0, 1)
        out_ref[:, 0, :, j // 2] = pair.reshape(GROUP, LOCAL, 2 * PLANES, N)


def dot3(value, high, low):
    first, second = halves(value)
    return dot(first, high) + dot(second, high) + dot(first, low)


def line_kernel(in_ref, green_ref, to_z_ref, from_z_ref, out_ref):
    for a in range(LOCAL):
        green = jnp.concatenate([green_ref[a]] * 2, 1)
        for j in range(ORBS // 2):
            field = in_ref[:, 0, a, j].reshape(2 * N, N)
            field = jnp.concatenate([field[:N].T, field[N:].T], 1)
            field = dot3(field, to_z_ref[0], to_z_ref[1]) * green
            field = dot3(field, from_z_ref[0], from_z_ref[1])
            field = jnp.concatenate([field[:, :N].T, field[:, N:].T], 0)
            out_ref[:, 0, a, j] = field.reshape(GROUP, 2 * PLANES, N)


def gather_kernel(in_ref, *refs):
    phi_refs, orb_refs, table_ref, applied_refs, owner_refs = refs[:2], refs[2:4], refs[4], refs[5:7], refs[7:]

    @pl.when(pl.program_id(0) == 0)
    def _():
        for ref in applied_refs:
            ref[...] = jnp.zeros_like(ref)

    owners = [None, None]
    for pair in range(ORBS // 2):
        both = jnp.swapaxes(in_ref[:, 0, :, pair].reshape(N, 2 * PLANES, N), 0, 1)
        for j in (2 * pair, 2 * pair + 1):
            field = both[(j % 2) * PLANES:(j % 2 + 1) * PLANES].reshape(PLANES * N, N)
            field = turned(rows_by_table(field, table_ref[...]))
            result = (rows_by_table(field, table_ref[...]) * MIX).reshape(2, 2, N, N)
            for q in range(2):
                applied_refs[q][j] += result[q] * phi_refs[q][0]
                part = result[q] * orb_refs[q][j]
                owners[q] = part if j == 0 else owners[q] + part
    for ref, owner in zip(owner_refs, owners):
        ref[0] = owner


def params():
    return pltpu.CompilerParams(vmem_limit_bytes=VMEM)


def cost(planes):
    return pl.CostEstimate(flops=planes * N * N * 2048, bytes_accessed=planes * N * N * 12, transcendentals=0)


FIELD_SHAPE = jax.ShapeDtypeStruct((GROUP, SENT, LOCAL, ORBS // 2, 2 * PLANES, N), jnp.float32)
FIELD_BLOCK = pl.BlockSpec((GROUP, 1, LOCAL, ORBS // 2, 2 * PLANES, N), lambda i: (0, i, 0, 0, 0, 0))
SENT_BLOCK = pl.BlockSpec((1, 2, N, N), lambda i: (i, 0, 0, 0))
PLANE_SHAPE = jax.ShapeDtypeStruct((4, 2, N, N), jnp.float32)


def whole(array):
    return pl.BlockSpec(array.shape, lambda *_: (0,) * array.ndim)


def spread(phis, orbs, table):
    given = (*orbs, table)
    return pl.pallas_call(
        spread_kernel,
        grid=(SENT,),
        out_shape=FIELD_SHAPE,
        in_specs=[SENT_BLOCK] * 2 + [whole(array) for array in given],
        out_specs=FIELD_BLOCK,
        compiler_params=params(),
        cost_estimate=cost(SENT * ROWS),
    )(*phis, *given)


def lines(field, green, to_z, from_z):
    return pl.pallas_call(
        line_kernel,
        grid=(SENT,),
        out_shape=FIELD_SHAPE,
        in_specs=[FIELD_BLOCK, whole(green), whole(to_z), whole(from_z)],
        out_specs=FIELD_BLOCK,
        compiler_params=params(),
        cost_estimate=cost(SENT * ROWS),
    )(field, green, to_z, from_z)


def collect(field, phis, orbs, table):
    given = (*orbs, table)
    return pl.pallas_call(
        gather_kernel,
        grid=(SENT,),
        out_shape=(PLANE_SHAPE,) * 4,
        in_specs=[FIELD_BLOCK] + [SENT_BLOCK] * 2 + [whole(array) for array in given],
        out_specs=(whole(PLANE_SHAPE),) * 2 + (SENT_BLOCK,) * 2,
        compiler_params=params(),
        cost_estimate=cost(SENT * ROWS),
    )(field, *phis, *given)


def wavenumber(idx):
    shifted = jnp.where(idx < N // 2, idx, idx - N)
    return 2.0 * math.pi / (N * SPACING) * shifted.astype(jnp.float32)


def green_table(group):
    every = jnp.arange(N, dtype=jnp.int32)
    g_y = wavenumber(group * LOCAL + jnp.arange(LOCAL, dtype=jnp.int32))[:, None, None]
    g_z = wavenumber(every)[None, :, None]
    g_x = wavenumber(every)[None, None, :]
    ratio = (g_z * g_z + g_y * g_y + g_x * g_x) / (4.0 * OMEGA * OMEGA)
    safe = jnp.where(ratio > 0, ratio, 1.0)
    kernel = math.pi / (OMEGA * OMEGA) * jnp.where(ratio > 0, -jnp.expm1(-safe) / safe, 1.0)
    return kernel * (1.0 / N**3)


def over_core(array):
    return lax.ppermute(array, "fft", [(i, i ^ 1) for i in range(16)])


EVERY = ("band", "fft")
POOLS = [[4 * pool + k for k in range(4)] for pool in range(4)]
LINES = [[(4 * pool + k) * 16 + 2 * chip + c for chip in range(8) for k in range(4)] for pool in range(4) for c in range(2)]


def swap(array, axis, groups):
    return lax.all_to_all(array, axis, 0, 0, axis_index_groups=groups)


def to_pools(array, moves):
    return lax.ppermute(array, "band", [(4 * a + k, 4 * b + k) for a, b in moves for k in range(4)])


def around(array, distance):
    return to_pools(array, [(p, (p + distance) % 4) for p in range(4)])


def per_device(orbitals):
    place, band = lax.axis_index("fft"), lax.axis_index("band")
    core, pool = place % 2, band // 4
    table, to_z, from_z = (jnp.asarray(t) for t in cas_tables())
    to_z, from_z = (lax.dynamic_index_in_dim(t, core, 0, False) for t in (to_z, from_z))
    green = green_table(place // 2 * 4 + band % 4)

    held = swap(jnp.swapaxes(orbitals.reshape(2, 4, 2, N, N), 0, 1), "band", POOLS)
    near = held[0]
    across = to_pools(near, [(0, 2), (2, 0)])
    above = to_pools(near, [(0, 1), (2, 3)])
    below = to_pools(near, [(0, 3), (2, 1)])
    own = jnp.where(core == 0, held[:, 0], held[:, 1])
    orbs = (own, over_core(jnp.where(core == 0, held[:, 1], held[:, 0])))

    def pick(*options):
        return lax.select_n(pool, *options)

    phi = jnp.concatenate([pick(near, above, across, below), pick(across, below, near, above)])
    phis = (phi, over_core(phi))

    phis, orbs, green, to_z, from_z = lax.optimization_barrier((phis, orbs, green, to_z, from_z))
    field = swap(spread(phis, orbs, table), EVERY, LINES)
    field = swap(lines(field, green, to_z, from_z), EVERY, LINES)
    applied, applied_beside, owner, owner_beside = collect(field, phis, orbs, table)

    owner = owner + over_core(owner_beside)

    def part(distance):
        return lax.dynamic_index_in_dim(owner, lax.rem(pool + distance, 4), 0, False)

    share = part(0) + sum(around(part(d), d) for d in (1, 3, 2))
    shares = [share] + [around(share, d) for d in (1, 2, 3)]
    terms = jnp.stack([lax.select_n(pool, *(shares[(p - i) % 4] for p in range(4))) for i in range(SENT)])
    beside = over_core(applied_beside)
    back = jnp.stack([jnp.where(core == 0, applied, beside), jnp.where(core == 0, beside, applied)], 1)
    both = jnp.concatenate([back, jnp.broadcast_to(terms[None], (4,) + terms.shape)], 1)
    both = jnp.swapaxes(swap(both, "band", POOLS), 0, 1).reshape(6, SLAB, N, N)
    return both[:2], both[2:]


def solution(mesh):
    return jax.shard_map(
        per_device,
        mesh=mesh,
        in_specs=(P("band", "fft", None, None),),
        out_specs=(P("band", "fft", None, None), P(None, "fft", None, None)),
        check_vma=False,
    )
```

time: 271 us -> 261 us (0.963)
  blocking collectives: 215 us -> 151 us
  waiting for transfers between devices: 17.5 us -> 52 us
  starting transfers between devices: 11 us -> 34.8 us
  Pallas kernels: 20.3 us -> 13.8 us
    all_to_all x6 -> x3, blocking collectives: 215 us -> 151 us  [swap(): return lax.all_to_all(array, axis, 0, 0, axis_index_groups=groups)]
    ppermute x3 -> x9, waiting for transfers between devices: 14.1 us -> 34 us  [to_pools(): lax.ppermute(array, 'band', [(4 * a + k, 4 * b + k) for a, b in moves for...]
    ppermute x3 -> x9, starting transfers between devices: 10.8 us -> 28.2 us  [to_pools(): lax.ppermute(array, 'band', [(4 * a + k, 4 * b + k) for a, b in moves for...]
    all_to_all x0 -> x1, waiting for transfers between devices: none -> 15 us  [swap(): return lax.all_to_all(array, axis, 0, 0, axis_index_groups=groups)]
    all_to_all x0 -> x1, starting transfers between devices: none -> 5.82 us  [swap(): return lax.all_to_all(array, axis, 0, 0, axis_index_groups=groups)]
    pallas_call x1, Pallas kernels: 8.36 us -> 4.04 us  [collect(): pl.pallas_call(gather_kernel, grid=(SENT,), out_shape=(PLANE_SHAPE,) * 4,...]
  transfers between devices with their start and end apart: 5 -> 14, of which waited for: 4 -> 11; matrix products, arithmetic and copies ran while one was open for 0% -> 0% of each run, Pallas kernels for 0% -> 0%
where the time goes in v4:
time: 261 us; the launch traced here: 259 us
  blocking collectives  151 us (58%)
  waiting for transfers between devices  52 us (20%)
  starting transfers between devices  34.8 us (13%)
  Pallas kernels  13.8 us (5%)
  local copies, waits for them, and re-layouts  5.58 us (2%)
    all_to_all x3, blocking collectives, swap(): return lax.all_to_all(array, axis, 0, 0, axis_index_groups=groups)  151 us
    ppermute x9, waiting for transfers between devices, to_pools(): lax.ppermute(array, 'band', [(4 * a + k, 4 * b + k) for a, b in moves for...  34 us
    ppermute x9, starting transfers between devices, to_pools(): lax.ppermute(array, 'band', [(4 * a + k, 4 * b + k) for a, b in moves for...  28.2 us
    all_to_all x1, waiting for transfers between devices, swap(): return lax.all_to_all(array, axis, 0, 0, axis_index_groups=groups)  15 us
    all_to_all x1, starting transfers between devices, swap(): return lax.all_to_all(array, axis, 0, 0, axis_index_groups=groups)  5.82 us
    pallas_call x1, Pallas kernels, lines(): pl.pallas_call(line_kernel, grid=(SENT,), out_shape=FIELD_SHAPE, in_specs...  5.59 us
  transfers between devices with their start and end apart: 14, of which 11 were waited for; matrix products, arithmetic and copies ran while one was open for 0% of the time, Pallas kernels for 0%

profile of v4, /device:TPU:2, one launch (start us, length us, event | category | flops | bytes accessed | tf_op | source)
XLA Modules:
  0.0 259.4 jit_solution(547806240234099979)
XLA Ops:
  0.6 0.0 copy-start.1
  0.6 0.0 copy-start.2
  0.7 2.4 copy.10
  3.0 5.8 %all-to-all-start = ((f32[4,2,2,128,128]{4,3,2,1,0:T(8,128)}), f32[4,2,2,128,128]{4,3,2,1,0:T(8,128)S(1)}, u32[]{:S(2)}, u32[]{:S(2)}) async-start(f32[4,2,2,128,128]{4,3,2,1,0:T(8,128)} %copy.10), calls=%async_computation | async-start | bytes 2097152 | tf_op jit(solution)/shard_map/all_to_all | solution.py:203
  8.9 0.0 copy-done.1
  8.9 0.0 copy-done.2
  8.9 0.0 copy-start
  8.9 15.0 %all-to-all-done = f32[4,2,2,128,128]{4,3,2,1,0:T(8,128)S(1)} async-done(((f32[4,2,2,128,128]{4,3,2,1,0:T(8,128)}), f32[4,2,2,128,128]{4,3,2,1,0:T(8,128)S(1)}, u32[]{:S(2)}, u32[]{:S(2)}) %all-to-all-start) | async-done | bytes 1048608 | tf_op jit(solution)/shard_map/all_to_all | solution.py:203
  24.0 5.2 %collective-permute-start = (f32[2,2,128,128]{3,2,1,0:T(8,128)S(1)}, f32[2,2,128,128]{3,2,1,0:T(8,128)S(1)}, u32[]{:S(2)}, u32[]{:S(2)}) collective-permute-start(f32[2,2,128,128]{3,2,1,0:T(8,128)S(1)} %slice_bitcast_fusion.2), channel_id=1, source_target_pairs={{0,64},{16,80},{32,96},{48,112},{128,192},{144,208},{160,224},{176... | collective-permute-start | bytes 786440 | tf_op jit(solution)/shard_map/ppermute | solution.py:207
  29.2 6.4 %collective-permute-start.1 = (f32[2,2,128,128]{3,2,1,0:T(8,128)S(1)}, f32[2,2,128,128]{3,2,1,0:T(8,128)S(1)}, u32[]{:S(2)}, u32[]{:S(2)}) collective-permute-start(f32[2,2,128,128]{3,2,1,0:T(8,128)S(1)} %slice_bitcast_fusion.2), channel_id=1, source_target_pairs={{0,128},{16,144},{32,160},{48,176},{128,0},{144,16},{160,32},{176,... | collective-permute-start | bytes 786440 | tf_op jit(solution)/shard_map/ppermute | solution.py:207
  35.6 1.3 collective-permute-start.2
  36.9 0.1 select_bitcast_fusion.2
  37.0 0.1 collective-permute-start.4
  37.1 0.0 collective-permute-done
  37.1 7.5 %collective-permute-done.1 = f32[2,2,128,128]{3,2,1,0:T(8,128)S(1)} collective-permute-done((f32[2,2,128,128]{3,2,1,0:T(8,128)S(1)}, f32[2,2,128,128]{3,2,1,0:T(8,128)S(1)}, u32[]{:S(2)}, u32[]{:S(2)}) %collective-permute-start.1) | collective-permute-done | bytes 262176 | tf_op jit(solution)/shard_map/ppermute | solution.py:207
  44.6 8.0 %collective-permute-done.2 = f32[2,2,128,128]{3,2,1,0:T(8,128)S(1)} collective-permute-done((f32[2,2,128,128]{3,2,1,0:T(8,128)S(1)}, f32[2,2,128,128]{3,2,1,0:T(8,128)S(1)}, u32[]{:S(2)}, u32[]{:S(2)}) %collective-permute-start.2) | collective-permute-done | bytes 262176 | tf_op jit(solution)/shard_map/ppermute | solution.py:207
  52.6 0.1 select_select_fusion.1
  52.7 0.1 collective-permute-start.3
  52.8 0.1 broadcast_add_fusion
  52.9 0.2 fusion.green_ref
  53.1 0.0 collective-permute-done.4.orb_beside_ref.refs_3_
  53.1 1.6 collective-permute-done.3.phi_beside_ref.refs_1_
  54.7 0.0 copy-done
  54.7 4.2 %shard_map.59 = f32[32,4,4,2,8,128]{5,4,3,2,1,0:T(8,128)S(1)} custom-call(f32[4,2,128,128]{3,2,1,0:T(8,128)S(1)} %pad_maximum_fusion.1.phi_ref.refs_0_, f32[4,2,128,128]{3,2,1,0:T(8,128)S(1)} %collective-permute-done.3.phi_beside_ref.refs_1_, f32[4,2,128,128]{3,2,1,0:T(8,128)S(1)} %get-tuple-element.15.orb_ref.refs_2_, ...), custom_call_target="tpu_custom_call" | custom-call | flops 2147483648 | bytes 12582912 | tf_op jit(solution)/shard_map/pallas_call | solution.py:141
  58.9 55.9 %all_to_all.20.in_ref = f32[32,4,4,2,8,128]{5,4,3,2,1,0:T(8,128)S(1)} all-to-all(f32[32,4,4,2,8,128]{5,4,3,2,1,0:T(8,128)S(1)} %shard_map.59), channel_id=1, replica_groups={{0,16,32,48,2,18,34,50,4,20,36,52,6,22,38,54,8,24,40,56,10,26,42,58,12,..., dimensions={0} | all-to-all | bytes 8388608 | tf_op jit(solution)/shard_map/all_to_all | solution.py:203
  114.8 5.6 %shard_map.60 = f32[32,4,4,2,8,128]{5,4,3,2,1,0:T(8,128)S(1)} custom-call(f32[32,4,4,2,8,128]{5,4,3,2,1,0:T(8,128)S(1)} %all_to_all.20.in_ref, f32[4,128,128]{2,1,0:T(8,128)S(1)} %fusion.green_ref, bf16[2,256,256]{2,1,0:T(8,128)(2,1)S(1)} %get-tuple-element.18.to_z_ref, bf16[2,256,256]{2,1,0:T(8,128)(2,1)S(1)} %get-tuple-element.19.from_z_ref), custom_call_target="tpu_custom_call" | custom-call | flops 2147483648 | bytes 12582912 | tf_op jit(solution)/shard_map/pallas_call | solution.py:153
  120.4 54.6 %all_to_all.21.in_ref = f32[32,4,4,2,8,128]{5,4,3,2,1,0:T(8,128)S(1)} all-to-all(f32[32,4,4,2,8,128]{5,4,3,2,1,0:T(8,128)S(1)} %shard_map.60), channel_id=1, replica_groups={{0,16,32,48,2,18,34,50,4,20,36,52,6,22,38,54,8,24,40,56,10,26,42,58,12,..., dimensions={0} | all-to-all | bytes 8388608 | tf_op jit(solution)/shard_map/all_to_all | solution.py:203
  175.0 4.0 %shard_map.61 = (f32[4,2,128,128]{3,2,1,0:T(8,128)S(1)}, f32[4,2,128,128]{3,2,1,0:T(8,128)S(1)}, f32[4,2,128,128]{3,2,1,0:T(8,128)S(1)}, f32[4,2,128,128]{3,2,1,0:T(8,128)S(1)}) custom-call(f32[32,4,4,2,8,128]{5,4,3,2,1,0:T(8,128)S(1)} %all_to_all.21.in_ref, f32[4,2,128,128]{3,2,1,0:T(8,128)S(1)} %pad_maximum_fusion.1.phi_ref.refs_0_, ...), custom_call_target="tpu_custom_call" | custom-call | flops 2147483648 | bytes 12582912 | tf_op jit(solution)/shard_map/pallas_call | solution.py:166
  179.1 0.1 collective-permute-start.6
  179.2 0.5 collective-permute-start.5
  179.7 1.4 collective-permute-done.6
  181.1 0.1 add.118
  181.2 2.6 collective-permute-start.7
  183.7 2.2 collective-permute-start.8
  185.9 2.3 collective-permute-start.9
  188.2 3.9 %collective-permute-done.7 = f32[2,128,128]{2,1,0:T(8,128)S(1)} collective-permute-done((f32[2,128,128]{2,1,0:T(8,128)S(1)}, f32[2,128,128]{2,1,0:T(8,128)S(1)}, u32[]{:S(2)}, u32[]{:S(2)}) %collective-permute-start.7) | collective-permute-done | bytes 131104 | tf_op jit(solution)/shard_map/ppermute | solution.py:207
  192.1 3.0 %collective-permute-done.8 = f32[2,128,128]{2,1,0:T(8,128)S(1)} collective-permute-done((f32[2,128,128]{2,1,0:T(8,128)S(1)}, f32[2,128,128]{2,1,0:T(8,128)S(1)}, u32[]{:S(2)}, u32[]{:S(2)}) %collective-permute-start.8) | collective-permute-done | bytes 131104 | tf_op jit(solution)/shard_map/ppermute | solution.py:207
  195.1 1.3 collective-permute-done.9
  196.4 4.1 %collective-permute-start.10 = (f32[2,128,128]{2,1,0:T(8,128)S(1)}, f32[2,128,128]{2,1,0:T(8,128)S(1)}, u32[]{:S(2)}, u32[]{:S(2)}) collective-permute-start(f32[2,128,128]{2,1,0:T(8,128)S(1)} %bitcast_add_fusion), channel_id=1, source_target_pairs={{0,64},{16,80},{32,96},{48,112},{64,128},{80,144},{96,160},{112,17... | collective-permute-start | bytes 393224 | tf_op jit(solution)/shard_map/ppermute | solution.py:207
  200.5 2.4 collective-permute-start.11
  202.9 1.8 collective-permute-start.12
  204.7 0.0 collective-permute-done.5
  204.7 0.1 select_bitcast_fusion.1
  204.8 3.5 %collective-permute-done.10 = f32[2,128,128]{2,1,0:T(8,128)S(1)} collective-permute-done((f32[2,128,128]{2,1,0:T(8,128)S(1)}, f32[2,128,128]{2,1,0:T(8,128)S(1)}, u32[]{:S(2)}, u32[]{:S(2)}) %collective-permute-start.10) | collective-permute-done | bytes 131104 | tf_op jit(solution)/shard_map/ppermute | solution.py:207
  208.3 6.1 %collective-permute-done.11 = f32[2,128,128]{2,1,0:T(8,128)S(1)} collective-permute-done((f32[2,128,128]{2,1,0:T(8,128)S(1)}, f32[2,128,128]{2,1,0:T(8,128)S(1)}, u32[]{:S(2)}, u32[]{:S(2)}) %collective-permute-start.11) | collective-permute-done | bytes 131104 | tf_op jit(solution)/shard_map/ppermute | solution.py:207
  214.4 0.7 collective-permute-done.12
  215.1 0.1 select_bitcast_fusion.7
  215.2 0.2 broadcast_in_dim.8
  215.5 0.3 pad_maximum_fusion
  215.8 40.7 %all_to_all.22 = f32[4,6,2,128,128]{4,3,2,1,0:T(8,128)S(1)} all-to-all(f32[4,6,2,128,128]{4,3,2,1,0:T(8,128)S(1)} %pad_maximum_fusion), channel_id=1, replica_groups={{0,16,32,48},{64,80,96,112},{128,144,160,176},{192,208,224,240},{1,17,3..., dimensions={0} | all-to-all | bytes 6291456 | tf_op jit(solution)/shard_map/all_to_all | solution.py:203
  256.5 0.3 copy.19
  256.9 1.5 slice.34
  258.3 1.0 slice.33
  (8 shorter events, 0.2 us)
Async XLA Ops:
  0.6 8.2 %copy-start.1 = (bf16[2,2,256,256]{3,2,1,0:T(8,128)(2,1)S(1)}, bf16[2,2,256,256]{3,2,1,0:T(8,128)(2,1)}, u32[]{:S(2)}) copy-start(bf16[2,2,256,256]{3,2,1,0:T(8,128)(2,1)} %constant.105.clone) | copy-start | bytes 1572868
  0.6 8.2 %copy-start.2 = (bf16[2,2,256,256]{3,2,1,0:T(8,128)(2,1)S(1)}, bf16[2,2,256,256]{3,2,1,0:T(8,128)(2,1)}, u32[]{:S(2)}) copy-start(bf16[2,2,256,256]{3,2,1,0:T(8,128)(2,1)} %constant.106.clone) | copy-start | bytes 1572868
  3.0 20.9 %all-to-all-start = ((f32[4,2,2,128,128]{4,3,2,1,0:T(8,128)}), f32[4,2,2,128,128]{4,3,2,1,0:T(8,128)S(1)}, u32[]{:S(2)}, u32[]{:S(2)}) async-start(f32[4,2,2,128,128]{4,3,2,1,0:T(8,128)} %copy.10), calls=%async_computation | async-start | bytes 2097152 | tf_op jit(solution)/shard_map/all_to_all | solution.py:203
  8.9 45.8 %copy-start = (bf16[256,256]{1,0:T(8,128)(2,1)S(1)}, bf16[256,256]{1,0:T(8,128)(2,1)}, u32[]{:S(2)}) copy-start(bf16[256,256]{1,0:T(8,128)(2,1)} %constant.104.clone.table_ref.refs_4_) | copy-start | bytes 393220
  24.0 13.1 %collective-permute-start = (f32[2,2,128,128]{3,2,1,0:T(8,128)S(1)}, f32[2,2,128,128]{3,2,1,0:T(8,128)S(1)}, u32[]{:S(2)}, u32[]{:S(2)}) collective-permute-start(f32[2,2,128,128]{3,2,1,0:T(8,128)S(1)} %slice_bitcast_fusion.2), channel_id=1, source_target_pairs={{0,64},{16,80},{32,96},{48,112},{128,192},{144,208},{160,224},{176... | collective-permute-start | bytes 786440 | tf_op jit(solution)/shard_map/ppermute | solution.py:207
  29.2 15.4 %collective-permute-start.1 = (f32[2,2,128,128]{3,2,1,0:T(8,128)S(1)}, f32[2,2,128,128]{3,2,1,0:T(8,128)S(1)}, u32[]{:S(2)}, u32[]{:S(2)}) collective-permute-start(f32[2,2,128,128]{3,2,1,0:T(8,128)S(1)} %slice_bitcast_fusion.2), channel_id=1, source_target_pairs={{0,128},{16,144},{32,160},{48,176},{128,0},{144,16},{160,32},{176,... | collective-permute-start | bytes 786440 | tf_op jit(solution)/shard_map/ppermute | solution.py:207
  35.6 17.0 %collective-permute-start.2 = (f32[2,2,128,128]{3,2,1,0:T(8,128)S(1)}, f32[2,2,128,128]{3,2,1,0:T(8,128)S(1)}, u32[]{:S(2)}, u32[]{:S(2)}) collective-permute-start(f32[2,2,128,128]{3,2,1,0:T(8,128)S(1)} %slice_bitcast_fusion.2), channel_id=1, source_target_pairs={{0,192},{16,208},{32,224},{48,240},{128,64},{144,80},{160,96},{176... | collective-permute-start | bytes 786440 | tf_op jit(solution)/shard_map/ppermute | solution.py:207
  37.0 16.2 %collective-permute-start.4 = (f32[4,2,128,128]{3,2,1,0:T(8,128)S(1)}, f32[4,2,128,128]{3,2,1,0:T(8,128)S(1)}, u32[]{:S(2)}, u32[]{:S(2)}) collective-permute-start(f32[4,2,128,128]{3,2,1,0:T(8,128)S(1)} %get-tuple-element.28), channel_id=1, source_target_pairs={{0,1},{1,0},{2,3},{3,2},{4,5},{5,4},{6,7},{7,6},{8,9},{9,8},{10,11... | collective-permute-start | bytes 1572872 | tf_op jit(solution)/shard_map/ppermute | solution.py:194
  52.7 2.0 collective-permute-start.3
  179.1 2.0 collective-permute-start.6
  179.2 25.6 %collective-permute-start.5 = (f32[4,2,128,128]{3,2,1,0:T(8,128)S(1)}, f32[4,2,128,128]{3,2,1,0:T(8,128)S(1)}, u32[]{:S(2)}, u32[]{:S(2)}) collective-permute-start(f32[4,2,128,128]{3,2,1,0:T(8,128)S(1)} %get-tuple-element.21), channel_id=1, source_target_pairs={{0,1},{1,0},{2,3},{3,2},{4,5},{5,4},{6,7},{7,6},{8,9},{9,8},{10,11... | collective-permute-start | bytes 1572872 | tf_op jit(solution)/shard_map/ppermute | solution.py:194
  181.2 10.9 %collective-permute-start.7 = (f32[2,128,128]{2,1,0:T(8,128)S(1)}, f32[2,128,128]{2,1,0:T(8,128)S(1)}, u32[]{:S(2)}, u32[]{:S(2)}) collective-permute-start(f32[2,128,128]{2,1,0:T(8,128)S(1)} %get-tuple-element.36), channel_id=1, source_target_pairs={{0,64},{16,80},{32,96},{48,112},{64,128},{80,144},{96,160},{112,17... | collective-permute-start | bytes 393224 | tf_op jit(solution)/shard_map/ppermute | solution.py:207
  183.7 11.3 %collective-permute-start.8 = (f32[2,128,128]{2,1,0:T(8,128)S(1)}, f32[2,128,128]{2,1,0:T(8,128)S(1)}, u32[]{:S(2)}, u32[]{:S(2)}) collective-permute-start(f32[2,128,128]{2,1,0:T(8,128)S(1)} %get-tuple-element.34), channel_id=1, source_target_pairs={{0,192},{16,208},{32,224},{48,240},{64,0},{80,16},{96,32},{112,48}... | collective-permute-start | bytes 393224 | tf_op jit(solution)/shard_map/ppermute | solution.py:207
  185.9 10.5 %collective-permute-start.9 = (f32[2,128,128]{2,1,0:T(8,128)S(1)}, f32[2,128,128]{2,1,0:T(8,128)S(1)}, u32[]{:S(2)}, u32[]{:S(2)}) collective-permute-start(f32[2,128,128]{2,1,0:T(8,128)S(1)} %get-tuple-element.35), channel_id=1, source_target_pairs={{0,128},{16,144},{32,160},{48,176},{64,192},{80,208},{96,224},{112... | collective-permute-start | bytes 393224 | tf_op jit(solution)/shard_map/ppermute | solution.py:207
  196.4 11.9 %collective-permute-start.10 = (f32[2,128,128]{2,1,0:T(8,128)S(1)}, f32[2,128,128]{2,1,0:T(8,128)S(1)}, u32[]{:S(2)}, u32[]{:S(2)}) collective-permute-start(f32[2,128,128]{2,1,0:T(8,128)S(1)} %bitcast_add_fusion), channel_id=1, source_target_pairs={{0,64},{16,80},{32,96},{48,112},{64,128},{80,144},{96,160},{112,17... | collective-permute-start | bytes 393224 | tf_op jit(solution)/shard_map/ppermute | solution.py:207
  200.5 13.9 %collective-permute-start.11 = (f32[2,128,128]{2,1,0:T(8,128)S(1)}, f32[2,128,128]{2,1,0:T(8,128)S(1)}, u32[]{:S(2)}, u32[]{:S(2)}) collective-permute-start(f32[2,128,128]{2,1,0:T(8,128)S(1)} %bitcast_add_fusion), channel_id=1, source_target_pairs={{0,128},{16,144},{32,160},{48,176},{64,192},{80,208},{96,224},{112... | collective-permute-start | bytes 393224 | tf_op jit(solution)/shard_map/ppermute | solution.py:207
  202.9 12.2 %collective-permute-start.12 = (f32[2,128,128]{2,1,0:T(8,128)S(1)}, f32[2,128,128]{2,1,0:T(8,128)S(1)}, u32[]{:S(2)}, u32[]{:S(2)}) collective-permute-start(f32[2,128,128]{2,1,0:T(8,128)S(1)} %bitcast_add_fusion), channel_id=1, source_target_pairs={{0,192},{16,208},{32,224},{48,240},{64,0},{80,16},{96,32},{112,48}... | collective-permute-start | bytes 393224 | tf_op jit(solution)/shard_map/ppermute | solution.py:207

commit v5 on v4

--- a/solution.py
+++ b/solution.py
@@ -67,15 +67,17 @@
 
 
 def spread_kernel(phi_ref, phi_beside_ref, orb_ref, orb_beside_ref, table_ref, out_ref):
-    fields = []
-    for j in range(ORBS):
-        density = [phi_ref[0, p] * orb_ref[j, p] for p in range(2)]
-        density += [phi_beside_ref[0, p] * orb_beside_ref[j, p] for p in range(2)]
-        field = turned(rows_by_table(jnp.concatenate(density, 0), table_ref[...]))
-        fields.append(rows_by_table(field, table_ref[...]).reshape(PLANES, N, N))
-    for j in range(0, ORBS, 2):
-        pair = jnp.swapaxes(jnp.concatenate(fields[j:j + 2], 0), 0, 1)
-        out_ref[:, 0, :, j // 2] = pair.reshape(GROUP, LOCAL, 2 * PLANES, N)
+    @pl.loop(0, SENT)
+    def _(i):
+        fields = []
+        for j in range(ORBS):
+            density = [phi_ref[i, p] * orb_ref[j, p] for p in range(2)]
+            density += [phi_beside_ref[i, p] * orb_beside_ref[j, p] for p in range(2)]
+            field = turned(rows_by_table(jnp.concatenate(density, 0), table_ref[...]))
+            fields.append(rows_by_table(field, table_ref[...]).reshape(PLANES, N, N))
+        for j in range(0, ORBS, 2):
+            pair = jnp.swapaxes(jnp.concatenate(fields[j:j + 2], 0), 0, 1)
+            out_ref[:, i, :, j // 2] = pair.reshape(GROUP, LOCAL, 2 * PLANES, N)
 
 
 def dot3(value, high, low):
@@ -84,38 +86,39 @@
 
 
 def line_kernel(in_ref, green_ref, to_z_ref, from_z_ref, out_ref):
-    for a in range(LOCAL):
-        green = jnp.concatenate([green_ref[a]] * 2, 1)
-        for j in range(ORBS // 2):
-            field = in_ref[:, 0, a, j].reshape(2 * N, N)
-            field = jnp.concatenate([field[:N].T, field[N:].T], 1)
-            field = dot3(field, to_z_ref[0], to_z_ref[1]) * green
-            field = dot3(field, from_z_ref[0], from_z_ref[1])
-            field = jnp.concatenate([field[:, :N].T, field[:, N:].T], 0)
-            out_ref[:, 0, a, j] = field.reshape(GROUP, 2 * PLANES, N)
+    @pl.loop(0, SENT)
+    def _(i):
+        for a in range(LOCAL):
+            green = jnp.concatenate([green_ref[a]] * 2, 1)
+            for j in range(ORBS // 2):
+                field = in_ref[:, i, a, j].reshape(2 * N, N)
+                field = jnp.concatenate([field[:N].T, field[N:].T], 1)
+                field = dot3(field, to_z_ref[0], to_z_ref[1]) * green
+                field = dot3(field, from_z_ref[0], from_z_ref[1])
+                field = jnp.concatenate([field[:, :N].T, field[:, N:].T], 0)
+                out_ref[:, i, a, j] = field.reshape(GROUP, 2 * PLANES, N)
 
 
 def gather_kernel(in_ref, *refs):
     phi_refs, orb_refs, table_ref, applied_refs, owner_refs = refs[:2], refs[2:4], refs[4], refs[5:7], refs[7:]
-
-    @pl.when(pl.program_id(0) == 0)
-    def _():
-        for ref in applied_refs:
-            ref[...] = jnp.zeros_like(ref)
-
-    owners = [None, None]
-    for pair in range(ORBS // 2):
-        both = jnp.swapaxes(in_ref[:, 0, :, pair].reshape(N, 2 * PLANES, N), 0, 1)
-        for j in (2 * pair, 2 * pair + 1):
-            field = both[(j % 2) * PLANES:(j % 2 + 1) * PLANES].reshape(PLANES * N, N)
-            field = turned(rows_by_table(field, table_ref[...]))
-            result = (rows_by_table(field, table_ref[...]) * MIX).reshape(2, 2, N, N)
-            for q in range(2):
-                applied_refs[q][j] += result[q] * phi_refs[q][0]
-                part = result[q] * orb_refs[q][j]
-                owners[q] = part if j == 0 else owners[q] + part
-    for ref, owner in zip(owner_refs, owners):
-        ref[0] = owner
+    for ref in applied_refs:
+        ref[...] = jnp.zeros_like(ref)
+
+    @pl.loop(0, SENT)
+    def _(i):
+        owners = [None, None]
+        for pair in range(ORBS // 2):
+            both = jnp.swapaxes(in_ref[:, i, :, pair].reshape(N, 2 * PLANES, N), 0, 1)
+            for j in (2 * pair, 2 * pair + 1):
+                field = both[(j % 2) * PLANES:(j % 2 + 1) * PLANES].reshape(PLANES * N, N)
+                field = turned(rows_by_table(field, table_ref[...]))
+                result = (rows_by_table(field, table_ref[...]) * MIX).reshape(2, 2, N, N)
+                for q in range(2):
+                    applied_refs[q][j] += result[q] * phi_refs[q][i]
+                    part = result[q] * orb_refs[q][j]
+                    owners[q] = part if j == 0 else owners[q] + part
+        for ref, owner in zip(owner_refs, owners):
+            ref[i] = owner
 
 
 def params():
@@ -127,51 +130,34 @@
 
 
 FIELD_SHAPE = jax.ShapeDtypeStruct((GROUP, SENT, LOCAL, ORBS // 2, 2 * PLANES, N), jnp.float32)
-FIELD_BLOCK = pl.BlockSpec((GROUP, 1, LOCAL, ORBS // 2, 2 * PLANES, N), lambda i: (0, i, 0, 0, 0, 0))
-SENT_BLOCK = pl.BlockSpec((1, 2, N, N), lambda i: (i, 0, 0, 0))
 PLANE_SHAPE = jax.ShapeDtypeStruct((4, 2, N, N), jnp.float32)
 
 
-def whole(array):
-    return pl.BlockSpec(array.shape, lambda *_: (0,) * array.ndim)
-
-
 def spread(phis, orbs, table):
-    given = (*orbs, table)
     return pl.pallas_call(
         spread_kernel,
-        grid=(SENT,),
         out_shape=FIELD_SHAPE,
-        in_specs=[SENT_BLOCK] * 2 + [whole(array) for array in given],
-        out_specs=FIELD_BLOCK,
         compiler_params=params(),
         cost_estimate=cost(SENT * ROWS),
-    )(*phis, *given)
+    )(*phis, *orbs, table)
 
 
 def lines(field, green, to_z, from_z):
     return pl.pallas_call(
         line_kernel,
-        grid=(SENT,),
         out_shape=FIELD_SHAPE,
-        in_specs=[FIELD_BLOCK, whole(green), whole(to_z), whole(from_z)],
-        out_specs=FIELD_BLOCK,
         compiler_params=params(),
         cost_estimate=cost(SENT * ROWS),
     )(field, green, to_z, from_z)
 
 
 def collect(field, phis, orbs, table):
-    given = (*orbs, table)
     return pl.pallas_call(
         gather_kernel,
-        grid=(SENT,),
         out_shape=(PLANE_SHAPE,) * 4,
-        in_specs=[FIELD_BLOCK] + [SENT_BLOCK] * 2 + [whole(array) for array in given],
-        out_specs=(whole(PLANE_SHAPE),) * 2 + (SENT_BLOCK,) * 2,
         compiler_params=params(),
         cost_estimate=cost(SENT * ROWS),
-    )(field, *phis, *given)
+    )(field, *phis, *orbs, table)
 
 
 def wavenumber(idx):

time: 261 us -> 260 us (level)
  no operation moved by 1% of the time
where the time goes in v5:
time: 260 us; the launch traced here: 258 us
  blocking collectives  151 us (58%)
  waiting for transfers between devices  52 us (20%)
  starting transfers between devices  34.8 us (13%)
  Pallas kernels  12.7 us (5%)
  local copies, waits for them, and re-layouts  5.58 us (2%)
    all_to_all x3, blocking collectives, swap(): return lax.all_to_all(array, axis, 0, 0, axis_index_groups=groups)  151 us
    ppermute x9, waiting for transfers between devices, to_pools(): lax.ppermute(array, 'band', [(4 * a + k, 4 * b + k) for a, b in moves for...  34 us
    ppermute x9, starting transfers between devices, to_pools(): lax.ppermute(array, 'band', [(4 * a + k, 4 * b + k) for a, b in moves for...  28.2 us
    all_to_all x1, waiting for transfers between devices, swap(): return lax.all_to_all(array, axis, 0, 0, axis_index_groups=groups)  15 us
    all_to_all x1, starting transfers between devices, swap(): return lax.all_to_all(array, axis, 0, 0, axis_index_groups=groups)  5.82 us
  transfers between devices with their start and end apart: 14, of which 11 were waited for; matrix products, arithmetic and copies ran while one was open for 0% of the time, Pallas kernels for 0%

profile of v5, /device:TPU:2, one launch (start us, length us, event | category | flops | bytes accessed | tf_op | source)
XLA Modules:
  0.0 258.2 jit_solution(475365784908411145)
XLA Ops:
  0.6 0.0 copy-start.1
  0.6 0.0 copy-start.2
  0.7 2.4 copy.10
  3.0 5.8 %all-to-all-start = ((f32[4,2,2,128,128]{4,3,2,1,0:T(8,128)}), f32[4,2,2,128,128]{4,3,2,1,0:T(8,128)S(1)}, u32[]{:S(2)}, u32[]{:S(2)}) async-start(f32[4,2,2,128,128]{4,3,2,1,0:T(8,128)} %copy.10), calls=%async_computation | async-start | bytes 2097152 | tf_op jit(solution)/shard_map/all_to_all | solution.py:189
  8.9 0.0 copy-done.1
  8.9 0.0 copy-done.2
  8.9 0.0 copy-start
  8.9 15.0 %all-to-all-done = f32[4,2,2,128,128]{4,3,2,1,0:T(8,128)S(1)} async-done(((f32[4,2,2,128,128]{4,3,2,1,0:T(8,128)}), f32[4,2,2,128,128]{4,3,2,1,0:T(8,128)S(1)}, u32[]{:S(2)}, u32[]{:S(2)}) %all-to-all-start) | async-done | bytes 1048608 | tf_op jit(solution)/shard_map/all_to_all | solution.py:189
  24.0 5.2 %collective-permute-start = (f32[2,2,128,128]{3,2,1,0:T(8,128)S(1)}, f32[2,2,128,128]{3,2,1,0:T(8,128)S(1)}, u32[]{:S(2)}, u32[]{:S(2)}) collective-permute-start(f32[2,2,128,128]{3,2,1,0:T(8,128)S(1)} %slice_bitcast_fusion.2), channel_id=1, source_target_pairs={{0,64},{16,80},{32,96},{48,112},{128,192},{144,208},{160,224},{176... | collective-permute-start | bytes 786440 | tf_op jit(solution)/shard_map/ppermute | solution.py:193
  29.2 6.4 %collective-permute-start.1 = (f32[2,2,128,128]{3,2,1,0:T(8,128)S(1)}, f32[2,2,128,128]{3,2,1,0:T(8,128)S(1)}, u32[]{:S(2)}, u32[]{:S(2)}) collective-permute-start(f32[2,2,128,128]{3,2,1,0:T(8,128)S(1)} %slice_bitcast_fusion.2), channel_id=1, source_target_pairs={{0,128},{16,144},{32,160},{48,176},{128,0},{144,16},{160,32},{176,... | collective-permute-start | bytes 786440 | tf_op jit(solution)/shard_map/ppermute | solution.py:193
  35.6 1.3 collective-permute-start.2
  36.9 0.1 select_bitcast_fusion.2
  37.0 0.1 collective-permute-start.4
  37.1 0.0 collective-permute-done
  37.1 7.5 %collective-permute-done.1 = f32[2,2,128,128]{3,2,1,0:T(8,128)S(1)} collective-permute-done((f32[2,2,128,128]{3,2,1,0:T(8,128)S(1)}, f32[2,2,128,128]{3,2,1,0:T(8,128)S(1)}, u32[]{:S(2)}, u32[]{:S(2)}) %collective-permute-start.1) | collective-permute-done | bytes 262176 | tf_op jit(solution)/shard_map/ppermute | solution.py:193
  44.6 8.0 %collective-permute-done.2 = f32[2,2,128,128]{3,2,1,0:T(8,128)S(1)} collective-permute-done((f32[2,2,128,128]{3,2,1,0:T(8,128)S(1)}, f32[2,2,128,128]{3,2,1,0:T(8,128)S(1)}, u32[]{:S(2)}, u32[]{:S(2)}) %collective-permute-start.2) | collective-permute-done | bytes 262176 | tf_op jit(solution)/shard_map/ppermute | solution.py:193
  52.6 0.1 select_select_fusion.1
  52.7 0.1 collective-permute-start.3
  52.8 0.1 broadcast_add_fusion
  52.9 0.2 fusion.green_ref
  53.1 0.0 collective-permute-done.4.orb_beside_ref.refs_3_
  53.1 1.6 collective-permute-done.3.phi_beside_ref.refs_1_
  54.7 0.0 copy-done
  54.7 3.9 %shard_map.59 = f32[32,4,4,2,8,128]{5,4,3,2,1,0:T(8,128)S(1)} custom-call(f32[4,2,128,128]{3,2,1,0:T(8,128)S(1)} %pad_maximum_fusion.1.phi_ref.refs_0_, f32[4,2,128,128]{3,2,1,0:T(8,128)S(1)} %collective-permute-done.3.phi_beside_ref.refs_1_, f32[4,2,128,128]{3,2,1,0:T(8,128)S(1)} %get-tuple-element.15.orb_ref.refs_2_, ...), custom_call_target="tpu_custom_call" | custom-call | flops 2147483648 | bytes 12582912 | tf_op jit(solution)/shard_map/pallas_call | solution.py:137
  58.6 55.9 %all_to_all.20.in_ref = f32[32,4,4,2,8,128]{5,4,3,2,1,0:T(8,128)S(1)} all-to-all(f32[32,4,4,2,8,128]{5,4,3,2,1,0:T(8,128)S(1)} %shard_map.59), channel_id=1, replica_groups={{0,16,32,48,2,18,34,50,4,20,36,52,6,22,38,54,8,24,40,56,10,26,42,58,12,..., dimensions={0} | all-to-all | bytes 8388608 | tf_op jit(solution)/shard_map/all_to_all | solution.py:189
  114.5 5.1 %shard_map.60 = f32[32,4,4,2,8,128]{5,4,3,2,1,0:T(8,128)S(1)} custom-call(f32[32,4,4,2,8,128]{5,4,3,2,1,0:T(8,128)S(1)} %all_to_all.20.in_ref, f32[4,128,128]{2,1,0:T(8,128)S(1)} %fusion.green_ref, bf16[2,256,256]{2,1,0:T(8,128)(2,1)S(1)} %get-tuple-element.18.to_z_ref, bf16[2,256,256]{2,1,0:T(8,128)(2,1)S(1)} %get-tuple-element.19.from_z_ref), custom_call_target="tpu_custom_call" | custom-call | flops 2147483648 | bytes 12582912 | tf_op jit(solution)/shard_map/pallas_call | solution.py:146
  119.6 54.6 %all_to_all.21.in_ref = f32[32,4,4,2,8,128]{5,4,3,2,1,0:T(8,128)S(1)} all-to-all(f32[32,4,4,2,8,128]{5,4,3,2,1,0:T(8,128)S(1)} %shard_map.60), channel_id=1, replica_groups={{0,16,32,48,2,18,34,50,4,20,36,52,6,22,38,54,8,24,40,56,10,26,42,58,12,..., dimensions={0} | all-to-all | bytes 8388608 | tf_op jit(solution)/shard_map/all_to_all | solution.py:189
  174.2 3.7 %shard_map.61 = (f32[4,2,128,128]{3,2,1,0:T(8,128)S(1)}, f32[4,2,128,128]{3,2,1,0:T(8,128)S(1)}, f32[4,2,128,128]{3,2,1,0:T(8,128)S(1)}, f32[4,2,128,128]{3,2,1,0:T(8,128)S(1)}) custom-call(f32[32,4,4,2,8,128]{5,4,3,2,1,0:T(8,128)S(1)} %all_to_all.21.in_ref, f32[4,2,128,128]{3,2,1,0:T(8,128)S(1)} %pad_maximum_fusion.1.phi_ref.refs_0_, ...), custom_call_target="tpu_custom_call" | custom-call | flops 2147483648 | bytes 12582912 | tf_op jit(solution)/shard_map/pallas_call | solution.py:155
  177.9 0.1 collective-permute-start.6
  178.0 0.5 collective-permute-start.5
  178.5 1.4 collective-permute-done.6
  179.9 0.1 add.118
  180.1 2.5 collective-permute-start.7
  182.6 2.2 collective-permute-start.8
  184.8 2.3 collective-permute-start.9
  187.1 3.8 %collective-permute-done.7 = f32[2,128,128]{2,1,0:T(8,128)S(1)} collective-permute-done((f32[2,128,128]{2,1,0:T(8,128)S(1)}, f32[2,128,128]{2,1,0:T(8,128)S(1)}, u32[]{:S(2)}, u32[]{:S(2)}) %collective-permute-start.7) | collective-permute-done | bytes 131104 | tf_op jit(solution)/shard_map/ppermute | solution.py:193
  190.9 3.0 %collective-permute-done.8 = f32[2,128,128]{2,1,0:T(8,128)S(1)} collective-permute-done((f32[2,128,128]{2,1,0:T(8,128)S(1)}, f32[2,128,128]{2,1,0:T(8,128)S(1)}, u32[]{:S(2)}, u32[]{:S(2)}) %collective-permute-start.8) | collective-permute-done | bytes 131104 | tf_op jit(solution)/shard_map/ppermute | solution.py:193
  193.9 1.3 collective-permute-done.9
  195.3 4.1 %collective-permute-start.10 = (f32[2,128,128]{2,1,0:T(8,128)S(1)}, f32[2,128,128]{2,1,0:T(8,128)S(1)}, u32[]{:S(2)}, u32[]{:S(2)}) collective-permute-start(f32[2,128,128]{2,1,0:T(8,128)S(1)} %bitcast_add_fusion), channel_id=1, source_target_pairs={{0,64},{16,80},{32,96},{48,112},{64,128},{80,144},{96,160},{112,17... | collective-permute-start | bytes 393224 | tf_op jit(solution)/shard_map/ppermute | solution.py:193
  199.4 2.4 collective-permute-start.11
  201.8 1.7 collective-permute-start.12
  203.6 0.0 collective-permute-done.5
  203.6 0.1 select_bitcast_fusion.1
  203.6 3.6 %collective-permute-done.10 = f32[2,128,128]{2,1,0:T(8,128)S(1)} collective-permute-done((f32[2,128,128]{2,1,0:T(8,128)S(1)}, f32[2,128,128]{2,1,0:T(8,128)S(1)}, u32[]{:S(2)}, u32[]{:S(2)}) %collective-permute-start.10) | collective-permute-done | bytes 131104 | tf_op jit(solution)/shard_map/ppermute | solution.py:193
  207.3 6.1 %collective-permute-done.11 = f32[2,128,128]{2,1,0:T(8,128)S(1)} collective-permute-done((f32[2,128,128]{2,1,0:T(8,128)S(1)}, f32[2,128,128]{2,1,0:T(8,128)S(1)}, u32[]{:S(2)}, u32[]{:S(2)}) %collective-permute-start.11) | collective-permute-done | bytes 131104 | tf_op jit(solution)/shard_map/ppermute | solution.py:193
  213.3 0.7 collective-permute-done.12
  214.0 0.1 select_bitcast_fusion.7
  214.1 0.2 broadcast_in_dim.8
  214.3 0.3 pad_maximum_fusion
  214.7 40.7 %all_to_all.22 = f32[4,6,2,128,128]{4,3,2,1,0:T(8,128)S(1)} all-to-all(f32[4,6,2,128,128]{4,3,2,1,0:T(8,128)S(1)} %pad_maximum_fusion), channel_id=1, replica_groups={{0,16,32,48},{64,80,96,112},{128,144,160,176},{192,208,224,240},{1,17,3..., dimensions={0} | all-to-all | bytes 6291456 | tf_op jit(solution)/shard_map/all_to_all | solution.py:189
  255.4 0.3 copy.19
  255.7 1.5 slice.34
  257.2 1.0 slice.33
  (8 shorter events, 0.2 us)
Async XLA Ops:
  0.6 8.2 %copy-start.1 = (bf16[2,2,256,256]{3,2,1,0:T(8,128)(2,1)S(1)}, bf16[2,2,256,256]{3,2,1,0:T(8,128)(2,1)}, u32[]{:S(2)}) copy-start(bf16[2,2,256,256]{3,2,1,0:T(8,128)(2,1)} %constant.105.clone) | copy-start | bytes 1572868
  0.6 8.2 %copy-start.2 = (bf16[2,2,256,256]{3,2,1,0:T(8,128)(2,1)S(1)}, bf16[2,2,256,256]{3,2,1,0:T(8,128)(2,1)}, u32[]{:S(2)}) copy-start(bf16[2,2,256,256]{3,2,1,0:T(8,128)(2,1)} %constant.106.clone) | copy-start | bytes 1572868
  3.0 20.9 %all-to-all-start = ((f32[4,2,2,128,128]{4,3,2,1,0:T(8,128)}), f32[4,2,2,128,128]{4,3,2,1,0:T(8,128)S(1)}, u32[]{:S(2)}, u32[]{:S(2)}) async-start(f32[4,2,2,128,128]{4,3,2,1,0:T(8,128)} %copy.10), calls=%async_computation | async-start | bytes 2097152 | tf_op jit(solution)/shard_map/all_to_all | solution.py:189
  8.9 45.8 %copy-start = (bf16[256,256]{1,0:T(8,128)(2,1)S(1)}, bf16[256,256]{1,0:T(8,128)(2,1)}, u32[]{:S(2)}) copy-start(bf16[256,256]{1,0:T(8,128)(2,1)} %constant.104.clone.table_ref.refs_4_) | copy-start | bytes 393220
  24.0 13.1 %collective-permute-start = (f32[2,2,128,128]{3,2,1,0:T(8,128)S(1)}, f32[2,2,128,128]{3,2,1,0:T(8,128)S(1)}, u32[]{:S(2)}, u32[]{:S(2)}) collective-permute-start(f32[2,2,128,128]{3,2,1,0:T(8,128)S(1)} %slice_bitcast_fusion.2), channel_id=1, source_target_pairs={{0,64},{16,80},{32,96},{48,112},{128,192},{144,208},{160,224},{176... | collective-permute-start | bytes 786440 | tf_op jit(solution)/shard_map/ppermute | solution.py:193
  29.2 15.4 %collective-permute-start.1 = (f32[2,2,128,128]{3,2,1,0:T(8,128)S(1)}, f32[2,2,128,128]{3,2,1,0:T(8,128)S(1)}, u32[]{:S(2)}, u32[]{:S(2)}) collective-permute-start(f32[2,2,128,128]{3,2,1,0:T(8,128)S(1)} %slice_bitcast_fusion.2), channel_id=1, source_target_pairs={{0,128},{16,144},{32,160},{48,176},{128,0},{144,16},{160,32},{176,... | collective-permute-start | bytes 786440 | tf_op jit(solution)/shard_map/ppermute | solution.py:193
  35.6 17.0 %collective-permute-start.2 = (f32[2,2,128,128]{3,2,1,0:T(8,128)S(1)}, f32[2,2,128,128]{3,2,1,0:T(8,128)S(1)}, u32[]{:S(2)}, u32[]{:S(2)}) collective-permute-start(f32[2,2,128,128]{3,2,1,0:T(8,128)S(1)} %slice_bitcast_fusion.2), channel_id=1, source_target_pairs={{0,192},{16,208},{32,224},{48,240},{128,64},{144,80},{160,96},{176... | collective-permute-start | bytes 786440 | tf_op jit(solution)/shard_map/ppermute | solution.py:193
  37.0 16.2 %collective-permute-start.4 = (f32[4,2,128,128]{3,2,1,0:T(8,128)S(1)}, f32[4,2,128,128]{3,2,1,0:T(8,128)S(1)}, u32[]{:S(2)}, u32[]{:S(2)}) collective-permute-start(f32[4,2,128,128]{3,2,1,0:T(8,128)S(1)} %get-tuple-element.28), channel_id=1, source_target_pairs={{0,1},{1,0},{2,3},{3,2},{4,5},{5,4},{6,7},{7,6},{8,9},{9,8},{10,11... | collective-permute-start | bytes 1572872 | tf_op jit(solution)/shard_map/ppermute | solution.py:180
  52.7 2.0 collective-permute-start.3
  177.9 2.0 collective-permute-start.6
  178.0 25.5 %collective-permute-start.5 = (f32[4,2,128,128]{3,2,1,0:T(8,128)S(1)}, f32[4,2,128,128]{3,2,1,0:T(8,128)S(1)}, u32[]{:S(2)}, u32[]{:S(2)}) collective-permute-start(f32[4,2,128,128]{3,2,1,0:T(8,128)S(1)} %get-tuple-element.21), channel_id=1, source_target_pairs={{0,1},{1,0},{2,3},{3,2},{4,5},{5,4},{6,7},{7,6},{8,9},{9,8},{10,11... | collective-permute-start | bytes 1572872 | tf_op jit(solution)/shard_map/ppermute | solution.py:180
  180.1 10.9 %collective-permute-start.7 = (f32[2,128,128]{2,1,0:T(8,128)S(1)}, f32[2,128,128]{2,1,0:T(8,128)S(1)}, u32[]{:S(2)}, u32[]{:S(2)}) collective-permute-start(f32[2,128,128]{2,1,0:T(8,128)S(1)} %get-tuple-element.36), channel_id=1, source_target_pairs={{0,64},{16,80},{32,96},{48,112},{64,128},{80,144},{96,160},{112,17... | collective-permute-start | bytes 393224 | tf_op jit(solution)/shard_map/ppermute | solution.py:193
  182.6 11.3 %collective-permute-start.8 = (f32[2,128,128]{2,1,0:T(8,128)S(1)}, f32[2,128,128]{2,1,0:T(8,128)S(1)}, u32[]{:S(2)}, u32[]{:S(2)}) collective-permute-start(f32[2,128,128]{2,1,0:T(8,128)S(1)} %get-tuple-element.34), channel_id=1, source_target_pairs={{0,192},{16,208},{32,224},{48,240},{64,0},{80,16},{96,32},{112,48}... | collective-permute-start | bytes 393224 | tf_op jit(solution)/shard_map/ppermute | solution.py:193
  184.8 10.4 %collective-permute-start.9 = (f32[2,128,128]{2,1,0:T(8,128)S(1)}, f32[2,128,128]{2,1,0:T(8,128)S(1)}, u32[]{:S(2)}, u32[]{:S(2)}) collective-permute-start(f32[2,128,128]{2,1,0:T(8,128)S(1)} %get-tuple-element.35), channel_id=1, source_target_pairs={{0,128},{16,144},{32,160},{48,176},{64,192},{80,208},{96,224},{112... | collective-permute-start | bytes 393224 | tf_op jit(solution)/shard_map/ppermute | solution.py:193
  195.3 12.0 %collective-permute-start.10 = (f32[2,128,128]{2,1,0:T(8,128)S(1)}, f32[2,128,128]{2,1,0:T(8,128)S(1)}, u32[]{:S(2)}, u32[]{:S(2)}) collective-permute-start(f32[2,128,128]{2,1,0:T(8,128)S(1)} %bitcast_add_fusion), channel_id=1, source_target_pairs={{0,64},{16,80},{32,96},{48,112},{64,128},{80,144},{96,160},{112,17... | collective-permute-start | bytes 393224 | tf_op jit(solution)/shard_map/ppermute | solution.py:193
  199.4 13.9 %collective-permute-start.11 = (f32[2,128,128]{2,1,0:T(8,128)S(1)}, f32[2,128,128]{2,1,0:T(8,128)S(1)}, u32[]{:S(2)}, u32[]{:S(2)}) collective-permute-start(f32[2,128,128]{2,1,0:T(8,128)S(1)} %bitcast_add_fusion), channel_id=1, source_target_pairs={{0,128},{16,144},{32,160},{48,176},{64,192},{80,208},{96,224},{112... | collective-permute-start | bytes 393224 | tf_op jit(solution)/shard_map/ppermute | solution.py:193
  201.8 12.2 %collective-permute-start.12 = (f32[2,128,128]{2,1,0:T(8,128)S(1)}, f32[2,128,128]{2,1,0:T(8,128)S(1)}, u32[]{:S(2)}, u32[]{:S(2)}) collective-permute-start(f32[2,128,128]{2,1,0:T(8,128)S(1)} %bitcast_add_fusion), channel_id=1, source_target_pairs={{0,192},{16,208},{32,224},{48,240},{64,0},{80,16},{96,32},{112,48}... | collective-permute-start | bytes 393224 | tf_op jit(solution)/shard_map/ppermute | solution.py:193

commit v6 on v5

--- a/solution.py
+++ b/solution.py
@@ -22,6 +22,7 @@
 GROUP = 32
 LOCAL = N // GROUP
 ROWS = ORBS * PLANES
+PLACES = [(4 * y_lo + x, 2 * z + y_hi) for y_hi in range(2) for y_lo in range(2) for x in range(4) for z in range(2)]
 
 
 def split(full):
@@ -38,7 +39,7 @@
     for c in range(2):
         held = [
             (j, (2 * chip + (c ^ q)) * SLAB + 2 * k + p)
-            for chip in range(8) for k in range(4) for j in range(2) for q in range(2) for p in range(2)
+            for chip, k in PLACES for j in range(2) for q in range(2) for p in range(2)
         ]
         for row, (j, z) in enumerate(held):
             to_z[c, row, j] = full[z]
@@ -121,6 +122,16 @@
             ref[i] = owner
 
 
+def join_kernel(in_ref, applied_ref, terms_ref, sems):
+    refs = [applied_ref.at[i] for i in range(2)] + [terms_ref.at[i] for i in range(SENT)]
+    pairs = [(in_ref.at[k, i], ref.at[pl.ds(2 * k, 2)]) for k in range(4) for i, ref in enumerate(refs)]
+    copies = [pltpu.make_async_copy(source, target, sems.at[n]) for n, (source, target) in enumerate(pairs)]
+    for copy in copies:
+        copy.start()
+    for copy in copies:
+        copy.wait()
+
+
 def params():
     return pltpu.CompilerParams(vmem_limit_bytes=VMEM)
 
@@ -158,6 +169,17 @@
         compiler_params=params(),
         cost_estimate=cost(SENT * ROWS),
     )(field, *phis, *orbs, table)
+
+
+def join(both):
+    return pl.pallas_call(
+        join_kernel,
+        out_shape=tuple(jax.ShapeDtypeStruct((n, SLAB, N, N), jnp.float32) for n in (2, SENT)),
+        in_specs=[pl.BlockSpec(memory_space=pltpu.VMEM)],
+        out_specs=(pl.BlockSpec(memory_space=pl.ANY),) * 2,
+        scratch_shapes=[pltpu.SemaphoreType.DMA((24,))],
+        compiler_params=params(),
+    )(both)
 
 
 def wavenumber(idx):
@@ -182,7 +204,7 @@
 
 EVERY = ("band", "fft")
 POOLS = [[4 * pool + k for k in range(4)] for pool in range(4)]
-LINES = [[(4 * pool + k) * 16 + 2 * chip + c for chip in range(8) for k in range(4)] for pool in range(4) for c in range(2)]
+LINES = [[(4 * pool + k) * 16 + 2 * chip + c for chip, k in PLACES] for pool in range(4) for c in range(2)]
 
 
 def swap(array, axis, groups):
@@ -202,7 +224,7 @@
     core, pool = place % 2, band // 4
     table, to_z, from_z = (jnp.asarray(t) for t in cas_tables())
     to_z, from_z = (lax.dynamic_index_in_dim(t, core, 0, False) for t in (to_z, from_z))
-    green = green_table(place // 2 * 4 + band % 4)
+    green = green_table(band % 2 * 16 + place // 2 * 2 + band // 2 % 2)
 
     held = swap(jnp.swapaxes(orbitals.reshape(2, 4, 2, N, N), 0, 1), "band", POOLS)
     near = held[0]
@@ -234,8 +256,7 @@
     beside = over_core(applied_beside)
     back = jnp.stack([jnp.where(core == 0, applied, beside), jnp.where(core == 0, beside, applied)], 1)
     both = jnp.concatenate([back, jnp.broadcast_to(terms[None], (4,) + terms.shape)], 1)
-    both = jnp.swapaxes(swap(both, "band", POOLS), 0, 1).reshape(6, SLAB, N, N)
-    return both[:2], both[2:]
+    return join(swap(both, "band", POOLS))
 
 
 def solution(mesh):

time: 260 us -> 259 us (level)
  local copies, waits for them, and re-layouts: 5.58 us -> 2.73 us
where the time goes in v6:
time: 259 us; the launch traced here: 257 us
  blocking collectives  150 us (58%)
  waiting for transfers between devices  52.5 us (20%)
  starting transfers between devices  34.6 us (13%)
  Pallas kernels  14.6 us (6%)
  local copies, waits for them, and re-layouts  2.73 us (1%)
    all_to_all x3, blocking collectives, swap(): return lax.all_to_all(array, axis, 0, 0, axis_index_groups=groups)  150 us
    ppermute x9, waiting for transfers between devices, to_pools(): lax.ppermute(array, 'band', [(4 * a + k, 4 * b + k) for a, b in moves for...  34.5 us
    ppermute x9, starting transfers between devices, to_pools(): lax.ppermute(array, 'band', [(4 * a + k, 4 * b + k) for a, b in moves for...  28 us
    all_to_all x1, waiting for transfers between devices, swap(): return lax.all_to_all(array, axis, 0, 0, axis_index_groups=groups)  15 us
    all_to_all x1, starting transfers between devices, swap(): return lax.all_to_all(array, axis, 0, 0, axis_index_groups=groups)  5.82 us
  transfers between devices with their start and end apart: 14, of which 11 were waited for; matrix products, arithmetic and copies ran while one was open for 0% of the time, Pallas kernels for 0%

profile of v6, /device:TPU:2, one launch (start us, length us, event | category | flops | bytes accessed | tf_op | source)
XLA Modules:
  0.0 256.6 jit_solution(13097733691092546253)
XLA Ops:
  0.6 0.0 copy-start.1
  0.6 0.0 copy-start.2
  0.7 2.4 copy.10
  3.0 5.8 %all-to-all-start = ((f32[4,2,2,128,128]{4,3,2,1,0:T(8,128)}), f32[4,2,2,128,128]{4,3,2,1,0:T(8,128)S(1)}, u32[]{:S(2)}, u32[]{:S(2)}) async-start(f32[4,2,2,128,128]{4,3,2,1,0:T(8,128)} %copy.10), calls=%async_computation | async-start | bytes 2097152 | tf_op jit(solution)/shard_map/all_to_all | solution.py:211
  8.9 0.0 copy-done.1
  8.9 0.0 copy-done.2
  8.9 0.0 copy-start
  8.9 15.0 %all-to-all-done = f32[4,2,2,128,128]{4,3,2,1,0:T(8,128)S(1)} async-done(((f32[4,2,2,128,128]{4,3,2,1,0:T(8,128)}), f32[4,2,2,128,128]{4,3,2,1,0:T(8,128)S(1)}, u32[]{:S(2)}, u32[]{:S(2)}) %all-to-all-start) | async-done | bytes 1048608 | tf_op jit(solution)/shard_map/all_to_all | solution.py:211
  24.0 5.2 %collective-permute-start = (f32[2,2,128,128]{3,2,1,0:T(8,128)S(1)}, f32[2,2,128,128]{3,2,1,0:T(8,128)S(1)}, u32[]{:S(2)}, u32[]{:S(2)}) collective-permute-start(f32[2,2,128,128]{3,2,1,0:T(8,128)S(1)} %slice_bitcast_fusion.2), channel_id=1, source_target_pairs={{0,64},{16,80},{32,96},{48,112},{128,192},{144,208},{160,224},{176... | collective-permute-start | bytes 786440 | tf_op jit(solution)/shard_map/ppermute | solution.py:215
  29.2 6.4 %collective-permute-start.1 = (f32[2,2,128,128]{3,2,1,0:T(8,128)S(1)}, f32[2,2,128,128]{3,2,1,0:T(8,128)S(1)}, u32[]{:S(2)}, u32[]{:S(2)}) collective-permute-start(f32[2,2,128,128]{3,2,1,0:T(8,128)S(1)} %slice_bitcast_fusion.2), channel_id=1, source_target_pairs={{0,128},{16,144},{32,160},{48,176},{128,0},{144,16},{160,32},{176,... | collective-permute-start | bytes 786440 | tf_op jit(solution)/shard_map/ppermute | solution.py:215
  35.6 1.3 collective-permute-start.2
  36.9 0.1 select_bitcast_fusion.2
  37.0 0.1 collective-permute-start.4
  37.1 0.0 collective-permute-done
  37.1 7.5 %collective-permute-done.1 = f32[2,2,128,128]{3,2,1,0:T(8,128)S(1)} collective-permute-done((f32[2,2,128,128]{3,2,1,0:T(8,128)S(1)}, f32[2,2,128,128]{3,2,1,0:T(8,128)S(1)}, u32[]{:S(2)}, u32[]{:S(2)}) %collective-permute-start.1) | collective-permute-done | bytes 262176 | tf_op jit(solution)/shard_map/ppermute | solution.py:215
  44.6 8.0 %collective-permute-done.2 = f32[2,2,128,128]{3,2,1,0:T(8,128)S(1)} collective-permute-done((f32[2,2,128,128]{3,2,1,0:T(8,128)S(1)}, f32[2,2,128,128]{3,2,1,0:T(8,128)S(1)}, u32[]{:S(2)}, u32[]{:S(2)}) %collective-permute-start.2) | collective-permute-done | bytes 262176 | tf_op jit(solution)/shard_map/ppermute | solution.py:215
  52.6 0.1 select_select_fusion.1
  52.7 0.1 collective-permute-start.3
  52.8 0.1 broadcast_add_fusion
  52.9 0.2 fusion.green_ref
  53.1 0.0 collective-permute-done.4.orb_beside_ref.refs_3_
  53.1 1.6 collective-permute-done.3.phi_beside_ref.refs_1_
  54.7 0.0 copy-done
  54.7 3.9 %shard_map.59 = f32[32,4,4,2,8,128]{5,4,3,2,1,0:T(8,128)S(1)} custom-call(f32[4,2,128,128]{3,2,1,0:T(8,128)S(1)} %pad_maximum_fusion.1.phi_ref.refs_0_, f32[4,2,128,128]{3,2,1,0:T(8,128)S(1)} %collective-permute-done.3.phi_beside_ref.refs_1_, f32[4,2,128,128]{3,2,1,0:T(8,128)S(1)} %get-tuple-element.15.orb_ref.refs_2_, ...), custom_call_target="tpu_custom_call" | custom-call | flops 2147483648 | bytes 12582912 | tf_op jit(solution)/shard_map/pallas_call | solution.py:148
  58.6 55.7 %all_to_all.20.in_ref = f32[32,4,4,2,8,128]{5,4,3,2,1,0:T(8,128)S(1)} all-to-all(f32[32,4,4,2,8,128]{5,4,3,2,1,0:T(8,128)S(1)} %shard_map.59), channel_id=1, replica_groups={{0,32,2,34,4,36,6,38,8,40,10,42,12,44,14,46,16,48,18,50,20,52,22,54,24,..., dimensions={0} | all-to-all | bytes 8388608 | tf_op jit(solution)/shard_map/all_to_all | solution.py:211
  114.3 5.1 %shard_map.60 = f32[32,4,4,2,8,128]{5,4,3,2,1,0:T(8,128)S(1)} custom-call(f32[32,4,4,2,8,128]{5,4,3,2,1,0:T(8,128)S(1)} %all_to_all.20.in_ref, f32[4,128,128]{2,1,0:T(8,128)S(1)} %fusion.green_ref, bf16[2,256,256]{2,1,0:T(8,128)(2,1)S(1)} %get-tuple-element.18.to_z_ref, bf16[2,256,256]{2,1,0:T(8,128)(2,1)S(1)} %get-tuple-element.19.from_z_ref), custom_call_target="tpu_custom_call" | custom-call | flops 2147483648 | bytes 12582912 | tf_op jit(solution)/shard_map/pallas_call | solution.py:157
  119.5 54.0 %all_to_all.21.in_ref = f32[32,4,4,2,8,128]{5,4,3,2,1,0:T(8,128)S(1)} all-to-all(f32[32,4,4,2,8,128]{5,4,3,2,1,0:T(8,128)S(1)} %shard_map.60), channel_id=1, replica_groups={{0,32,2,34,4,36,6,38,8,40,10,42,12,44,14,46,16,48,18,50,20,52,22,54,24,..., dimensions={0} | all-to-all | bytes 8388608 | tf_op jit(solution)/shard_map/all_to_all | solution.py:211
  173.5 3.7 %shard_map.61 = (f32[4,2,128,128]{3,2,1,0:T(8,128)S(1)}, f32[4,2,128,128]{3,2,1,0:T(8,128)S(1)}, f32[4,2,128,128]{3,2,1,0:T(8,128)S(1)}, f32[4,2,128,128]{3,2,1,0:T(8,128)S(1)}) custom-call(f32[32,4,4,2,8,128]{5,4,3,2,1,0:T(8,128)S(1)} %all_to_all.21.in_ref, f32[4,2,128,128]{3,2,1,0:T(8,128)S(1)} %pad_maximum_fusion.1.phi_ref.refs_0_, ...), custom_call_target="tpu_custom_call" | custom-call | flops 2147483648 | bytes 12582912 | tf_op jit(solution)/shard_map/pallas_call | solution.py:166
  177.2 0.1 collective-permute-start.6
  177.3 0.5 collective-permute-start.5
  177.8 1.4 collective-permute-done.6
  179.2 0.1 add.127
  179.3 2.5 collective-permute-start.7
  181.8 2.2 collective-permute-start.8
  184.0 2.3 collective-permute-start.9
  186.3 4.3 %collective-permute-done.7 = f32[2,128,128]{2,1,0:T(8,128)S(1)} collective-permute-done((f32[2,128,128]{2,1,0:T(8,128)S(1)}, f32[2,128,128]{2,1,0:T(8,128)S(1)}, u32[]{:S(2)}, u32[]{:S(2)}) %collective-permute-start.7) | collective-permute-done | bytes 131104 | tf_op jit(solution)/shard_map/ppermute | solution.py:215
  190.6 2.9 %collective-permute-done.8 = f32[2,128,128]{2,1,0:T(8,128)S(1)} collective-permute-done((f32[2,128,128]{2,1,0:T(8,128)S(1)}, f32[2,128,128]{2,1,0:T(8,128)S(1)}, u32[]{:S(2)}, u32[]{:S(2)}) %collective-permute-start.8) | collective-permute-done | bytes 131104 | tf_op jit(solution)/shard_map/ppermute | solution.py:215
  193.6 1.5 collective-permute-done.9
  195.1 3.5 %collective-permute-start.10 = (f32[2,128,128]{2,1,0:T(8,128)S(1)}, f32[2,128,128]{2,1,0:T(8,128)S(1)}, u32[]{:S(2)}, u32[]{:S(2)}) collective-permute-start(f32[2,128,128]{2,1,0:T(8,128)S(1)} %bitcast_add_fusion), channel_id=1, source_target_pairs={{0,64},{16,80},{32,96},{48,112},{64,128},{80,144},{96,160},{112,17... | collective-permute-start | bytes 393224 | tf_op jit(solution)/shard_map/ppermute | solution.py:215
  198.6 2.6 %collective-permute-start.11 = (f32[2,128,128]{2,1,0:T(8,128)S(1)}, f32[2,128,128]{2,1,0:T(8,128)S(1)}, u32[]{:S(2)}, u32[]{:S(2)}) collective-permute-start(f32[2,128,128]{2,1,0:T(8,128)S(1)} %bitcast_add_fusion), channel_id=1, source_target_pairs={{0,128},{16,144},{32,160},{48,176},{64,192},{80,208},{96,224},{112... | collective-permute-start | bytes 393224 | tf_op jit(solution)/shard_map/ppermute | solution.py:215
  201.2 2.0 collective-permute-start.12
  203.2 0.0 collective-permute-done.5
  203.2 0.1 select_bitcast_fusion.1
  203.3 2.6 %collective-permute-done.10 = f32[2,128,128]{2,1,0:T(8,128)S(1)} collective-permute-done((f32[2,128,128]{2,1,0:T(8,128)S(1)}, f32[2,128,128]{2,1,0:T(8,128)S(1)}, u32[]{:S(2)}, u32[]{:S(2)}) %collective-permute-start.10) | collective-permute-done | bytes 131104 | tf_op jit(solution)/shard_map/ppermute | solution.py:215
  205.9 6.7 %collective-permute-done.11 = f32[2,128,128]{2,1,0:T(8,128)S(1)} collective-permute-done((f32[2,128,128]{2,1,0:T(8,128)S(1)}, f32[2,128,128]{2,1,0:T(8,128)S(1)}, u32[]{:S(2)}, u32[]{:S(2)}) %collective-permute-start.11) | collective-permute-done | bytes 131104 | tf_op jit(solution)/shard_map/ppermute | solution.py:215
  212.6 0.9 collective-permute-done.12
  213.5 0.1 select_bitcast_fusion.7
  213.6 0.2 broadcast_in_dim.8
  213.9 0.3 pad_maximum_fusion
  214.2 40.5 %all_to_all.22.in_ref = f32[4,6,2,128,128]{4,3,2,1,0:T(8,128)S(1)} all-to-all(f32[4,6,2,128,128]{4,3,2,1,0:T(8,128)S(1)} %pad_maximum_fusion), channel_id=1, replica_groups={{0,16,32,48},{64,80,96,112},{128,144,160,176},{192,208,224,240},{1,17,3..., dimensions={0} | all-to-all | bytes 6291456 | tf_op jit(solution)/shard_map/all_to_all | solution.py:211
  254.7 1.8 shard_map.62
  (8 shorter events, 0.2 us)
Async XLA Ops:
  0.6 8.2 %copy-start.1 = (bf16[2,2,256,256]{3,2,1,0:T(8,128)(2,1)S(1)}, bf16[2,2,256,256]{3,2,1,0:T(8,128)(2,1)}, u32[]{:S(2)}) copy-start(bf16[2,2,256,256]{3,2,1,0:T(8,128)(2,1)} %constant.115.clone) | copy-start | bytes 1572868
  0.6 8.2 %copy-start.2 = (bf16[2,2,256,256]{3,2,1,0:T(8,128)(2,1)S(1)}, bf16[2,2,256,256]{3,2,1,0:T(8,128)(2,1)}, u32[]{:S(2)}) copy-start(bf16[2,2,256,256]{3,2,1,0:T(8,128)(2,1)} %constant.116.clone) | copy-start | bytes 1572868
  3.0 20.9 %all-to-all-start = ((f32[4,2,2,128,128]{4,3,2,1,0:T(8,128)}), f32[4,2,2,128,128]{4,3,2,1,0:T(8,128)S(1)}, u32[]{:S(2)}, u32[]{:S(2)}) async-start(f32[4,2,2,128,128]{4,3,2,1,0:T(8,128)} %copy.10), calls=%async_computation | async-start | bytes 2097152 | tf_op jit(solution)/shard_map/all_to_all | solution.py:211
  8.9 45.8 %copy-start = (bf16[256,256]{1,0:T(8,128)(2,1)S(1)}, bf16[256,256]{1,0:T(8,128)(2,1)}, u32[]{:S(2)}) copy-start(bf16[256,256]{1,0:T(8,128)(2,1)} %constant.114.clone.table_ref.refs_4_) | copy-start | bytes 393220
  24.0 13.1 %collective-permute-start = (f32[2,2,128,128]{3,2,1,0:T(8,128)S(1)}, f32[2,2,128,128]{3,2,1,0:T(8,128)S(1)}, u32[]{:S(2)}, u32[]{:S(2)}) collective-permute-start(f32[2,2,128,128]{3,2,1,0:T(8,128)S(1)} %slice_bitcast_fusion.2), channel_id=1, source_target_pairs={{0,64},{16,80},{32,96},{48,112},{128,192},{144,208},{160,224},{176... | collective-permute-start | bytes 786440 | tf_op jit(solution)/shard_map/ppermute | solution.py:215
  29.2 15.4 %collective-permute-start.1 = (f32[2,2,128,128]{3,2,1,0:T(8,128)S(1)}, f32[2,2,128,128]{3,2,1,0:T(8,128)S(1)}, u32[]{:S(2)}, u32[]{:S(2)}) collective-permute-start(f32[2,2,128,128]{3,2,1,0:T(8,128)S(1)} %slice_bitcast_fusion.2), channel_id=1, source_target_pairs={{0,128},{16,144},{32,160},{48,176},{128,0},{144,16},{160,32},{176,... | collective-permute-start | bytes 786440 | tf_op jit(solution)/shard_map/ppermute | solution.py:215
  35.6 17.0 %collective-permute-start.2 = (f32[2,2,128,128]{3,2,1,0:T(8,128)S(1)}, f32[2,2,128,128]{3,2,1,0:T(8,128)S(1)}, u32[]{:S(2)}, u32[]{:S(2)}) collective-permute-start(f32[2,2,128,128]{3,2,1,0:T(8,128)S(1)} %slice_bitcast_fusion.2), channel_id=1, source_target_pairs={{0,192},{16,208},{32,224},{48,240},{128,64},{144,80},{160,96},{176... | collective-permute-start | bytes 786440 | tf_op jit(solution)/shard_map/ppermute | solution.py:215
  37.0 16.2 %collective-permute-start.4 = (f32[4,2,128,128]{3,2,1,0:T(8,128)S(1)}, f32[4,2,128,128]{3,2,1,0:T(8,128)S(1)}, u32[]{:S(2)}, u32[]{:S(2)}) collective-permute-start(f32[4,2,128,128]{3,2,1,0:T(8,128)S(1)} %get-tuple-element.28), channel_id=1, source_target_pairs={{0,1},{1,0},{2,3},{3,2},{4,5},{5,4},{6,7},{7,6},{8,9},{9,8},{10,11... | collective-permute-start | bytes 1572872 | tf_op jit(solution)/shard_map/ppermute | solution.py:202
  52.7 2.0 collective-permute-start.3
  177.2 2.0 collective-permute-start.6
  177.3 26.0 %collective-permute-start.5 = (f32[4,2,128,128]{3,2,1,0:T(8,128)S(1)}, f32[4,2,128,128]{3,2,1,0:T(8,128)S(1)}, u32[]{:S(2)}, u32[]{:S(2)}) collective-permute-start(f32[4,2,128,128]{3,2,1,0:T(8,128)S(1)} %get-tuple-element.21), channel_id=1, source_target_pairs={{0,1},{1,0},{2,3},{3,2},{4,5},{5,4},{6,7},{7,6},{8,9},{9,8},{10,11... | collective-permute-start | bytes 1572872 | tf_op jit(solution)/shard_map/ppermute | solution.py:202
  179.3 11.4 %collective-permute-start.7 = (f32[2,128,128]{2,1,0:T(8,128)S(1)}, f32[2,128,128]{2,1,0:T(8,128)S(1)}, u32[]{:S(2)}, u32[]{:S(2)}) collective-permute-start(f32[2,128,128]{2,1,0:T(8,128)S(1)} %get-tuple-element.36), channel_id=1, source_target_pairs={{0,64},{16,80},{32,96},{48,112},{64,128},{80,144},{96,160},{112,17... | collective-permute-start | bytes 393224 | tf_op jit(solution)/shard_map/ppermute | solution.py:215
  181.8 11.8 %collective-permute-start.8 = (f32[2,128,128]{2,1,0:T(8,128)S(1)}, f32[2,128,128]{2,1,0:T(8,128)S(1)}, u32[]{:S(2)}, u32[]{:S(2)}) collective-permute-start(f32[2,128,128]{2,1,0:T(8,128)S(1)} %get-tuple-element.34), channel_id=1, source_target_pairs={{0,192},{16,208},{32,224},{48,240},{64,0},{80,16},{96,32},{112,48}... | collective-permute-start | bytes 393224 | tf_op jit(solution)/shard_map/ppermute | solution.py:215
  184.0 11.0 %collective-permute-start.9 = (f32[2,128,128]{2,1,0:T(8,128)S(1)}, f32[2,128,128]{2,1,0:T(8,128)S(1)}, u32[]{:S(2)}, u32[]{:S(2)}) collective-permute-start(f32[2,128,128]{2,1,0:T(8,128)S(1)} %get-tuple-element.35), channel_id=1, source_target_pairs={{0,128},{16,144},{32,160},{48,176},{64,192},{80,208},{96,224},{112... | collective-permute-start | bytes 393224 | tf_op jit(solution)/shard_map/ppermute | solution.py:215
  195.1 10.8 %collective-permute-start.10 = (f32[2,128,128]{2,1,0:T(8,128)S(1)}, f32[2,128,128]{2,1,0:T(8,128)S(1)}, u32[]{:S(2)}, u32[]{:S(2)}) collective-permute-start(f32[2,128,128]{2,1,0:T(8,128)S(1)} %bitcast_add_fusion), channel_id=1, source_target_pairs={{0,64},{16,80},{32,96},{48,112},{64,128},{80,144},{96,160},{112,17... | collective-permute-start | bytes 393224 | tf_op jit(solution)/shard_map/ppermute | solution.py:215
  198.6 14.0 %collective-permute-start.11 = (f32[2,128,128]{2,1,0:T(8,128)S(1)}, f32[2,128,128]{2,1,0:T(8,128)S(1)}, u32[]{:S(2)}, u32[]{:S(2)}) collective-permute-start(f32[2,128,128]{2,1,0:T(8,128)S(1)} %bitcast_add_fusion), channel_id=1, source_target_pairs={{0,128},{16,144},{32,160},{48,176},{64,192},{80,208},{96,224},{112... | collective-permute-start | bytes 393224 | tf_op jit(solution)/shard_map/ppermute | solution.py:215
  201.2 12.3 %collective-permute-start.12 = (f32[2,128,128]{2,1,0:T(8,128)S(1)}, f32[2,128,128]{2,1,0:T(8,128)S(1)}, u32[]{:S(2)}, u32[]{:S(2)}) collective-permute-start(f32[2,128,128]{2,1,0:T(8,128)S(1)} %bitcast_add_fusion), channel_id=1, source_target_pairs={{0,192},{16,208},{32,224},{48,240},{64,0},{80,16},{96,32},{112,48}... | collective-permute-start | bytes 393224 | tf_op jit(solution)/shard_map/ppermute | solution.py:215

commit v7 on v6

--- a/solution.py
+++ b/solution.py
@@ -250,8 +250,8 @@
     def part(distance):
         return lax.dynamic_index_in_dim(owner, lax.rem(pool + distance, 4), 0, False)
 
-    share = part(0) + sum(around(part(d), d) for d in (1, 3, 2))
-    shares = [share] + [around(share, d) for d in (1, 2, 3)]
+    share = part(0) + sum(around(part(d), d) for d in (2, 1, 3))
+    shares = {0: share, **{d: around(share, d) for d in (2, 1, 3)}}
     terms = jnp.stack([lax.select_n(pool, *(shares[(p - i) % 4] for p in range(4))) for i in range(SENT)])
     beside = over_core(applied_beside)
     back = jnp.stack([jnp.where(core == 0, applied, beside), jnp.where(core == 0, beside, applied)], 1)

time: 259 us -> 259 us (level)
  transfers between devices with their start and end apart: 14 -> 14, of which waited for: 11 -> 9; matrix products, arithmetic and copies ran while one was open for 0% -> 0% of each run, Pallas kernels for 0% -> 0%
where the time goes in v7:
time: 259 us; the launch traced here: 258 us
  blocking collectives  152 us (59%)
  waiting for transfers between devices  53.8 us (21%)
  starting transfers between devices  32.5 us (13%)
  Pallas kernels  14.6 us (6%)
  local copies, waits for them, and re-layouts  2.73 us (1%)
    all_to_all x3, blocking collectives, swap(): return lax.all_to_all(array, axis, 0, 0, axis_index_groups=groups)  152 us
    ppermute x9, waiting for transfers between devices, to_pools(): lax.ppermute(array, 'band', [(4 * a + k, 4 * b + k) for a, b in moves for...  35.8 us
    ppermute x9, starting transfers between devices, to_pools(): lax.ppermute(array, 'band', [(4 * a + k, 4 * b + k) for a, b in moves for...  25.9 us
    all_to_all x1, waiting for transfers between devices, swap(): return lax.all_to_all(array, axis, 0, 0, axis_index_groups=groups)  15 us
    all_to_all x1, starting transfers between devices, swap(): return lax.all_to_all(array, axis, 0, 0, axis_index_groups=groups)  5.82 us
  transfers between devices with their start and end apart: 14, of which 9 were waited for; matrix products, arithmetic and copies ran while one was open for 0% of the time, Pallas kernels for 0%

profile of v7, /device:TPU:2, one launch (start us, length us, event | category | flops | bytes accessed | tf_op | source)
XLA Modules:
  0.0 258.0 jit_solution(15758112474624698616)
XLA Ops:
  0.6 0.0 copy-start.1
  0.6 0.0 copy-start.2
  0.7 2.4 copy.10
  3.0 5.8 %all-to-all-start = ((f32[4,2,2,128,128]{4,3,2,1,0:T(8,128)}), f32[4,2,2,128,128]{4,3,2,1,0:T(8,128)S(1)}, u32[]{:S(2)}, u32[]{:S(2)}) async-start(f32[4,2,2,128,128]{4,3,2,1,0:T(8,128)} %copy.10), calls=%async_computation | async-start | bytes 2097152 | tf_op jit(solution)/shard_map/all_to_all | solution.py:211
  8.9 0.0 copy-done.1
  8.9 0.0 copy-done.2
  8.9 0.0 copy-start
  8.9 15.0 %all-to-all-done = f32[4,2,2,128,128]{4,3,2,1,0:T(8,128)S(1)} async-done(((f32[4,2,2,128,128]{4,3,2,1,0:T(8,128)}), f32[4,2,2,128,128]{4,3,2,1,0:T(8,128)S(1)}, u32[]{:S(2)}, u32[]{:S(2)}) %all-to-all-start) | async-done | bytes 1048608 | tf_op jit(solution)/shard_map/all_to_all | solution.py:211
  24.0 5.2 %collective-permute-start = (f32[2,2,128,128]{3,2,1,0:T(8,128)S(1)}, f32[2,2,128,128]{3,2,1,0:T(8,128)S(1)}, u32[]{:S(2)}, u32[]{:S(2)}) collective-permute-start(f32[2,2,128,128]{3,2,1,0:T(8,128)S(1)} %slice_bitcast_fusion.2), channel_id=1, source_target_pairs={{0,64},{16,80},{32,96},{48,112},{128,192},{144,208},{160,224},{176... | collective-permute-start | bytes 786440 | tf_op jit(solution)/shard_map/ppermute | solution.py:215
  29.2 6.4 %collective-permute-start.1 = (f32[2,2,128,128]{3,2,1,0:T(8,128)S(1)}, f32[2,2,128,128]{3,2,1,0:T(8,128)S(1)}, u32[]{:S(2)}, u32[]{:S(2)}) collective-permute-start(f32[2,2,128,128]{3,2,1,0:T(8,128)S(1)} %slice_bitcast_fusion.2), channel_id=1, source_target_pairs={{0,128},{16,144},{32,160},{48,176},{128,0},{144,16},{160,32},{176,... | collective-permute-start | bytes 786440 | tf_op jit(solution)/shard_map/ppermute | solution.py:215
  35.6 1.3 collective-permute-start.2
  36.9 0.1 select_bitcast_fusion.2
  37.0 0.1 collective-permute-start.4
  37.1 0.0 collective-permute-done
  37.1 7.5 %collective-permute-done.1 = f32[2,2,128,128]{3,2,1,0:T(8,128)S(1)} collective-permute-done((f32[2,2,128,128]{3,2,1,0:T(8,128)S(1)}, f32[2,2,128,128]{3,2,1,0:T(8,128)S(1)}, u32[]{:S(2)}, u32[]{:S(2)}) %collective-permute-start.1) | collective-permute-done | bytes 262176 | tf_op jit(solution)/shard_map/ppermute | solution.py:215
  44.6 8.0 %collective-permute-done.2 = f32[2,2,128,128]{3,2,1,0:T(8,128)S(1)} collective-permute-done((f32[2,2,128,128]{3,2,1,0:T(8,128)S(1)}, f32[2,2,128,128]{3,2,1,0:T(8,128)S(1)}, u32[]{:S(2)}, u32[]{:S(2)}) %collective-permute-start.2) | collective-permute-done | bytes 262176 | tf_op jit(solution)/shard_map/ppermute | solution.py:215
  52.6 0.1 select_select_fusion.1
  52.7 0.1 collective-permute-start.3
  52.8 0.1 broadcast_add_fusion
  52.9 0.2 fusion.green_ref
  53.1 0.0 collective-permute-done.4.orb_beside_ref.refs_3_
  53.1 1.6 collective-permute-done.3.phi_beside_ref.refs_1_
  54.7 0.0 copy-done
  54.7 3.9 %shard_map.59 = f32[32,4,4,2,8,128]{5,4,3,2,1,0:T(8,128)S(1)} custom-call(f32[4,2,128,128]{3,2,1,0:T(8,128)S(1)} %pad_maximum_fusion.1.phi_ref.refs_0_, f32[4,2,128,128]{3,2,1,0:T(8,128)S(1)} %collective-permute-done.3.phi_beside_ref.refs_1_, f32[4,2,128,128]{3,2,1,0:T(8,128)S(1)} %get-tuple-element.15.orb_ref.refs_2_, ...), custom_call_target="tpu_custom_call" | custom-call | flops 2147483648 | bytes 12582912 | tf_op jit(solution)/shard_map/pallas_call | solution.py:148
  58.6 55.7 %all_to_all.20.in_ref = f32[32,4,4,2,8,128]{5,4,3,2,1,0:T(8,128)S(1)} all-to-all(f32[32,4,4,2,8,128]{5,4,3,2,1,0:T(8,128)S(1)} %shard_map.59), channel_id=1, replica_groups={{0,32,2,34,4,36,6,38,8,40,10,42,12,44,14,46,16,48,18,50,20,52,22,54,24,..., dimensions={0} | all-to-all | bytes 8388608 | tf_op jit(solution)/shard_map/all_to_all | solution.py:211
  114.3 5.1 %shard_map.60 = f32[32,4,4,2,8,128]{5,4,3,2,1,0:T(8,128)S(1)} custom-call(f32[32,4,4,2,8,128]{5,4,3,2,1,0:T(8,128)S(1)} %all_to_all.20.in_ref, f32[4,128,128]{2,1,0:T(8,128)S(1)} %fusion.green_ref, bf16[2,256,256]{2,1,0:T(8,128)(2,1)S(1)} %get-tuple-element.18.to_z_ref, bf16[2,256,256]{2,1,0:T(8,128)(2,1)S(1)} %get-tuple-element.19.from_z_ref), custom_call_target="tpu_custom_call" | custom-call | flops 2147483648 | bytes 12582912 | tf_op jit(solution)/shard_map/pallas_call | solution.py:157
  119.5 54.0 %all_to_all.21.in_ref = f32[32,4,4,2,8,128]{5,4,3,2,1,0:T(8,128)S(1)} all-to-all(f32[32,4,4,2,8,128]{5,4,3,2,1,0:T(8,128)S(1)} %shard_map.60), channel_id=1, replica_groups={{0,32,2,34,4,36,6,38,8,40,10,42,12,44,14,46,16,48,18,50,20,52,22,54,24,..., dimensions={0} | all-to-all | bytes 8388608 | tf_op jit(solution)/shard_map/all_to_all | solution.py:211
  173.5 3.7 %shard_map.61 = (f32[4,2,128,128]{3,2,1,0:T(8,128)S(1)}, f32[4,2,128,128]{3,2,1,0:T(8,128)S(1)}, f32[4,2,128,128]{3,2,1,0:T(8,128)S(1)}, f32[4,2,128,128]{3,2,1,0:T(8,128)S(1)}) custom-call(f32[32,4,4,2,8,128]{5,4,3,2,1,0:T(8,128)S(1)} %all_to_all.21.in_ref, f32[4,2,128,128]{3,2,1,0:T(8,128)S(1)} %pad_maximum_fusion.1.phi_ref.refs_0_, ...), custom_call_target="tpu_custom_call" | custom-call | flops 2147483648 | bytes 12582912 | tf_op jit(solution)/shard_map/pallas_call | solution.py:166
  177.2 0.1 collective-permute-start.6
  177.3 0.5 collective-permute-start.5
  177.8 1.4 collective-permute-done.6
  179.2 0.1 add.127
  179.3 1.5 collective-permute-start.7
  180.8 5.5 %collective-permute-start.8 = (f32[2,128,128]{2,1,0:T(8,128)S(1)}, f32[2,128,128]{2,1,0:T(8,128)S(1)}, u32[]{:S(2)}, u32[]{:S(2)}) collective-permute-start(f32[2,128,128]{2,1,0:T(8,128)S(1)} %get-tuple-element.34), channel_id=1, source_target_pairs={{0,64},{16,80},{32,96},{48,112},{64,128},{80,144},{96,160},{112,17... | collective-permute-start | bytes 393224 | tf_op jit(solution)/shard_map/ppermute | solution.py:215
  186.3 0.0 collective-permute-start.9
  186.3 3.3 %collective-permute-done.7 = f32[2,128,128]{2,1,0:T(8,128)S(1)} collective-permute-done((f32[2,128,128]{2,1,0:T(8,128)S(1)}, f32[2,128,128]{2,1,0:T(8,128)S(1)}, u32[]{:S(2)}, u32[]{:S(2)}) %collective-permute-start.7) | collective-permute-done | bytes 131104 | tf_op jit(solution)/shard_map/ppermute | solution.py:215
  189.6 7.7 %collective-permute-done.8 = f32[2,128,128]{2,1,0:T(8,128)S(1)} collective-permute-done((f32[2,128,128]{2,1,0:T(8,128)S(1)}, f32[2,128,128]{2,1,0:T(8,128)S(1)}, u32[]{:S(2)}, u32[]{:S(2)}) %collective-permute-start.8) | collective-permute-done | bytes 131104 | tf_op jit(solution)/shard_map/ppermute | solution.py:215
  197.3 0.0 collective-permute-done.9
  197.3 1.0 collective-permute-start.10
  198.3 3.0 %collective-permute-start.11 = (f32[2,128,128]{2,1,0:T(8,128)S(1)}, f32[2,128,128]{2,1,0:T(8,128)S(1)}, u32[]{:S(2)}, u32[]{:S(2)}) collective-permute-start(f32[2,128,128]{2,1,0:T(8,128)S(1)} %bitcast_add_fusion), channel_id=1, source_target_pairs={{0,128},{16,144},{32,160},{48,176},{64,192},{80,208},{96,224},{112... | collective-permute-start | bytes 393224 | tf_op jit(solution)/shard_map/ppermute | solution.py:215
  201.2 2.0 collective-permute-start.12
  203.3 0.0 collective-permute-done.5
  203.3 0.1 select_bitcast_fusion.1
  203.4 2.6 %collective-permute-done.10 = f32[2,128,128]{2,1,0:T(8,128)S(1)} collective-permute-done((f32[2,128,128]{2,1,0:T(8,128)S(1)}, f32[2,128,128]{2,1,0:T(8,128)S(1)}, u32[]{:S(2)}, u32[]{:S(2)}) %collective-permute-start.10) | collective-permute-done | bytes 131104 | tf_op jit(solution)/shard_map/ppermute | solution.py:215
  205.9 6.8 %collective-permute-done.11 = f32[2,128,128]{2,1,0:T(8,128)S(1)} collective-permute-done((f32[2,128,128]{2,1,0:T(8,128)S(1)}, f32[2,128,128]{2,1,0:T(8,128)S(1)}, u32[]{:S(2)}, u32[]{:S(2)}) %collective-permute-start.11) | collective-permute-done | bytes 131104 | tf_op jit(solution)/shard_map/ppermute | solution.py:215
  212.7 0.0 collective-permute-done.12
  212.7 0.1 select_bitcast_fusion.7
  212.8 0.2 broadcast_in_dim.8
  213.1 0.3 pad_maximum_fusion
  213.4 42.7 %all_to_all.22.in_ref = f32[4,6,2,128,128]{4,3,2,1,0:T(8,128)S(1)} all-to-all(f32[4,6,2,128,128]{4,3,2,1,0:T(8,128)S(1)} %pad_maximum_fusion), channel_id=1, replica_groups={{0,16,32,48},{64,80,96,112},{128,144,160,176},{192,208,224,240},{1,17,3..., dimensions={0} | all-to-all | bytes 6291456 | tf_op jit(solution)/shard_map/all_to_all | solution.py:211
  256.1 1.8 shard_map.62
  (8 shorter events, 0.2 us)
Async XLA Ops:
  0.6 8.2 %copy-start.1 = (bf16[2,2,256,256]{3,2,1,0:T(8,128)(2,1)S(1)}, bf16[2,2,256,256]{3,2,1,0:T(8,128)(2,1)}, u32[]{:S(2)}) copy-start(bf16[2,2,256,256]{3,2,1,0:T(8,128)(2,1)} %constant.115.clone) | copy-start | bytes 1572868
  0.6 8.2 %copy-start.2 = (bf16[2,2,256,256]{3,2,1,0:T(8,128)(2,1)S(1)}, bf16[2,2,256,256]{3,2,1,0:T(8,128)(2,1)}, u32[]{:S(2)}) copy-start(bf16[2,2,256,256]{3,2,1,0:T(8,128)(2,1)} %constant.116.clone) | copy-start | bytes 1572868
  3.0 20.9 %all-to-all-start = ((f32[4,2,2,128,128]{4,3,2,1,0:T(8,128)}), f32[4,2,2,128,128]{4,3,2,1,0:T(8,128)S(1)}, u32[]{:S(2)}, u32[]{:S(2)}) async-start(f32[4,2,2,128,128]{4,3,2,1,0:T(8,128)} %copy.10), calls=%async_computation | async-start | bytes 2097152 | tf_op jit(solution)/shard_map/all_to_all | solution.py:211
  8.9 45.8 %copy-start = (bf16[256,256]{1,0:T(8,128)(2,1)S(1)}, bf16[256,256]{1,0:T(8,128)(2,1)}, u32[]{:S(2)}) copy-start(bf16[256,256]{1,0:T(8,128)(2,1)} %constant.114.clone.table_ref.refs_4_) | copy-start | bytes 393220
  24.0 13.1 %collective-permute-start = (f32[2,2,128,128]{3,2,1,0:T(8,128)S(1)}, f32[2,2,128,128]{3,2,1,0:T(8,128)S(1)}, u32[]{:S(2)}, u32[]{:S(2)}) collective-permute-start(f32[2,2,128,128]{3,2,1,0:T(8,128)S(1)} %slice_bitcast_fusion.2), channel_id=1, source_target_pairs={{0,64},{16,80},{32,96},{48,112},{128,192},{144,208},{160,224},{176... | collective-permute-start | bytes 786440 | tf_op jit(solution)/shard_map/ppermute | solution.py:215
  29.2 15.4 %collective-permute-start.1 = (f32[2,2,128,128]{3,2,1,0:T(8,128)S(1)}, f32[2,2,128,128]{3,2,1,0:T(8,128)S(1)}, u32[]{:S(2)}, u32[]{:S(2)}) collective-permute-start(f32[2,2,128,128]{3,2,1,0:T(8,128)S(1)} %slice_bitcast_fusion.2), channel_id=1, source_target_pairs={{0,128},{16,144},{32,160},{48,176},{128,0},{144,16},{160,32},{176,... | collective-permute-start | bytes 786440 | tf_op jit(solution)/shard_map/ppermute | solution.py:215
  35.6 17.0 %collective-permute-start.2 = (f32[2,2,128,128]{3,2,1,0:T(8,128)S(1)}, f32[2,2,128,128]{3,2,1,0:T(8,128)S(1)}, u32[]{:S(2)}, u32[]{:S(2)}) collective-permute-start(f32[2,2,128,128]{3,2,1,0:T(8,128)S(1)} %slice_bitcast_fusion.2), channel_id=1, source_target_pairs={{0,192},{16,208},{32,224},{48,240},{128,64},{144,80},{160,96},{176... | collective-permute-start | bytes 786440 | tf_op jit(solution)/shard_map/ppermute | solution.py:215
  37.0 16.2 %collective-permute-start.4 = (f32[4,2,128,128]{3,2,1,0:T(8,128)S(1)}, f32[4,2,128,128]{3,2,1,0:T(8,128)S(1)}, u32[]{:S(2)}, u32[]{:S(2)}) collective-permute-start(f32[4,2,128,128]{3,2,1,0:T(8,128)S(1)} %get-tuple-element.28), channel_id=1, source_target_pairs={{0,1},{1,0},{2,3},{3,2},{4,5},{5,4},{6,7},{7,6},{8,9},{9,8},{10,11... | collective-permute-start | bytes 1572872 | tf_op jit(solution)/shard_map/ppermute | solution.py:202
  52.7 2.0 collective-permute-start.3
  177.2 2.0 collective-permute-start.6
  177.3 26.0 %collective-permute-start.5 = (f32[4,2,128,128]{3,2,1,0:T(8,128)S(1)}, f32[4,2,128,128]{3,2,1,0:T(8,128)S(1)}, u32[]{:S(2)}, u32[]{:S(2)}) collective-permute-start(f32[4,2,128,128]{3,2,1,0:T(8,128)S(1)} %get-tuple-element.21), channel_id=1, source_target_pairs={{0,1},{1,0},{2,3},{3,2},{4,5},{5,4},{6,7},{7,6},{8,9},{9,8},{10,11... | collective-permute-start | bytes 1572872 | tf_op jit(solution)/shard_map/ppermute | solution.py:202
  179.3 10.3 %collective-permute-start.7 = (f32[2,128,128]{2,1,0:T(8,128)S(1)}, f32[2,128,128]{2,1,0:T(8,128)S(1)}, u32[]{:S(2)}, u32[]{:S(2)}) collective-permute-start(f32[2,128,128]{2,1,0:T(8,128)S(1)} %get-tuple-element.36), channel_id=1, source_target_pairs={{0,128},{16,144},{32,160},{48,176},{64,192},{80,208},{96,224},{112... | collective-permute-start | bytes 393224 | tf_op jit(solution)/shard_map/ppermute | solution.py:215
  180.8 16.5 %collective-permute-start.8 = (f32[2,128,128]{2,1,0:T(8,128)S(1)}, f32[2,128,128]{2,1,0:T(8,128)S(1)}, u32[]{:S(2)}, u32[]{:S(2)}) collective-permute-start(f32[2,128,128]{2,1,0:T(8,128)S(1)} %get-tuple-element.34), channel_id=1, source_target_pairs={{0,64},{16,80},{32,96},{48,112},{64,128},{80,144},{96,160},{112,17... | collective-permute-start | bytes 393224 | tf_op jit(solution)/shard_map/ppermute | solution.py:215
  186.3 11.0 %collective-permute-start.9 = (f32[2,128,128]{2,1,0:T(8,128)S(1)}, f32[2,128,128]{2,1,0:T(8,128)S(1)}, u32[]{:S(2)}, u32[]{:S(2)}) collective-permute-start(f32[2,128,128]{2,1,0:T(8,128)S(1)} %get-tuple-element.35), channel_id=1, source_target_pairs={{0,192},{16,208},{32,224},{48,240},{64,0},{80,16},{96,32},{112,48}... | collective-permute-start | bytes 393224 | tf_op jit(solution)/shard_map/ppermute | solution.py:215
  197.3 8.6 %collective-permute-start.10 = (f32[2,128,128]{2,1,0:T(8,128)S(1)}, f32[2,128,128]{2,1,0:T(8,128)S(1)}, u32[]{:S(2)}, u32[]{:S(2)}) collective-permute-start(f32[2,128,128]{2,1,0:T(8,128)S(1)} %bitcast_add_fusion), channel_id=1, source_target_pairs={{0,64},{16,80},{32,96},{48,112},{64,128},{80,144},{96,160},{112,17... | collective-permute-start | bytes 393224 | tf_op jit(solution)/shard_map/ppermute | solution.py:215
  198.3 14.4 %collective-permute-start.11 = (f32[2,128,128]{2,1,0:T(8,128)S(1)}, f32[2,128,128]{2,1,0:T(8,128)S(1)}, u32[]{:S(2)}, u32[]{:S(2)}) collective-permute-start(f32[2,128,128]{2,1,0:T(8,128)S(1)} %bitcast_add_fusion), channel_id=1, source_target_pairs={{0,128},{16,144},{32,160},{48,176},{64,192},{80,208},{96,224},{112... | collective-permute-start | bytes 393224 | tf_op jit(solution)/shard_map/ppermute | solution.py:215
  201.2 11.5 %collective-permute-start.12 = (f32[2,128,128]{2,1,0:T(8,128)S(1)}, f32[2,128,128]{2,1,0:T(8,128)S(1)}, u32[]{:S(2)}, u32[]{:S(2)}) collective-permute-start(f32[2,128,128]{2,1,0:T(8,128)S(1)} %bitcast_add_fusion), channel_id=1, source_target_pairs={{0,192},{16,208},{32,224},{48,240},{64,0},{80,16},{96,32},{112,48}... | collective-permute-start | bytes 393224 | tf_op jit(solution)/shard_map/ppermute | solution.py:215

commit v8 on v6

--- a/solution.py
+++ b/solution.py
@@ -100,26 +100,24 @@
                 out_ref[:, i, a, j] = field.reshape(GROUP, 2 * PLANES, N)
 
 
-def gather_kernel(in_ref, *refs):
-    phi_refs, orb_refs, table_ref, applied_refs, owner_refs = refs[:2], refs[2:4], refs[4], refs[5:7], refs[7:]
-    for ref in applied_refs:
-        ref[...] = jnp.zeros_like(ref)
+def gather_kernel(side, in_ref, phi_ref, orb_ref, table_ref, applied_ref, owner_ref):
+    applied_ref[...] = jnp.zeros_like(applied_ref)
 
     @pl.loop(0, SENT)
     def _(i):
-        owners = [None, None]
+        owner = None
         for pair in range(ORBS // 2):
             both = jnp.swapaxes(in_ref[:, i, :, pair].reshape(N, 2 * PLANES, N), 0, 1)
-            for j in (2 * pair, 2 * pair + 1):
-                field = both[(j % 2) * PLANES:(j % 2 + 1) * PLANES].reshape(PLANES * N, N)
-                field = turned(rows_by_table(field, table_ref[...]))
-                result = (rows_by_table(field, table_ref[...]) * MIX).reshape(2, 2, N, N)
-                for q in range(2):
-                    applied_refs[q][j] += result[q] * phi_refs[q][i]
-                    part = result[q] * orb_refs[q][j]
-                    owners[q] = part if j == 0 else owners[q] + part
-        for ref, owner in zip(owner_refs, owners):
-            ref[i] = owner
+            first = 2 * side
+            field = jnp.concatenate([both[first:first + 2], both[PLANES + first:PLANES + first + 2]], 0)
+            field = turned(rows_by_table(field.reshape(PLANES * N, N), table_ref[...]))
+            result = (rows_by_table(field, table_ref[...]) * MIX).reshape(2, 2, N, N)
+            for n in range(2):
+                j = 2 * pair + n
+                applied_ref[j] += result[n] * phi_ref[i]
+                part = result[n] * orb_ref[j]
+                owner = part if j == 0 else owner + part
+        owner_ref[i] = owner
 
 
 def join_kernel(in_ref, applied_ref, terms_ref, sems):
@@ -162,13 +160,13 @@
     )(field, green, to_z, from_z)
 
 
-def collect(field, phis, orbs, table):
-    return pl.pallas_call(
-        gather_kernel,
-        out_shape=(PLANE_SHAPE,) * 4,
-        compiler_params=params(),
-        cost_estimate=cost(SENT * ROWS),
-    )(field, *phis, *orbs, table)
+def collect(side, field, phis, orbs, table):
+    return pl.pallas_call(
+        functools.partial(gather_kernel, side),
+        out_shape=(PLANE_SHAPE,) * 2,
+        compiler_params=params(),
+        cost_estimate=cost(SENT * ROWS // 2),
+    )(field, phis[side], orbs[side], table)
 
 
 def join(both):
@@ -243,7 +241,8 @@
     phis, orbs, green, to_z, from_z = lax.optimization_barrier((phis, orbs, green, to_z, from_z))
     field = swap(spread(phis, orbs, table), EVERY, LINES)
     field = swap(lines(field, green, to_z, from_z), EVERY, LINES)
-    applied, applied_beside, owner, owner_beside = collect(field, phis, orbs, table)
+    applied_beside, owner_beside = collect(1, field, phis, orbs, table)
+    applied, owner = collect(0, field, phis, orbs, table)
 
     owner = owner + over_core(owner_beside)
 

time: 259 us -> 264 us (1.019)
  local copies, waits for them, and re-layouts: 2.73 us -> 6.86 us
    unnamed x6 -> x10, local copies, waits for them, and re-layouts: 0.02 us -> 4.15 us
  transfers between devices with their start and end apart: 14 -> 14, of which waited for: 11 -> 10; matrix products, arithmetic and copies ran while one was open for 0% -> 1% of each run, Pallas kernels for 0% -> 1%
where the time goes in v8:
time: 264 us; the launch traced here: 262 us
  blocking collectives  150 us (57%)
  waiting for transfers between devices  51.1 us (19%)
  starting transfers between devices  34.4 us (13%)
  Pallas kernels  15.9 us (6%)
  local copies, waits for them, and re-layouts  6.86 us (3%)
    all_to_all x3, blocking collectives, swap(): return lax.all_to_all(array, axis, 0, 0, axis_index_groups=groups)  150 us
    ppermute x9, waiting for transfers between devices, to_pools(): lax.ppermute(array, 'band', [(4 * a + k, 4 * b + k) for a, b in moves for...  34.6 us
    ppermute x9, starting transfers between devices, to_pools(): lax.ppermute(array, 'band', [(4 * a + k, 4 * b + k) for a, b in moves for...  27.9 us
    all_to_all x1, waiting for transfers between devices, swap(): return lax.all_to_all(array, axis, 0, 0, axis_index_groups=groups)  15 us
    all_to_all x1, starting transfers between devices, swap(): return lax.all_to_all(array, axis, 0, 0, axis_index_groups=groups)  5.82 us
  transfers between devices with their start and end apart: 14, of which 10 were waited for; matrix products, arithmetic and copies ran while one was open for 1% of the time, Pallas kernels for 1%

profile of v8, /device:TPU:2, one launch (start us, length us, event | category | flops | bytes accessed | tf_op | source)
XLA Modules:
  0.0 261.6 jit_solution(3949677708593433228)
XLA Ops:
  0.6 0.0 copy-start.3
  0.6 0.0 copy-start.4
  0.7 2.4 copy.10
  3.0 5.8 %all-to-all-start = ((f32[4,2,2,128,128]{4,3,2,1,0:T(8,128)}), f32[4,2,2,128,128]{4,3,2,1,0:T(8,128)S(1)}, u32[]{:S(2)}, u32[]{:S(2)}) async-start(f32[4,2,2,128,128]{4,3,2,1,0:T(8,128)} %copy.10), calls=%async_computation | async-start | bytes 2097152 | tf_op jit(solution)/shard_map/all_to_all | solution.py:209
  8.9 0.0 copy-done.3
  8.9 0.0 copy-done.4
  8.9 0.0 copy-start.2
  8.9 15.0 %all-to-all-done = f32[4,2,2,128,128]{4,3,2,1,0:T(8,128)S(1)} async-done(((f32[4,2,2,128,128]{4,3,2,1,0:T(8,128)}), f32[4,2,2,128,128]{4,3,2,1,0:T(8,128)S(1)}, u32[]{:S(2)}, u32[]{:S(2)}) %all-to-all-start) | async-done | bytes 1048608 | tf_op jit(solution)/shard_map/all_to_all | solution.py:209
  24.0 5.2 %collective-permute-start = (f32[2,2,128,128]{3,2,1,0:T(8,128)S(1)}, f32[2,2,128,128]{3,2,1,0:T(8,128)S(1)}, u32[]{:S(2)}, u32[]{:S(2)}) collective-permute-start(f32[2,2,128,128]{3,2,1,0:T(8,128)S(1)} %slice_bitcast_fusion.2), channel_id=1, source_target_pairs={{0,64},{16,80},{32,96},{48,112},{128,192},{144,208},{160,224},{176... | collective-permute-start | bytes 786440 | tf_op jit(solution)/shard_map/ppermute | solution.py:213
  29.2 6.4 %collective-permute-start.1 = (f32[2,2,128,128]{3,2,1,0:T(8,128)S(1)}, f32[2,2,128,128]{3,2,1,0:T(8,128)S(1)}, u32[]{:S(2)}, u32[]{:S(2)}) collective-permute-start(f32[2,2,128,128]{3,2,1,0:T(8,128)S(1)} %slice_bitcast_fusion.2), channel_id=1, source_target_pairs={{0,128},{16,144},{32,160},{48,176},{128,0},{144,16},{160,32},{176,... | collective-permute-start | bytes 786440 | tf_op jit(solution)/shard_map/ppermute | solution.py:213
  35.6 1.3 collective-permute-start.2
  36.9 0.1 select_bitcast_fusion.2
  37.0 0.1 collective-permute-start.4
  37.1 0.0 collective-permute-done
  37.1 7.5 %collective-permute-done.1 = f32[2,2,128,128]{3,2,1,0:T(8,128)S(1)} collective-permute-done((f32[2,2,128,128]{3,2,1,0:T(8,128)S(1)}, f32[2,2,128,128]{3,2,1,0:T(8,128)S(1)}, u32[]{:S(2)}, u32[]{:S(2)}) %collective-permute-start.1) | collective-permute-done | bytes 262176 | tf_op jit(solution)/shard_map/ppermute | solution.py:213
  44.6 8.0 %collective-permute-done.2 = f32[2,2,128,128]{3,2,1,0:T(8,128)S(1)} collective-permute-done((f32[2,2,128,128]{3,2,1,0:T(8,128)S(1)}, f32[2,2,128,128]{3,2,1,0:T(8,128)S(1)}, u32[]{:S(2)}, u32[]{:S(2)}) %collective-permute-start.2) | collective-permute-done | bytes 262176 | tf_op jit(solution)/shard_map/ppermute | solution.py:213
  52.6 0.1 select_select_fusion.1
  52.7 0.1 collective-permute-start.3
  52.8 0.1 broadcast_add_fusion
  52.9 0.2 fusion.green_ref
  53.1 0.0 collective-permute-done.4.orb_beside_ref.orb_ref
  53.1 1.6 collective-permute-done.3.phi_beside_ref.phi_ref
  54.7 0.0 copy-done.2
  54.7 3.9 %shard_map.59 = f32[32,4,4,2,8,128]{5,4,3,2,1,0:T(8,128)S(1)} custom-call(f32[4,2,128,128]{3,2,1,0:T(8,128)S(1)} %pad_maximum_fusion.1.phi_ref, f32[4,2,128,128]{3,2,1,0:T(8,128)S(1)} %collective-permute-done.3.phi_beside_ref.phi_ref, f32[4,2,128,128]{3,2,1,0:T(8,128)S(1)} %get-tuple-element.15.orb_ref, ...), custom_call_target="tpu_custom_call" | custom-call | flops 2147483648 | bytes 12582912 | tf_op jit(solution)/shard_map/pallas_call | solution.py:146
  58.6 55.7 %all_to_all.20.in_ref = f32[32,4,4,2,8,128]{5,4,3,2,1,0:T(8,128)S(1)} all-to-all(f32[32,4,4,2,8,128]{5,4,3,2,1,0:T(8,128)S(1)} %shard_map.59), channel_id=1, replica_groups={{0,32,2,34,4,36,6,38,8,40,10,42,12,44,14,46,16,48,18,50,20,52,22,54,24,..., dimensions={0} | all-to-all | bytes 8388608 | tf_op jit(solution)/shard_map/all_to_all | solution.py:209
  114.3 5.1 %shard_map.60 = f32[32,4,4,2,8,128]{5,4,3,2,1,0:T(8,128)S(1)} custom-call(f32[32,4,4,2,8,128]{5,4,3,2,1,0:T(8,128)S(1)} %all_to_all.20.in_ref, f32[4,128,128]{2,1,0:T(8,128)S(1)} %fusion.green_ref, bf16[2,256,256]{2,1,0:T(8,128)(2,1)S(1)} %get-tuple-element.18.to_z_ref, bf16[2,256,256]{2,1,0:T(8,128)(2,1)S(1)} %get-tuple-element.19.from_z_ref), custom_call_target="tpu_custom_call" | custom-call | flops 2147483648 | bytes 12582912 | tf_op jit(solution)/shard_map/pallas_call | solution.py:155
  119.5 54.0 %all_to_all.21.in_ref = f32[32,4,4,2,8,128]{5,4,3,2,1,0:T(8,128)S(1)} all-to-all(f32[32,4,4,2,8,128]{5,4,3,2,1,0:T(8,128)S(1)} %shard_map.60), channel_id=1, replica_groups={{0,32,2,34,4,36,6,38,8,40,10,42,12,44,14,46,16,48,18,50,20,52,22,54,24,..., dimensions={0} | all-to-all | bytes 8388608 | tf_op jit(solution)/shard_map/all_to_all | solution.py:209
  173.5 2.5 shard_map.62
  176.0 0.0 copy-start
  176.0 1.9 copy-done
  177.9 0.0 collective-permute-start.6
  177.9 0.5 collective-permute-start.5
  178.4 0.0 copy-start.1
  178.4 2.2 copy-done.1
  180.6 2.5 shard_map.61
  183.1 0.0 collective-permute-done.6
  183.2 1.1 add.127
  184.3 2.5 collective-permute-start.7
  186.8 2.2 collective-permute-start.8
  189.1 2.3 collective-permute-start.9
  191.3 4.4 %collective-permute-done.7 = f32[2,128,128]{2,1,0:T(8,128)S(1)} collective-permute-done((f32[2,128,128]{2,1,0:T(8,128)S(1)}, f32[2,128,128]{2,1,0:T(8,128)S(1)}, u32[]{:S(2)}, u32[]{:S(2)}) %collective-permute-start.7) | collective-permute-done | bytes 131104 | tf_op jit(solution)/shard_map/ppermute | solution.py:213
  195.7 2.8 %collective-permute-done.8 = f32[2,128,128]{2,1,0:T(8,128)S(1)} collective-permute-done((f32[2,128,128]{2,1,0:T(8,128)S(1)}, f32[2,128,128]{2,1,0:T(8,128)S(1)}, u32[]{:S(2)}, u32[]{:S(2)}) %collective-permute-start.8) | collective-permute-done | bytes 131104 | tf_op jit(solution)/shard_map/ppermute | solution.py:213
  198.5 1.7 collective-permute-done.9
  200.2 3.4 %collective-permute-start.10 = (f32[2,128,128]{2,1,0:T(8,128)S(1)}, f32[2,128,128]{2,1,0:T(8,128)S(1)}, u32[]{:S(2)}, u32[]{:S(2)}) collective-permute-start(f32[2,128,128]{2,1,0:T(8,128)S(1)} %bitcast_add_fusion), channel_id=1, source_target_pairs={{0,64},{16,80},{32,96},{48,112},{64,128},{80,144},{96,160},{112,17... | collective-permute-start | bytes 393224 | tf_op jit(solution)/shard_map/ppermute | solution.py:213
  203.5 2.5 collective-permute-start.11
  206.0 2.1 collective-permute-start.12
  208.1 0.0 collective-permute-done.5
  208.1 0.1 select_bitcast_fusion.1
  208.2 2.6 %collective-permute-done.10 = f32[2,128,128]{2,1,0:T(8,128)S(1)} collective-permute-done((f32[2,128,128]{2,1,0:T(8,128)S(1)}, f32[2,128,128]{2,1,0:T(8,128)S(1)}, u32[]{:S(2)}, u32[]{:S(2)}) %collective-permute-start.10) | collective-permute-done | bytes 131104 | tf_op jit(solution)/shard_map/ppermute | solution.py:213
  210.9 6.5 %collective-permute-done.11 = f32[2,128,128]{2,1,0:T(8,128)S(1)} collective-permute-done((f32[2,128,128]{2,1,0:T(8,128)S(1)}, f32[2,128,128]{2,1,0:T(8,128)S(1)}, u32[]{:S(2)}, u32[]{:S(2)}) %collective-permute-start.11) | collective-permute-done | bytes 131104 | tf_op jit(solution)/shard_map/ppermute | solution.py:213
  217.4 1.1 collective-permute-done.12
  218.5 0.1 select_bitcast_fusion.7
  218.6 0.2 broadcast_in_dim.8
  218.8 0.3 pad_maximum_fusion
  219.2 40.6 %all_to_all.22.in_ref = f32[4,6,2,128,128]{4,3,2,1,0:T(8,128)S(1)} all-to-all(f32[4,6,2,128,128]{4,3,2,1,0:T(8,128)S(1)} %pad_maximum_fusion), channel_id=1, replica_groups={{0,16,32,48},{64,80,96,112},{128,144,160,176},{192,208,224,240},{1,17,3..., dimensions={0} | all-to-all | bytes 6291456 | tf_op jit(solution)/shard_map/all_to_all | solution.py:209
  259.7 1.8 shard_map.63
  (8 shorter events, 0.2 us)
Async XLA Ops:
  0.6 8.2 %copy-start.3 = (bf16[2,2,256,256]{3,2,1,0:T(8,128)(2,1)S(1)}, bf16[2,2,256,256]{3,2,1,0:T(8,128)(2,1)}, u32[]{:S(2)}) copy-start(bf16[2,2,256,256]{3,2,1,0:T(8,128)(2,1)} %constant.115.clone) | copy-start | bytes 1572868
  0.6 8.2 %copy-start.4 = (bf16[2,2,256,256]{3,2,1,0:T(8,128)(2,1)S(1)}, bf16[2,2,256,256]{3,2,1,0:T(8,128)(2,1)}, u32[]{:S(2)}) copy-start(bf16[2,2,256,256]{3,2,1,0:T(8,128)(2,1)} %constant.116.clone) | copy-start | bytes 1572868
  3.0 20.9 %all-to-all-start = ((f32[4,2,2,128,128]{4,3,2,1,0:T(8,128)}), f32[4,2,2,128,128]{4,3,2,1,0:T(8,128)S(1)}, u32[]{:S(2)}, u32[]{:S(2)}) async-start(f32[4,2,2,128,128]{4,3,2,1,0:T(8,128)} %copy.10), calls=%async_computation | async-start | bytes 2097152 | tf_op jit(solution)/shard_map/all_to_all | solution.py:209
  8.9 45.8 %copy-start.2 = (bf16[256,256]{1,0:T(8,128)(2,1)S(1)}, bf16[256,256]{1,0:T(8,128)(2,1)}, u32[]{:S(2)}) copy-start(bf16[256,256]{1,0:T(8,128)(2,1)} %constant.114.clone.table_ref) | copy-start | bytes 393220
  24.0 13.1 %collective-permute-start = (f32[2,2,128,128]{3,2,1,0:T(8,128)S(1)}, f32[2,2,128,128]{3,2,1,0:T(8,128)S(1)}, u32[]{:S(2)}, u32[]{:S(2)}) collective-permute-start(f32[2,2,128,128]{3,2,1,0:T(8,128)S(1)} %slice_bitcast_fusion.2), channel_id=1, source_target_pairs={{0,64},{16,80},{32,96},{48,112},{128,192},{144,208},{160,224},{176... | collective-permute-start | bytes 786440 | tf_op jit(solution)/shard_map/ppermute | solution.py:213
  29.2 15.4 %collective-permute-start.1 = (f32[2,2,128,128]{3,2,1,0:T(8,128)S(1)}, f32[2,2,128,128]{3,2,1,0:T(8,128)S(1)}, u32[]{:S(2)}, u32[]{:S(2)}) collective-permute-start(f32[2,2,128,128]{3,2,1,0:T(8,128)S(1)} %slice_bitcast_fusion.2), channel_id=1, source_target_pairs={{0,128},{16,144},{32,160},{48,176},{128,0},{144,16},{160,32},{176,... | collective-permute-start | bytes 786440 | tf_op jit(solution)/shard_map/ppermute | solution.py:213
  35.6 17.0 %collective-permute-start.2 = (f32[2,2,128,128]{3,2,1,0:T(8,128)S(1)}, f32[2,2,128,128]{3,2,1,0:T(8,128)S(1)}, u32[]{:S(2)}, u32[]{:S(2)}) collective-permute-start(f32[2,2,128,128]{3,2,1,0:T(8,128)S(1)} %slice_bitcast_fusion.2), channel_id=1, source_target_pairs={{0,192},{16,208},{32,224},{48,240},{128,64},{144,80},{160,96},{176... | collective-permute-start | bytes 786440 | tf_op jit(solution)/shard_map/ppermute | solution.py:213
  37.0 16.1 %collective-permute-start.4 = (f32[4,2,128,128]{3,2,1,0:T(8,128)S(1)}, f32[4,2,128,128]{3,2,1,0:T(8,128)S(1)}, u32[]{:S(2)}, u32[]{:S(2)}) collective-permute-start(f32[4,2,128,128]{3,2,1,0:T(8,128)S(1)} %get-tuple-element.28), channel_id=1, source_target_pairs={{0,1},{1,0},{2,3},{3,2},{4,5},{5,4},{6,7},{7,6},{8,9},{9,8},{10,11... | collective-permute-start | bytes 1572872 | tf_op jit(solution)/shard_map/ppermute | solution.py:200
  52.7 2.0 collective-permute-start.3
  176.0 2.0 copy-start
  177.9 5.2 %collective-permute-start.6 = (f32[4,2,128,128]{3,2,1,0:T(8,128)S(1)}, f32[4,2,128,128]{3,2,1,0:T(8,128)}, u32[]{:S(2)}, u32[]{:S(2)}) collective-permute-start(f32[4,2,128,128]{3,2,1,0:T(8,128)S(1)} %get-tuple-element.23), channel_id=1, source_target_pairs={{0,1},{1,0},{2,3},{3,2},{4,5},{5,4},{6,7},{7,6},{8,9},{9,8},{10,11... | collective-permute-start | bytes 1572872 | tf_op jit(solution)/shard_map/ppermute | solution.py:200
  177.9 30.2 %collective-permute-start.5 = (f32[4,2,128,128]{3,2,1,0:T(8,128)S(1)}, f32[4,2,128,128]{3,2,1,0:T(8,128)S(1)}, u32[]{:S(2)}, u32[]{:S(2)}) collective-permute-start(f32[4,2,128,128]{3,2,1,0:T(8,128)S(1)} %get-tuple-element.21), channel_id=1, source_target_pairs={{0,1},{1,0},{2,3},{3,2},{4,5},{5,4},{6,7},{7,6},{8,9},{9,8},{10,11... | collective-permute-start | bytes 1572872 | tf_op jit(solution)/shard_map/ppermute | solution.py:200
  178.4 2.2 copy-start.1
  184.3 11.4 %collective-permute-start.7 = (f32[2,128,128]{2,1,0:T(8,128)S(1)}, f32[2,128,128]{2,1,0:T(8,128)S(1)}, u32[]{:S(2)}, u32[]{:S(2)}) collective-permute-start(f32[2,128,128]{2,1,0:T(8,128)S(1)} %get-tuple-element.36), channel_id=1, source_target_pairs={{0,64},{16,80},{32,96},{48,112},{64,128},{80,144},{96,160},{112,17... | collective-permute-start | bytes 393224 | tf_op jit(solution)/shard_map/ppermute | solution.py:213
  186.8 11.6 %collective-permute-start.8 = (f32[2,128,128]{2,1,0:T(8,128)S(1)}, f32[2,128,128]{2,1,0:T(8,128)S(1)}, u32[]{:S(2)}, u32[]{:S(2)}) collective-permute-start(f32[2,128,128]{2,1,0:T(8,128)S(1)} %get-tuple-element.34), channel_id=1, source_target_pairs={{0,192},{16,208},{32,224},{48,240},{64,0},{80,16},{96,32},{112,48}... | collective-permute-start | bytes 393224 | tf_op jit(solution)/shard_map/ppermute | solution.py:213
  189.1 11.1 %collective-permute-start.9 = (f32[2,128,128]{2,1,0:T(8,128)S(1)}, f32[2,128,128]{2,1,0:T(8,128)S(1)}, u32[]{:S(2)}, u32[]{:S(2)}) collective-permute-start(f32[2,128,128]{2,1,0:T(8,128)S(1)} %get-tuple-element.35), channel_id=1, source_target_pairs={{0,128},{16,144},{32,160},{48,176},{64,192},{80,208},{96,224},{112... | collective-permute-start | bytes 393224 | tf_op jit(solution)/shard_map/ppermute | solution.py:213
  200.2 10.7 %collective-permute-start.10 = (f32[2,128,128]{2,1,0:T(8,128)S(1)}, f32[2,128,128]{2,1,0:T(8,128)S(1)}, u32[]{:S(2)}, u32[]{:S(2)}) collective-permute-start(f32[2,128,128]{2,1,0:T(8,128)S(1)} %bitcast_add_fusion), channel_id=1, source_target_pairs={{0,64},{16,80},{32,96},{48,112},{64,128},{80,144},{96,160},{112,17... | collective-permute-start | bytes 393224 | tf_op jit(solution)/shard_map/ppermute | solution.py:213
  203.5 13.8 %collective-permute-start.11 = (f32[2,128,128]{2,1,0:T(8,128)S(1)}, f32[2,128,128]{2,1,0:T(8,128)S(1)}, u32[]{:S(2)}, u32[]{:S(2)}) collective-permute-start(f32[2,128,128]{2,1,0:T(8,128)S(1)} %bitcast_add_fusion), channel_id=1, source_target_pairs={{0,128},{16,144},{32,160},{48,176},{64,192},{80,208},{96,224},{112... | collective-permute-start | bytes 393224 | tf_op jit(solution)/shard_map/ppermute | solution.py:213
  206.0 12.4 %collective-permute-start.12 = (f32[2,128,128]{2,1,0:T(8,128)S(1)}, f32[2,128,128]{2,1,0:T(8,128)S(1)}, u32[]{:S(2)}, u32[]{:S(2)}) collective-permute-start(f32[2,128,128]{2,1,0:T(8,128)S(1)} %bitcast_add_fusion), channel_id=1, source_target_pairs={{0,192},{16,208},{32,224},{48,240},{64,0},{80,16},{96,32},{112,48}... | collective-permute-start | bytes 393224 | tf_op jit(solution)/shard_map/ppermute | solution.py:213

commit v9 on v6

--- a/solution.py
+++ b/solution.py
@@ -113,7 +113,7 @@
             for j in (2 * pair, 2 * pair + 1):
                 field = both[(j % 2) * PLANES:(j % 2 + 1) * PLANES].reshape(PLANES * N, N)
                 field = turned(rows_by_table(field, table_ref[...]))
-                result = (rows_by_table(field, table_ref[...]) * MIX).reshape(2, 2, N, N)
+                result = rows_by_table(field, table_ref[...]).reshape(2, 2, N, N)
                 for q in range(2):
                     applied_refs[q][j] += result[q] * phi_refs[q][i]
                     part = result[q] * orb_refs[q][j]
@@ -195,7 +195,7 @@
     ratio = (g_z * g_z + g_y * g_y + g_x * g_x) / (4.0 * OMEGA * OMEGA)
     safe = jnp.where(ratio > 0, ratio, 1.0)
     kernel = math.pi / (OMEGA * OMEGA) * jnp.where(ratio > 0, -jnp.expm1(-safe) / safe, 1.0)
-    return kernel * (1.0 / N**3)
+    return kernel * (MIX / N**3)
 
 
 def over_core(array):

time: 259 us -> 259 us (level)
  no operation moved by 1% of the time
where the time goes in v9:
time: 259 us; the launch traced here: 257 us
  blocking collectives  150 us (58%)
  waiting for transfers between devices  52.5 us (20%)
  starting transfers between devices  34.6 us (13%)
  Pallas kernels  14.6 us (6%)
  local copies, waits for them, and re-layouts  2.73 us (1%)
    all_to_all x3, blocking collectives, swap(): return lax.all_to_all(array, axis, 0, 0, axis_index_groups=groups)  150 us
    ppermute x9, waiting for transfers between devices, to_pools(): lax.ppermute(array, 'band', [(4 * a + k, 4 * b + k) for a, b in moves for...  34.5 us
    ppermute x9, starting transfers between devices, to_pools(): lax.ppermute(array, 'band', [(4 * a + k, 4 * b + k) for a, b in moves for...  28 us
    all_to_all x1, waiting for transfers between devices, swap(): return lax.all_to_all(array, axis, 0, 0, axis_index_groups=groups)  15 us
    all_to_all x1, starting transfers between devices, swap(): return lax.all_to_all(array, axis, 0, 0, axis_index_groups=groups)  5.82 us
  transfers between devices with their start and end apart: 14, of which 11 were waited for; matrix products, arithmetic and copies ran while one was open for 0% of the time, Pallas kernels for 0%

profile of v9, /device:TPU:2, one launch (start us, length us, event | category | flops | bytes accessed | tf_op | source)
XLA Modules:
  0.0 256.6 jit_solution(15445424435163890456)
XLA Ops:
  0.6 0.0 copy-start.1
  0.6 0.0 copy-start.2
  0.7 2.4 copy.10
  3.0 5.8 %all-to-all-start = ((f32[4,2,2,128,128]{4,3,2,1,0:T(8,128)}), f32[4,2,2,128,128]{4,3,2,1,0:T(8,128)S(1)}, u32[]{:S(2)}, u32[]{:S(2)}) async-start(f32[4,2,2,128,128]{4,3,2,1,0:T(8,128)} %copy.10), calls=%async_computation | async-start | bytes 2097152 | tf_op jit(solution)/shard_map/all_to_all | solution.py:211
  8.9 0.0 copy-done.1
  8.9 0.0 copy-done.2
  8.9 0.0 copy-start
  8.9 15.0 %all-to-all-done = f32[4,2,2,128,128]{4,3,2,1,0:T(8,128)S(1)} async-done(((f32[4,2,2,128,128]{4,3,2,1,0:T(8,128)}), f32[4,2,2,128,128]{4,3,2,1,0:T(8,128)S(1)}, u32[]{:S(2)}, u32[]{:S(2)}) %all-to-all-start) | async-done | bytes 1048608 | tf_op jit(solution)/shard_map/all_to_all | solution.py:211
  24.0 5.2 %collective-permute-start = (f32[2,2,128,128]{3,2,1,0:T(8,128)S(1)}, f32[2,2,128,128]{3,2,1,0:T(8,128)S(1)}, u32[]{:S(2)}, u32[]{:S(2)}) collective-permute-start(f32[2,2,128,128]{3,2,1,0:T(8,128)S(1)} %slice_bitcast_fusion.2), channel_id=1, source_target_pairs={{0,64},{16,80},{32,96},{48,112},{128,192},{144,208},{160,224},{176... | collective-permute-start | bytes 786440 | tf_op jit(solution)/shard_map/ppermute | solution.py:215
  29.2 6.4 %collective-permute-start.1 = (f32[2,2,128,128]{3,2,1,0:T(8,128)S(1)}, f32[2,2,128,128]{3,2,1,0:T(8,128)S(1)}, u32[]{:S(2)}, u32[]{:S(2)}) collective-permute-start(f32[2,2,128,128]{3,2,1,0:T(8,128)S(1)} %slice_bitcast_fusion.2), channel_id=1, source_target_pairs={{0,128},{16,144},{32,160},{48,176},{128,0},{144,16},{160,32},{176,... | collective-permute-start | bytes 786440 | tf_op jit(solution)/shard_map/ppermute | solution.py:215
  35.6 1.3 collective-permute-start.2
  36.9 0.1 select_bitcast_fusion.2
  37.0 0.1 collective-permute-start.4
  37.1 0.0 collective-permute-done
  37.1 7.5 %collective-permute-done.1 = f32[2,2,128,128]{3,2,1,0:T(8,128)S(1)} collective-permute-done((f32[2,2,128,128]{3,2,1,0:T(8,128)S(1)}, f32[2,2,128,128]{3,2,1,0:T(8,128)S(1)}, u32[]{:S(2)}, u32[]{:S(2)}) %collective-permute-start.1) | collective-permute-done | bytes 262176 | tf_op jit(solution)/shard_map/ppermute | solution.py:215
  44.6 8.0 %collective-permute-done.2 = f32[2,2,128,128]{3,2,1,0:T(8,128)S(1)} collective-permute-done((f32[2,2,128,128]{3,2,1,0:T(8,128)S(1)}, f32[2,2,128,128]{3,2,1,0:T(8,128)S(1)}, u32[]{:S(2)}, u32[]{:S(2)}) %collective-permute-start.2) | collective-permute-done | bytes 262176 | tf_op jit(solution)/shard_map/ppermute | solution.py:215
  52.6 0.1 select_select_fusion.1
  52.7 0.1 collective-permute-start.3
  52.8 0.1 broadcast_add_fusion
  52.9 0.2 fusion.green_ref
  53.1 0.0 collective-permute-done.4.orb_beside_ref.refs_3_
  53.1 1.6 collective-permute-done.3.phi_beside_ref.refs_1_
  54.7 0.0 copy-done
  54.7 3.9 %shard_map.59 = f32[32,4,4,2,8,128]{5,4,3,2,1,0:T(8,128)S(1)} custom-call(f32[4,2,128,128]{3,2,1,0:T(8,128)S(1)} %pad_maximum_fusion.1.phi_ref.refs_0_, f32[4,2,128,128]{3,2,1,0:T(8,128)S(1)} %collective-permute-done.3.phi_beside_ref.refs_1_, f32[4,2,128,128]{3,2,1,0:T(8,128)S(1)} %get-tuple-element.15.orb_ref.refs_2_, ...), custom_call_target="tpu_custom_call" | custom-call | flops 2147483648 | bytes 12582912 | tf_op jit(solution)/shard_map/pallas_call | solution.py:148
  58.6 55.7 %all_to_all.20.in_ref = f32[32,4,4,2,8,128]{5,4,3,2,1,0:T(8,128)S(1)} all-to-all(f32[32,4,4,2,8,128]{5,4,3,2,1,0:T(8,128)S(1)} %shard_map.59), channel_id=1, replica_groups={{0,32,2,34,4,36,6,38,8,40,10,42,12,44,14,46,16,48,18,50,20,52,22,54,24,..., dimensions={0} | all-to-all | bytes 8388608 | tf_op jit(solution)/shard_map/all_to_all | solution.py:211
  114.3 5.1 %shard_map.60 = f32[32,4,4,2,8,128]{5,4,3,2,1,0:T(8,128)S(1)} custom-call(f32[32,4,4,2,8,128]{5,4,3,2,1,0:T(8,128)S(1)} %all_to_all.20.in_ref, f32[4,128,128]{2,1,0:T(8,128)S(1)} %fusion.green_ref, bf16[2,256,256]{2,1,0:T(8,128)(2,1)S(1)} %get-tuple-element.18.to_z_ref, bf16[2,256,256]{2,1,0:T(8,128)(2,1)S(1)} %get-tuple-element.19.from_z_ref), custom_call_target="tpu_custom_call" | custom-call | flops 2147483648 | bytes 12582912 | tf_op jit(solution)/shard_map/pallas_call | solution.py:157
  119.5 54.0 %all_to_all.21.in_ref = f32[32,4,4,2,8,128]{5,4,3,2,1,0:T(8,128)S(1)} all-to-all(f32[32,4,4,2,8,128]{5,4,3,2,1,0:T(8,128)S(1)} %shard_map.60), channel_id=1, replica_groups={{0,32,2,34,4,36,6,38,8,40,10,42,12,44,14,46,16,48,18,50,20,52,22,54,24,..., dimensions={0} | all-to-all | bytes 8388608 | tf_op jit(solution)/shard_map/all_to_all | solution.py:211
  173.5 3.7 %shard_map.61 = (f32[4,2,128,128]{3,2,1,0:T(8,128)S(1)}, f32[4,2,128,128]{3,2,1,0:T(8,128)S(1)}, f32[4,2,128,128]{3,2,1,0:T(8,128)S(1)}, f32[4,2,128,128]{3,2,1,0:T(8,128)S(1)}) custom-call(f32[32,4,4,2,8,128]{5,4,3,2,1,0:T(8,128)S(1)} %all_to_all.21.in_ref, f32[4,2,128,128]{3,2,1,0:T(8,128)S(1)} %pad_maximum_fusion.1.phi_ref.refs_0_, ...), custom_call_target="tpu_custom_call" | custom-call | flops 2147483648 | bytes 12582912 | tf_op jit(solution)/shard_map/pallas_call | solution.py:166
  177.2 0.1 collective-permute-start.6
  177.3 0.5 collective-permute-start.5
  177.8 1.4 collective-permute-done.6
  179.2 0.1 add.127
  179.3 2.5 collective-permute-start.7
  181.8 2.2 collective-permute-start.8
  184.0 2.3 collective-permute-start.9
  186.3 4.3 %collective-permute-done.7 = f32[2,128,128]{2,1,0:T(8,128)S(1)} collective-permute-done((f32[2,128,128]{2,1,0:T(8,128)S(1)}, f32[2,128,128]{2,1,0:T(8,128)S(1)}, u32[]{:S(2)}, u32[]{:S(2)}) %collective-permute-start.7) | collective-permute-done | bytes 131104 | tf_op jit(solution)/shard_map/ppermute | solution.py:215
  190.6 2.9 %collective-permute-done.8 = f32[2,128,128]{2,1,0:T(8,128)S(1)} collective-permute-done((f32[2,128,128]{2,1,0:T(8,128)S(1)}, f32[2,128,128]{2,1,0:T(8,128)S(1)}, u32[]{:S(2)}, u32[]{:S(2)}) %collective-permute-start.8) | collective-permute-done | bytes 131104 | tf_op jit(solution)/shard_map/ppermute | solution.py:215
  193.6 1.5 collective-permute-done.9
  195.1 3.5 %collective-permute-start.10 = (f32[2,128,128]{2,1,0:T(8,128)S(1)}, f32[2,128,128]{2,1,0:T(8,128)S(1)}, u32[]{:S(2)}, u32[]{:S(2)}) collective-permute-start(f32[2,128,128]{2,1,0:T(8,128)S(1)} %bitcast_add_fusion), channel_id=1, source_target_pairs={{0,64},{16,80},{32,96},{48,112},{64,128},{80,144},{96,160},{112,17... | collective-permute-start | bytes 393224 | tf_op jit(solution)/shard_map/ppermute | solution.py:215
  198.6 2.6 %collective-permute-start.11 = (f32[2,128,128]{2,1,0:T(8,128)S(1)}, f32[2,128,128]{2,1,0:T(8,128)S(1)}, u32[]{:S(2)}, u32[]{:S(2)}) collective-permute-start(f32[2,128,128]{2,1,0:T(8,128)S(1)} %bitcast_add_fusion), channel_id=1, source_target_pairs={{0,128},{16,144},{32,160},{48,176},{64,192},{80,208},{96,224},{112... | collective-permute-start | bytes 393224 | tf_op jit(solution)/shard_map/ppermute | solution.py:215
  201.2 2.0 collective-permute-start.12
  203.2 0.0 collective-permute-done.5
  203.2 0.1 select_bitcast_fusion.1
  203.3 2.6 %collective-permute-done.10 = f32[2,128,128]{2,1,0:T(8,128)S(1)} collective-permute-done((f32[2,128,128]{2,1,0:T(8,128)S(1)}, f32[2,128,128]{2,1,0:T(8,128)S(1)}, u32[]{:S(2)}, u32[]{:S(2)}) %collective-permute-start.10) | collective-permute-done | bytes 131104 | tf_op jit(solution)/shard_map/ppermute | solution.py:215
  205.9 6.7 %collective-permute-done.11 = f32[2,128,128]{2,1,0:T(8,128)S(1)} collective-permute-done((f32[2,128,128]{2,1,0:T(8,128)S(1)}, f32[2,128,128]{2,1,0:T(8,128)S(1)}, u32[]{:S(2)}, u32[]{:S(2)}) %collective-permute-start.11) | collective-permute-done | bytes 131104 | tf_op jit(solution)/shard_map/ppermute | solution.py:215
  212.6 0.9 collective-permute-done.12
  213.5 0.1 select_bitcast_fusion.7
  213.6 0.2 broadcast_in_dim.8
  213.9 0.3 pad_maximum_fusion
  214.2 40.5 %all_to_all.22.in_ref = f32[4,6,2,128,128]{4,3,2,1,0:T(8,128)S(1)} all-to-all(f32[4,6,2,128,128]{4,3,2,1,0:T(8,128)S(1)} %pad_maximum_fusion), channel_id=1, replica_groups={{0,16,32,48},{64,80,96,112},{128,144,160,176},{192,208,224,240},{1,17,3..., dimensions={0} | all-to-all | bytes 6291456 | tf_op jit(solution)/shard_map/all_to_all | solution.py:211
  254.7 1.8 shard_map.62
  (8 shorter events, 0.2 us)
Async XLA Ops:
  0.6 8.2 %copy-start.1 = (bf16[2,2,256,256]{3,2,1,0:T(8,128)(2,1)S(1)}, bf16[2,2,256,256]{3,2,1,0:T(8,128)(2,1)}, u32[]{:S(2)}) copy-start(bf16[2,2,256,256]{3,2,1,0:T(8,128)(2,1)} %constant.115.clone) | copy-start | bytes 1572868
  0.6 8.2 %copy-start.2 = (bf16[2,2,256,256]{3,2,1,0:T(8,128)(2,1)S(1)}, bf16[2,2,256,256]{3,2,1,0:T(8,128)(2,1)}, u32[]{:S(2)}) copy-start(bf16[2,2,256,256]{3,2,1,0:T(8,128)(2,1)} %constant.116.clone) | copy-start | bytes 1572868
  3.0 20.9 %all-to-all-start = ((f32[4,2,2,128,128]{4,3,2,1,0:T(8,128)}), f32[4,2,2,128,128]{4,3,2,1,0:T(8,128)S(1)}, u32[]{:S(2)}, u32[]{:S(2)}) async-start(f32[4,2,2,128,128]{4,3,2,1,0:T(8,128)} %copy.10), calls=%async_computation | async-start | bytes 2097152 | tf_op jit(solution)/shard_map/all_to_all | solution.py:211
  8.9 45.8 %copy-start = (bf16[256,256]{1,0:T(8,128)(2,1)S(1)}, bf16[256,256]{1,0:T(8,128)(2,1)}, u32[]{:S(2)}) copy-start(bf16[256,256]{1,0:T(8,128)(2,1)} %constant.114.clone.table_ref.refs_4_) | copy-start | bytes 393220
  24.0 13.1 %collective-permute-start = (f32[2,2,128,128]{3,2,1,0:T(8,128)S(1)}, f32[2,2,128,128]{3,2,1,0:T(8,128)S(1)}, u32[]{:S(2)}, u32[]{:S(2)}) collective-permute-start(f32[2,2,128,128]{3,2,1,0:T(8,128)S(1)} %slice_bitcast_fusion.2), channel_id=1, source_target_pairs={{0,64},{16,80},{32,96},{48,112},{128,192},{144,208},{160,224},{176... | collective-permute-start | bytes 786440 | tf_op jit(solution)/shard_map/ppermute | solution.py:215
  29.2 15.4 %collective-permute-start.1 = (f32[2,2,128,128]{3,2,1,0:T(8,128)S(1)}, f32[2,2,128,128]{3,2,1,0:T(8,128)S(1)}, u32[]{:S(2)}, u32[]{:S(2)}) collective-permute-start(f32[2,2,128,128]{3,2,1,0:T(8,128)S(1)} %slice_bitcast_fusion.2), channel_id=1, source_target_pairs={{0,128},{16,144},{32,160},{48,176},{128,0},{144,16},{160,32},{176,... | collective-permute-start | bytes 786440 | tf_op jit(solution)/shard_map/ppermute | solution.py:215
  35.6 17.0 %collective-permute-start.2 = (f32[2,2,128,128]{3,2,1,0:T(8,128)S(1)}, f32[2,2,128,128]{3,2,1,0:T(8,128)S(1)}, u32[]{:S(2)}, u32[]{:S(2)}) collective-permute-start(f32[2,2,128,128]{3,2,1,0:T(8,128)S(1)} %slice_bitcast_fusion.2), channel_id=1, source_target_pairs={{0,192},{16,208},{32,224},{48,240},{128,64},{144,80},{160,96},{176... | collective-permute-start | bytes 786440 | tf_op jit(solution)/shard_map/ppermute | solution.py:215
  37.0 16.2 %collective-permute-start.4 = (f32[4,2,128,128]{3,2,1,0:T(8,128)S(1)}, f32[4,2,128,128]{3,2,1,0:T(8,128)S(1)}, u32[]{:S(2)}, u32[]{:S(2)}) collective-permute-start(f32[4,2,128,128]{3,2,1,0:T(8,128)S(1)} %get-tuple-element.28), channel_id=1, source_target_pairs={{0,1},{1,0},{2,3},{3,2},{4,5},{5,4},{6,7},{7,6},{8,9},{9,8},{10,11... | collective-permute-start | bytes 1572872 | tf_op jit(solution)/shard_map/ppermute | solution.py:202
  52.7 2.0 collective-permute-start.3
  177.2 2.0 collective-permute-start.6
  177.3 26.0 %collective-permute-start.5 = (f32[4,2,128,128]{3,2,1,0:T(8,128)S(1)}, f32[4,2,128,128]{3,2,1,0:T(8,128)S(1)}, u32[]{:S(2)}, u32[]{:S(2)}) collective-permute-start(f32[4,2,128,128]{3,2,1,0:T(8,128)S(1)} %get-tuple-element.21), channel_id=1, source_target_pairs={{0,1},{1,0},{2,3},{3,2},{4,5},{5,4},{6,7},{7,6},{8,9},{9,8},{10,11... | collective-permute-start | bytes 1572872 | tf_op jit(solution)/shard_map/ppermute | solution.py:202
  179.3 11.4 %collective-permute-start.7 = (f32[2,128,128]{2,1,0:T(8,128)S(1)}, f32[2,128,128]{2,1,0:T(8,128)S(1)}, u32[]{:S(2)}, u32[]{:S(2)}) collective-permute-start(f32[2,128,128]{2,1,0:T(8,128)S(1)} %get-tuple-element.36), channel_id=1, source_target_pairs={{0,64},{16,80},{32,96},{48,112},{64,128},{80,144},{96,160},{112,17... | collective-permute-start | bytes 393224 | tf_op jit(solution)/shard_map/ppermute | solution.py:215
  181.8 11.8 %collective-permute-start.8 = (f32[2,128,128]{2,1,0:T(8,128)S(1)}, f32[2,128,128]{2,1,0:T(8,128)S(1)}, u32[]{:S(2)}, u32[]{:S(2)}) collective-permute-start(f32[2,128,128]{2,1,0:T(8,128)S(1)} %get-tuple-element.34), channel_id=1, source_target_pairs={{0,192},{16,208},{32,224},{48,240},{64,0},{80,16},{96,32},{112,48}... | collective-permute-start | bytes 393224 | tf_op jit(solution)/shard_map/ppermute | solution.py:215
  184.0 11.1 %collective-permute-start.9 = (f32[2,128,128]{2,1,0:T(8,128)S(1)}, f32[2,128,128]{2,1,0:T(8,128)S(1)}, u32[]{:S(2)}, u32[]{:S(2)}) collective-permute-start(f32[2,128,128]{2,1,0:T(8,128)S(1)} %get-tuple-element.35), channel_id=1, source_target_pairs={{0,128},{16,144},{32,160},{48,176},{64,192},{80,208},{96,224},{112... | collective-permute-start | bytes 393224 | tf_op jit(solution)/shard_map/ppermute | solution.py:215
  195.1 10.8 %collective-permute-start.10 = (f32[2,128,128]{2,1,0:T(8,128)S(1)}, f32[2,128,128]{2,1,0:T(8,128)S(1)}, u32[]{:S(2)}, u32[]{:S(2)}) collective-permute-start(f32[2,128,128]{2,1,0:T(8,128)S(1)} %bitcast_add_fusion), channel_id=1, source_target_pairs={{0,64},{16,80},{32,96},{48,112},{64,128},{80,144},{96,160},{112,17... | collective-permute-start | bytes 393224 | tf_op jit(solution)/shard_map/ppermute | solution.py:215
  198.6 14.0 %collective-permute-start.11 = (f32[2,128,128]{2,1,0:T(8,128)S(1)}, f32[2,128,128]{2,1,0:T(8,128)S(1)}, u32[]{:S(2)}, u32[]{:S(2)}) collective-permute-start(f32[2,128,128]{2,1,0:T(8,128)S(1)} %bitcast_add_fusion), channel_id=1, source_target_pairs={{0,128},{16,144},{32,160},{48,176},{64,192},{80,208},{96,224},{112... | collective-permute-start | bytes 393224 | tf_op jit(solution)/shard_map/ppermute | solution.py:215
  201.2 12.3 %collective-permute-start.12 = (f32[2,128,128]{2,1,0:T(8,128)S(1)}, f32[2,128,128]{2,1,0:T(8,128)S(1)}, u32[]{:S(2)}, u32[]{:S(2)}) collective-permute-start(f32[2,128,128]{2,1,0:T(8,128)S(1)} %bitcast_add_fusion), channel_id=1, source_target_pairs={{0,192},{16,208},{32,224},{48,240},{64,0},{80,16},{96,32},{112,48}... | collective-permute-start | bytes 393224 | tf_op jit(solution)/shard_map/ppermute | solution.py:215
